TPU v7x, 128 devices: a whole 4x4x4 slice. The times are simulated.
128 devices in a mesh: row: 32 (over x, z, core), col: 4 (over y).
Axes of the slice: x: 4, y: 4, z: 4, core: 2. Of those that a mesh axis runs over, the one named last changes fastest.
Arguments:
- front: float32 [8, 32, 128, 6144], P(None, 'row', None, 'col'), as said below
- child_tiles: bfloat16 [1024, 128, 6144], P('row', None, 'col'), may hold values from -0.75 to 0.75
- tile_parent: int32 [1024], P('row'), may hold values from 0 to 255, as said below
- tile_rows: int32 [1024, 128], P('row'), may hold values from -1 to 127, as said below
- tile_count: int32 [32], P('row'), may hold values from 24 to 32, as said below
Outputs:
- factored: float32 [8, 32, 128, 6144], P(None, 'row', None, 'col')
Inputs may be any that keep to these rules, and one draw needn't show every extreme that they name: `tile_count`: the live slots of each index of row are the first ones, and one index has all 32 live. The live tiles of every index add into at most 2 parent row tiles t with the same t % 32; some value of t % 32 receives exactly 2 live tiles from every index of row. `tile_parent`: parent row tiles of the front. `tile_rows`: in each tile the non-negative positions are distinct. `front`: the first 1024 x 1024 block plus assembly stays positive definite.
All inputs are finite; a program needn't handle non-finite values.
Results may differ from a plain program's by a relative error of at most 0.00059.
Values may be sent and summed in bfloat16 or wider, within the bound.
No kernel may reach another device: no remote copies, remote signals or barrier semaphores. Data moves between devices by JAX's collectives and lax.ppermute only.
A program may use at most 256 MiB of HBM per device.

v0:
```python
import jax
import jax.numpy as jnp
from jax import lax
from jax.sharding import PartitionSpec as P

P_SIZE = 1024


def from_root(value, axis, source):
    kept = jnp.where(lax.axis_index(axis) == source, value, 0).astype(value.dtype)
    return lax.psum(kept, axis)


def deposit(field, got_tiles, got_places):
    values = got_tiles.reshape(-1, got_tiles.shape[-1])
    return field.at[got_places.reshape(-1)].add(values, mode="drop")


def factor_panel(panel_cols, row_count, row_index, width_panel):
    local_tiles = panel_cols.shape[0] // 128
    diag_tiles = width_panel // 128
    stacked = panel_cols.reshape(local_tiles, 128, width_panel)
    pieces = []
    for number in range(diag_tiles):
        pieces.append(from_root(stacked[number // row_count], "row", number % row_count))
    diagonal = jnp.concatenate(pieces, axis=0)
    diag_factor = jnp.linalg.cholesky(diagonal)
    inverse = jax.scipy.linalg.solve_triangular(
        diag_factor, jnp.eye(width_panel, dtype=jnp.float32), lower=True
    )
    lower = jnp.dot(
        panel_cols, inverse.T, precision=lax.Precision.HIGHEST, preferred_element_type=jnp.float32
    )
    lower = lower.reshape(local_tiles, 128, width_panel)
    global_tile = 0 + row_index
    inside = global_tile < diag_tiles
    start = jnp.minimum(global_tile, diag_tiles - 1) * 128
    chosen = lax.dynamic_slice_in_dim(diag_factor, start, 128, 0)
    lower = lower.at[0].set(jnp.where(inside, chosen, lower[0]))
    return lower.reshape(local_tiles * 128, width_panel)


def body(front, child_tiles, tile_parent, tile_rows, tile_count):
    local_tiles = front.shape[0]
    width_local = front.shape[3]
    width_panel = P_SIZE
    row_count = lax.axis_size("row")
    row_index = lax.axis_index("row")
    col_index = lax.axis_index("col")
    slot_total = child_tiles.shape[0]
    capacity = max(2, -(-(4 * slot_total) // (3 * row_count)))
    live = jnp.arange(slot_total, dtype=jnp.int32) < tile_count[0]
    owner = tile_parent % row_count
    owner_local = tile_parent // row_count
    member = (
        (owner[:, None] == jnp.arange(row_count, dtype=jnp.int32)[None, :]) & live[:, None]
    ).astype(jnp.int32)
    before = jnp.sum((jnp.cumsum(member, axis=0) - member) * member, axis=1)
    position = jnp.where(live, owner * capacity + before, row_count * capacity)
    outside = local_tiles * 128
    places = jnp.where(tile_rows >= 0, owner_local[:, None] * 128 + tile_rows, outside)
    send_places = (
        jnp.full((row_count * capacity, 128), outside, jnp.int32)
        .at[position]
        .set(places, mode="drop")
    )
    send_places = send_places.reshape(row_count, capacity, 128)
    field = front.reshape(local_tiles * 128, width_local)
    buffer = jnp.zeros((row_count * capacity, 128, child_tiles.shape[2]), jnp.bfloat16)
    buffer = buffer.at[position].set(child_tiles, mode="drop")
    got_tiles = lax.all_to_all(
        buffer.reshape(row_count, capacity, 128, child_tiles.shape[2]),
        "row",
        split_axis=0,
        concat_axis=0,
        tiled=True,
    )
    got_places = lax.all_to_all(send_places, "row", split_axis=0, concat_axis=0, tiled=True)
    field = deposit(field, got_tiles, got_places)
    lower = factor_panel(field[:, :width_panel], row_count, row_index, width_panel)
    spread = from_root(lower.astype(jnp.bfloat16), "col", 0)
    spread_tiles = spread.reshape(local_tiles, 128, width_panel)
    slab_tiles = width_local // 128

    def fetch(number, gathered):
        global_tile = col_index * slab_tiles + number
        piece = lax.dynamic_index_in_dim(spread_tiles, global_tile // row_count, 0, keepdims=False)
        got = from_root(piece, "row", global_tile % row_count)
        return lax.dynamic_update_index_in_dim(gathered, got, number, 0)

    slab_rows = lax.fori_loop(
        0, slab_tiles, fetch, jnp.zeros((slab_tiles, 128, width_panel), jnp.bfloat16)
    )
    slab_rows = slab_rows.reshape(width_local, width_panel)
    update = lax.dot_general(
        spread, slab_rows, (((1,), (1,)), ((), ())), preferred_element_type=jnp.float32
    )
    result = field - update
    result = result.at[:, :width_panel].set(
        jnp.where(col_index == 0, lower, result[:, :width_panel])
    )
    return result.reshape(local_tiles, 1, 128, width_local)


def solution(mesh):
    placed = (
        P(None, "row", None, "col"),
        P("row", None, "col"),
        P("row"),
        P("row", None),
        P("row"),
    )
    return jax.shard_map(
        body, mesh=mesh, in_specs=placed, out_specs=P(None, "row", None, "col"), check_vma=False
    )
```

profile of v0, /device:TPU:1, one launch (start us, length us, event | category | flops | bytes accessed | tf_op | source)
XLA Modules:
  0.0 2419.2 jit_solution(13875058447475463318)
XLA Ops:
  6.5 6.0 copy.91
  14.8 9.4 all-to-all-start
  24.2 8.5 broadcast_in_dim.69
  32.8 35.8 %scatter_fusion = bf16[64,128,1536]{2,1,0:T(8,128)(2,1)} fusion(bf16[64,128,1536]{2,1,0:T(8,128)(2,1)} %broadcast_in_dim.69, s32[32]{0:T(128)S(1)} %compare_select_fusion.1, bf16[32,128,1536]{2,1,0:T(8,128)(2,1)} %param.12), kind=kCustom, calls=%fused_computation.1 | custom fusion | bytes 37748864 | tf_op jit(solution)/shard_map/scatter | solution.py:70
  68.6 9.0 all-to-all-start.1
  77.8 359.1 %all-to-all-done.1 = bf16[32,2,128,1536]{3,2,1,0:T(8,128)(2,1)} async-done(((bf16[32,2,128,1536]{3,2,1,0:T(8,128)(2,1)}), bf16[32,2,128,1536]{3,2,1,0:T(8,128)(2,1)}, u32[]{:S(2)}, u32[]{:S(2)}) %all-to-all-start.1) | async-done | bytes 25165856 | tf_op jit(solution)/shard_map/all_to_all | solution.py:71
  436.8 88.1 %scatter_custom_fusion.2 = f32[1024,1536]{1,0:T(8,128)} fusion(f32[1024,1536]{1,0:T(8,128)} %bitcast.130, s32[8192]{0:T(1024)S(1)} %bitcast.137, bf16[8192,1536]{1,0:T(8,128)(2,1)} %bitcast.40), kind=kCustom, calls=%fused_computation.7 | custom fusion | flops 25165824 | bytes 31457280 | tf_op jit(solution)/shard_map/scatter-add | solution.py:16
  531.1 162.1 %all-reduce.8.cloned.1.call-done = (f32[128,1024]{0,1:T(8,128)}, f32[128,1024]{0,1:T(8,128)}, f32[128,1024]{0,1:T(8,128)}, f32[128,1024]{0,1:T(8,128)}, f32[128,...) async-done(((f32[128,1024]{0,1:T(8,128)}, f32[128,1024]{0,1:T(8,128)}, f32[128,1024]{0,1:T(8,128)}, f32[128,1024]{0,1:T(8,128)}, ...) | async-done | bytes 4194320 | tf_op jit(solution)/shard_map/psum | solution.py:11
  704.6 5.5 copy.14
  710.1 4.4 fusion.5
  716.5 11.7 cholesky.223
  730.8 9.8 custom-call.63
  744.5 12.1 cholesky.244
  757.3 9.8 custom-call.64
  770.5 11.7 cholesky.468
  783.4 9.8 custom-call.65
  796.8 11.8 cholesky.487
  809.9 9.8 custom-call.66
  823.2 11.7 cholesky.506
  836.2 10.0 custom-call.67
  849.5 11.7 cholesky.526
  862.5 9.8 custom-call.68
  875.3 12.1 cholesky.546
  888.6 9.8 custom-call.69
  901.1 11.7 cholesky.564
  919.7 6.6 fusion.6
  926.3 23.6 while.19
  949.9 78.8 %custom-call.70 = f32[8,128,128]{1,2,0:T(8,128)S(1)} custom-call(f32[8,128,128]{2,1,0:T(8,128)S(1)} %get-tuple-element.153), custom_call_target="InvertDiagBlocksLowerTriangular" | custom-call | tf_op jit(solution)/shard_map/jit(_solve_triangular)/triangular_solve | solution.py:28
  1040.0 2.6 convolution_subtract_fusion.3
  1043.4 3.2 convolution_subtract_fusion.2
  1047.2 3.5 convolution_subtract_fusion.4
  1051.3 13.7 fusion.3
  1070.6 55.6 %all-reduce.6.cloned.1.call-done = bf16[1024,1024]{1,0:T(8,128)(2,1)} async-done(((bf16[1024,1024]{1,0:T(8,128)(2,1)}), bf16[1024,1024]{1,0:T(8,128)(2,1)}) %all-reduce.6.cloned.1.call-update) | async-done | bytes 2097168 | tf_op jit(solution)/shard_map/psum | solution.py:11
  1126.2 1275.1 %while.18 = (s32[]{:T(128)}, bf16[12,128,1024]{2,1,0:T(8,128)(2,1)S(1)}, s32[]{:T(128)}, bf16[8,128,1024]{2,1,0:T(8,128)(2,1)}, s32[]{:T(128)}, /*index=5*/s32[]...) while((s32[]{:T(128)}, ...), condition=%wide.region_32.33_spmd, body=%wide.region_30.32_spmd.sunk | while | flops 262173 | bytes 2621896 | solution.py:91
  1127.9 104.0 %all-reduce.10.cloned.1.call-done = bf16[1,128,1024]{2,1,0:T(8,128)(2,1)} async-done(((bf16[1,128,1024]{2,1,0:T(8,128)(2,1)}), bf16[1,128,1024]{2,1,0:T(8,128)(2,1)}) %all-reduce.10.cloned.1.call-update) | async-done | bytes 262160 | tf_op jit(solution)/shard_map/while/body/eval_jaxpr/psum | solution.py:11
  1234.7 103.3 %all-reduce.10.cloned.1.call-done = bf16[1,128,1024]{2,1,0:T(8,128)(2,1)} async-done(((bf16[1,128,1024]{2,1,0:T(8,128)(2,1)}), bf16[1,128,1024]{2,1,0:T(8,128)(2,1)}) %all-reduce.10.cloned.1.call-update) | async-done | bytes 262160 | tf_op jit(solution)/shard_map/while/body/eval_jaxpr/psum | solution.py:11
  1340.8 103.3 %all-reduce.10.cloned.1.call-done = bf16[1,128,1024]{2,1,0:T(8,128)(2,1)} async-done(((bf16[1,128,1024]{2,1,0:T(8,128)(2,1)}), bf16[1,128,1024]{2,1,0:T(8,128)(2,1)}) %all-reduce.10.cloned.1.call-update) | async-done | bytes 262160 | tf_op jit(solution)/shard_map/while/body/eval_jaxpr/psum | solution.py:11
  1446.8 103.3 %all-reduce.10.cloned.1.call-done = bf16[1,128,1024]{2,1,0:T(8,128)(2,1)} async-done(((bf16[1,128,1024]{2,1,0:T(8,128)(2,1)}), bf16[1,128,1024]{2,1,0:T(8,128)(2,1)}) %all-reduce.10.cloned.1.call-update) | async-done | bytes 262160 | tf_op jit(solution)/shard_map/while/body/eval_jaxpr/psum | solution.py:11
  1552.9 103.6 %all-reduce.10.cloned.1.call-done = bf16[1,128,1024]{2,1,0:T(8,128)(2,1)} async-done(((bf16[1,128,1024]{2,1,0:T(8,128)(2,1)}), bf16[1,128,1024]{2,1,0:T(8,128)(2,1)}) %all-reduce.10.cloned.1.call-update) | async-done | bytes 262160 | tf_op jit(solution)/shard_map/while/body/eval_jaxpr/psum | solution.py:11
  1659.3 103.6 %all-reduce.10.cloned.1.call-done = bf16[1,128,1024]{2,1,0:T(8,128)(2,1)} async-done(((bf16[1,128,1024]{2,1,0:T(8,128)(2,1)}), bf16[1,128,1024]{2,1,0:T(8,128)(2,1)}) %all-reduce.10.cloned.1.call-update) | async-done | bytes 262160 | tf_op jit(solution)/shard_map/while/body/eval_jaxpr/psum | solution.py:11
  1765.7 103.6 %all-reduce.10.cloned.1.call-done = bf16[1,128,1024]{2,1,0:T(8,128)(2,1)} async-done(((bf16[1,128,1024]{2,1,0:T(8,128)(2,1)}), bf16[1,128,1024]{2,1,0:T(8,128)(2,1)}) %all-reduce.10.cloned.1.call-update) | async-done | bytes 262160 | tf_op jit(solution)/shard_map/while/body/eval_jaxpr/psum | solution.py:11
  1872.1 103.3 %all-reduce.10.cloned.1.call-done = bf16[1,128,1024]{2,1,0:T(8,128)(2,1)} async-done(((bf16[1,128,1024]{2,1,0:T(8,128)(2,1)}), bf16[1,128,1024]{2,1,0:T(8,128)(2,1)}) %all-reduce.10.cloned.1.call-update) | async-done | bytes 262160 | tf_op jit(solution)/shard_map/while/body/eval_jaxpr/psum | solution.py:11
  1978.2 103.6 %all-reduce.10.cloned.1.call-done = bf16[1,128,1024]{2,1,0:T(8,128)(2,1)} async-done(((bf16[1,128,1024]{2,1,0:T(8,128)(2,1)}), bf16[1,128,1024]{2,1,0:T(8,128)(2,1)}) %all-reduce.10.cloned.1.call-update) | async-done | bytes 262160 | tf_op jit(solution)/shard_map/while/body/eval_jaxpr/psum | solution.py:11
  2084.5 103.3 %all-reduce.10.cloned.1.call-done = bf16[1,128,1024]{2,1,0:T(8,128)(2,1)} async-done(((bf16[1,128,1024]{2,1,0:T(8,128)(2,1)}), bf16[1,128,1024]{2,1,0:T(8,128)(2,1)}) %all-reduce.10.cloned.1.call-update) | async-done | bytes 262160 | tf_op jit(solution)/shard_map/while/body/eval_jaxpr/psum | solution.py:11
  2190.6 103.6 %all-reduce.10.cloned.1.call-done = bf16[1,128,1024]{2,1,0:T(8,128)(2,1)} async-done(((bf16[1,128,1024]{2,1,0:T(8,128)(2,1)}), bf16[1,128,1024]{2,1,0:T(8,128)(2,1)}) %all-reduce.10.cloned.1.call-update) | async-done | bytes 262160 | tf_op jit(solution)/shard_map/while/body/eval_jaxpr/psum | solution.py:11
  2297.0 103.3 %all-reduce.10.cloned.1.call-done = bf16[1,128,1024]{2,1,0:T(8,128)(2,1)} async-done(((bf16[1,128,1024]{2,1,0:T(8,128)(2,1)}), bf16[1,128,1024]{2,1,0:T(8,128)(2,1)}) %all-reduce.10.cloned.1.call-update) | async-done | bytes 262160 | tf_op jit(solution)/shard_map/while/body/eval_jaxpr/psum | solution.py:11
  2401.3 6.4 convolution_subtract_fusion
  2409.6 2.7 copy-done.4
  (182 shorter events, 132.3 us)
Async XLA Ops:
  6.5 6.0 copy-start.10
  6.5 7.0 copy-start.9
  14.8 53.8 %all-to-all-start = ((s32[32,2,128]{2,1,0:T(2,128)}), s32[32,2,128]{2,1,0:T(2,128)S(1)}, u32[]{:S(2)}, u32[]{:S(2)}) async-start(s32[32,2,128]{2,1,0:T(2,128)} %bitcast.2), calls=%async_computation | async-start | bytes 65536 | tf_op jit(solution)/shard_map/all_to_all | solution.py:78
  68.6 368.2 %all-to-all-start.1 = ((bf16[32,2,128,1536]{3,2,1,0:T(8,128)(2,1)}), bf16[32,2,128,1536]{3,2,1,0:T(8,128)(2,1)}, u32[]{:S(2)}, u32[]{:S(2)}) async-start(bf16[32,2,128,1536]{3,2,1,0:T(8,128)(2,1)} %bitcast.128), calls=%async_computation.1 | async-start | bytes 50331648 | tf_op jit(solution)/shard_map/all_to_all | solution.py:71
  77.6 615.6 %all-reduce.8.cloned.1.call-start = ((), (), s32[]{:S(2)}) async-start(), calls=%async_computation.3 | async-start | bytes 8388608 | tf_op jit(solution)/shard_map/psum | solution.py:11
  528.3 597.9 %all-reduce.6.cloned.1.call-start = ((), (), s32[]{:S(2)}) async-start(), calls=%async_computation.2 | async-start | bytes 4194304 | tf_op jit(solution)/shard_map/psum | solution.py:11
  693.2 7.8 copy-start.8
  693.2 8.7 copy-start.7
  693.2 9.6 copy-start.6
  693.2 10.5 copy-start.5
  714.5 2.0 copy-start.3
  1028.7 3.2 copy-start.2
  1042.7 8.6 slice-start
  1046.5 4.8 slice-start.1
  1066.5 1.9 copy-start
  1126.2 105.7 %all-reduce.10.cloned.1.call-start = ((), (), s32[]{:S(2)}) async-start(), calls=%async_computation.4 | async-start | bytes 524288 | tf_op jit(solution)/shard_map/while/body/eval_jaxpr/psum | solution.py:11
  1232.9 105.1 %all-reduce.10.cloned.1.call-start = ((), (), s32[]{:S(2)}) async-start(), calls=%async_computation.4 | async-start | bytes 524288 | tf_op jit(solution)/shard_map/while/body/eval_jaxpr/psum | solution.py:11
  1339.0 105.1 %all-reduce.10.cloned.1.call-start = ((), (), s32[]{:S(2)}) async-start(), calls=%async_computation.4 | async-start | bytes 524288 | tf_op jit(solution)/shard_map/while/body/eval_jaxpr/psum | solution.py:11
  1445.0 105.1 %all-reduce.10.cloned.1.call-start = ((), (), s32[]{:S(2)}) async-start(), calls=%async_computation.4 | async-start | bytes 524288 | tf_op jit(solution)/shard_map/while/body/eval_jaxpr/psum | solution.py:11
  1551.1 105.4 %all-reduce.10.cloned.1.call-start = ((), (), s32[]{:S(2)}) async-start(), calls=%async_computation.4 | async-start | bytes 524288 | tf_op jit(solution)/shard_map/while/body/eval_jaxpr/psum | solution.py:11
  1657.5 105.4 %all-reduce.10.cloned.1.call-start = ((), (), s32[]{:S(2)}) async-start(), calls=%async_computation.4 | async-start | bytes 524288 | tf_op jit(solution)/shard_map/while/body/eval_jaxpr/psum | solution.py:11
  1763.9 105.4 %all-reduce.10.cloned.1.call-start = ((), (), s32[]{:S(2)}) async-start(), calls=%async_computation.4 | async-start | bytes 524288 | tf_op jit(solution)/shard_map/while/body/eval_jaxpr/psum | solution.py:11
  1870.3 105.1 %all-reduce.10.cloned.1.call-start = ((), (), s32[]{:S(2)}) async-start(), calls=%async_computation.4 | async-start | bytes 524288 | tf_op jit(solution)/shard_map/while/body/eval_jaxpr/psum | solution.py:11
  1976.4 105.4 %all-reduce.10.cloned.1.call-start = ((), (), s32[]{:S(2)}) async-start(), calls=%async_computation.4 | async-start | bytes 524288 | tf_op jit(solution)/shard_map/while/body/eval_jaxpr/psum | solution.py:11
  2082.8 105.1 %all-reduce.10.cloned.1.call-start = ((), (), s32[]{:S(2)}) async-start(), calls=%async_computation.4 | async-start | bytes 524288 | tf_op jit(solution)/shard_map/while/body/eval_jaxpr/psum | solution.py:11
  2188.8 105.4 %all-reduce.10.cloned.1.call-start = ((), (), s32[]{:S(2)}) async-start(), calls=%async_computation.4 | async-start | bytes 524288 | tf_op jit(solution)/shard_map/while/body/eval_jaxpr/psum | solution.py:11
  2295.2 105.1 %all-reduce.10.cloned.1.call-start = ((), (), s32[]{:S(2)}) async-start(), calls=%async_computation.4 | async-start | bytes 524288 | tf_op jit(solution)/shard_map/while/body/eval_jaxpr/psum | solution.py:11
  2401.3 6.4 copy-start.1
  2409.6 2.7 copy-start.4
Sparse Core Ops, SparseCore 0:
  528.4 164.7 all-reduce.7
  1070.1 56.0 all-reduce.5
  1130.5 101.3 all-reduce.9
  1237.0 100.9 all-reduce.9
  1343.0 100.9 all-reduce.9
  1449.1 100.9 all-reduce.9
  1555.5 100.9 all-reduce.9
  1661.9 100.9 all-reduce.9
  1768.3 100.9 all-reduce.9
  1874.4 100.9 all-reduce.9
  1980.8 100.9 all-reduce.9
  2086.8 100.9 all-reduce.9
  2193.2 100.9 all-reduce.9
  2299.3 100.9 all-reduce.9
where the time goes:
time: 2430 us; the launch traced here: 2420 us
  waiting for transfers between devices  1820 us (75%)
  other arithmetic  382 us (16%)
  local copies, waits for them, and re-layouts  113 us (5%)
  matrix products  65.7 us (3%)
    psum x14, waiting for transfers between devices, from_root(): return lax.psum(kept, axis)  1460 us
    all_to_all x1, waiting for transfers between devices, body(): lax.all_to_all(buffer.reshape(row_count, capacity, 128, child_tiles.shape...  359 us
    another operation x30, other arithmetic, factor_panel(): diag_factor = jnp.linalg.cholesky(diagonal)  173 us
    scatter-add x1, other arithmetic, deposit(): return field.at[got_places.reshape(-1)].add(values, mode='drop')  88.1 us
    another operation x3, other arithmetic, factor_panel(): jax.scipy.linalg.solve_triangular(diag_factor, jnp.eye(width_panel, dtype...  85.4 us
  transfers between devices with their start and end apart: 16, of which 15 were waited for; matrix products, arithmetic and copies ran while one was open for 2% of the time, Pallas kernels for 0%

commit v1 on v0

v1 whole, which is shorter than its diff:
```python
import jax
import jax.numpy as jnp
from jax import lax
from jax.experimental import pallas as pl
from jax.experimental.pallas import tpu as pltpu
from jax.sharding import PartitionSpec as P

PANEL = 1024
HIGH = lax.Precision.HIGHEST
f32 = jnp.float32
bf16 = jnp.bfloat16
MIB = 2**20


def times_transposed(a, b, precision=HIGH):
    return lax.dot_general(
        a, b, (((1,), (1,)), ((), ())), precision=precision, preferred_element_type=f32
    )


def times(a, b):
    return lax.dot_general(
        a, b, (((1,), (0,)), ((), ())), precision=HIGH, preferred_element_type=f32
    )


def place_kernel(rows_ref, child_ref, out_ref):
    width = out_ref.shape[-1]
    position = lax.broadcasted_iota(jnp.int32, (128, 128), 0)
    for slot in range(4):
        hot = jnp.where(rows_ref[0, slot : slot + 1, :] == position, 1.0, 0.0).astype(bf16)
        placed = jnp.dot(hot, child_ref[slot], preferred_element_type=f32).astype(bf16)
        for jp in range(8):
            for jc in range(4):
                out_ref[jp, jc, slot] = placed[
                    jp * 16 : jp * 16 + 16, jc * width : jc * width + width
                ]


def place(rows, child_tiles, width, block):
    slots = child_tiles.shape[0]
    return pl.pallas_call(
        place_kernel,
        grid=(slots // 4,),
        in_specs=[
            pl.BlockSpec((1, 4, 128), lambda t: (t, 0, 0)),
            pl.BlockSpec((4, 128, 4 * width), lambda t: (t, 0, block)),
        ],
        out_specs=pl.BlockSpec((8, 4, 4, 16, width), lambda t: (0, 0, t, 0, 0)),
        out_shape=jax.ShapeDtypeStruct((8, 4, slots, 16, width), bf16),
        compiler_params=pltpu.CompilerParams(vmem_limit_bytes=32 * MIB),
        cost_estimate=pl.CostEstimate(
            flops=2 * slots * 128 * 128 * 4 * width,
            bytes_accessed=2 * slots * 128 * 4 * width * 2,
            transcendentals=0,
        ),
        name="place_rows",
    )(rows.reshape(slots // 4, 4, 128), child_tiles)


def collect_kernel(at_ref, got_ref, out_ref):
    step = pl.program_id(0)

    @pl.when(step == 0)
    def _():
        out_ref[...] = jnp.zeros_like(out_ref)

    sources, slots = got_ref.shape[:2]

    def add(source, carry):
        base = (step * sources + source) * slots
        for slot in range(slots):
            at = at_ref[base + slot]
            out_ref[at] = out_ref[at] + got_ref[source, slot].astype(f32)
        return carry

    lax.fori_loop(0, sources, add, 0)


def collect(at, got):
    sources, slots, _, width = got.shape
    return pl.pallas_call(
        collect_kernel,
        grid_spec=pltpu.PrefetchScalarGridSpec(
            num_scalar_prefetch=1,
            grid=(sources // 4,),
            in_specs=[pl.BlockSpec((4, slots, 16, width), lambda s, at: (s, 0, 0, 0))],
            out_specs=pl.BlockSpec((256, 16, width), lambda s, at: (0, 0, 0)),
        ),
        out_shape=jax.ShapeDtypeStruct((256, 16, width), f32),
        compiler_params=pltpu.CompilerParams(vmem_limit_bytes=32 * MIB),
        cost_estimate=pl.CostEstimate(
            flops=sources * slots * 16 * width,
            bytes_accessed=sources * slots * 16 * width * 2 + 256 * 16 * width * 4,
            transcendentals=0,
        ),
        name="collect_parents",
    )(at, got)


def factor_block(block, u_ref, w_ref):
    sub = lax.broadcasted_iota(jnp.int32, (8, 128), 0)
    lane = lax.broadcasted_iota(jnp.int32, (8, 128), 1)
    s = [block[8 * g : 8 * g + 8, :] for g in range(16)]
    v = [jnp.where(lane == sub + 8 * g, 1.0, 0.0).astype(f32) for g in range(16)]
    for k in range(128):
        g0, s0 = divmod(k, 8)
        cols = [jnp.broadcast_to(s[g][:, k : k + 1], (8, 128)) for g in range(g0, 16)]
        pivot = jnp.broadcast_to(cols[0][s0 : s0 + 1, :], (8, 128))
        inverse = 1.0 / pivot
        row = jnp.broadcast_to(s[g0][s0 : s0 + 1, :], (8, 128))
        vrow = jnp.broadcast_to(v[g0][s0 : s0 + 1, :], (8, 128))
        root = lax.rsqrt(pivot)
        root = root * (1.5 - 0.5 * pivot * root * root)
        u_ref[k : k + 1, :] = jnp.where(lane >= k, row * root, 0.0)[:1]
        w_ref[k : k + 1, :] = (vrow * root)[:1]
        row, vrow = row * inverse, vrow * inverse
        for g in range(g0, 16):
            if g == g0 and s0 == 7:
                continue
            col = cols[g - g0]
            if g == g0:
                col = jnp.where(sub > s0, col, 0.0)
            s[g] = s[g] - col * row
            v[g] = v[g] - col * vrow


def factor_kernel(pieces_ref, l_ref, x_ref, a_ref, u_ref, w_ref):
    for jp in range(8):
        for jc in range(4):
            for tile in range(8):
                at = tile * 128 + jp * 16
                a_ref[at : at + 16, jc * 256 : jc * 256 + 256] = pieces_ref[jp * 4 + jc, tile]
    l_ref[...] = jnp.zeros_like(l_ref)
    x_ref[...] = jnp.zeros_like(x_ref)
    for i in range(8):
        for j in range(i + 1):
            bi, bj = slice(128 * i, 128 * i + 128), slice(128 * j, 128 * j + 128)
            a_ref[bi, bj] = 0.5 * (a_ref[bi, bj] + a_ref[bj, bi].T)

    def step(b, carry):
        at = pl.ds(pl.multiple_of(b * 128, 128), 128)
        factor_block(a_ref[at, at], u_ref, w_ref)
        w = w_ref[...]
        l_ref[at, at] = u_ref[...].T
        x_ref[at, at] = w
        for n in range(8):

            @pl.when(b == n)
            def _():
                here = slice(128 * n, 128 * n + 128)
                if n < 7:
                    below = slice(128 * n + 128, PANEL)
                    low = times_transposed(a_ref[below, here], w)
                    l_ref[below, here] = low
                    for j in range(n + 1, 8):
                        rows, cols = slice(128 * j, PANEL), slice(128 * j, 128 * j + 128)
                        off = 128 * (j - n - 1)
                        a_ref[rows, cols] = a_ref[rows, cols] - times_transposed(
                            low[off:], low[off : off + 128]
                        )
                if n > 0:
                    done = slice(0, 128 * n)
                    x_ref[here, done] = -times(w, times(l_ref[here, done], x_ref[done, done]))

        return carry

    lax.fori_loop(0, 8, step, 0)


def factor(pieces):
    return pl.pallas_call(
        factor_kernel,
        out_shape=[jax.ShapeDtypeStruct((PANEL, PANEL), f32)] * 2,
        scratch_shapes=[
            pltpu.VMEM((PANEL, PANEL), f32),
            pltpu.VMEM((128, 128), f32),
            pltpu.VMEM((128, 128), f32),
        ],
        compiler_params=pltpu.CompilerParams(vmem_limit_bytes=40 * MIB),
        cost_estimate=pl.CostEstimate(
            flops=10**11, bytes_accessed=12 * MIB, transcendentals=0
        ),
        name="factor_and_invert",
    )(pieces)


def finish_kernel(col_ref, panel_ref, lower_ref, front_ref, got_ref, spread_ref, slab_ref, out_ref):
    tiles = panel_ref.shape[0]
    rows = spread_ref[...].reshape(tiles * 128, PANEL)

    @pl.when(col_ref[0] == 0)
    def _():
        out_ref[:, 0, :, :PANEL] = lower_ref[...]

    @pl.when(col_ref[0] != 0)
    def _():
        update = times_transposed(rows, slab_ref[:PANEL, :], None)
        out_ref[:, 0, :, :PANEL] = panel_ref[...] - update.reshape(tiles, 128, PANEL)

    update = times_transposed(rows, slab_ref[PANEL:, :], None).reshape(tiles, 128, -1)
    for jc in range(4):
        for tile in range(tiles):
            cols = slice(jc * 128, jc * 128 + 128)
            sums = got_ref[:, jc, tile].reshape(128, 128)
            out_ref[tile, 0, :, PANEL + jc * 128 : PANEL + jc * 128 + 128] = (
                front_ref[tile, 0, :, cols] + sums - update[tile, :, cols]
            )


def finish(col_index, panel, lower, front, got, spread, slab):
    k, _, _, width = front.shape
    step = 2
    return pl.pallas_call(
        finish_kernel,
        grid_spec=pltpu.PrefetchScalarGridSpec(
            num_scalar_prefetch=1,
            grid=(k // step,),
            in_specs=[
                pl.BlockSpec((step, 128, PANEL), lambda i, c: (i, 0, 0)),
                pl.BlockSpec((step, 128, PANEL), lambda i, c: (i, 0, 0)),
                pl.BlockSpec((step, 1, 128, 512), lambda i, c: (i, 0, 0, 2)),
                pl.BlockSpec((8, 4, step, 16, 128), lambda i, c: (0, 0, i, 0, 0)),
                pl.BlockSpec((step, 128, PANEL), lambda i, c: (i, 0, 0)),
                pl.BlockSpec((width, PANEL), lambda i, c: (0, 0)),
            ],
            out_specs=pl.BlockSpec((step, 1, 128, width), lambda i, c: (i, 0, 0, 0)),
        ),
        out_shape=jax.ShapeDtypeStruct(front.shape, f32),
        compiler_params=pltpu.CompilerParams(vmem_limit_bytes=40 * MIB),
        cost_estimate=pl.CostEstimate(
            flops=2 * k * 128 * width * PANEL,
            bytes_accessed=28 * MIB,
            transcendentals=0,
        ),
        name="trailing_update",
    )(col_index.reshape(1), panel, lower, front, got, spread, slab)


def exchange(x, groups=None, axis="row"):
    return lax.all_to_all(
        x, axis, split_axis=0, concat_axis=0, axis_index_groups=groups, tiled=True
    )


def gather_rows(x, row_index):
    chips = lax.axis_size("row") // 2
    groups = [[2 * chip + core for chip in range(chips)] for core in range(2)]
    mine = exchange(jnp.broadcast_to(x[None], (chips,) + x.shape), groups)
    other = lax.ppermute(mine, "row", [(r, r ^ 1) for r in range(2 * chips)])
    first = row_index % 2 == 0
    both = jnp.stack([jnp.where(first, mine, other), jnp.where(first, other, mine)], axis=1)
    return both.reshape((2 * chips,) + x.shape)


def from_first(pieces, col_index):
    result = jnp.where(col_index == 0, pieces[0], 0)
    for c in range(1, len(pieces)):
        result = result + lax.ppermute(pieces[c], "col", [(0, c)])
    return result


def body(front, child_tiles, tile_parent, tile_rows, tile_count):
    row_index = lax.axis_index("row")
    col_index = lax.axis_index("col")
    slots = child_tiles.shape[0]
    live = jnp.arange(slots, dtype=jnp.int32) < tile_count[0]
    rows = jnp.where(live[:, None], tile_rows, -1)
    at = (tile_parent % 32) * 8 + tile_parent // 32
    at = exchange(jnp.broadcast_to(at[None], (32, slots))).reshape(32 * slots)

    early = front[:2, 0, :, :PANEL].reshape(2, 8, 16, 4, 256).transpose(1, 3, 0, 2, 4)
    early = exchange(early.reshape(32, 2, 16, 256))

    sent_panel = place(rows, child_tiles, 256, 0).reshape(32, slots, 16, 256)
    sums_panel = collect(at, exchange(sent_panel))
    sent_rest = place(rows, child_tiles, 128, 2).reshape(32, slots, 16, 128)
    sums_rest = collect(at, exchange(sent_rest))

    sums = sums_panel.reshape(32, 8, 16, 256)
    tiles = (sums[:, :2] + early).transpose(1, 0, 2, 3).reshape(64, 16, 256)
    pieces = [jnp.concatenate([tiles[:8], tiles[12 * c : 12 * c + 12]]) for c in range(4)]
    piece = from_first(pieces, col_index)
    diagonal = gather_rows(piece[:8], row_index)
    quads = [[4 * q + i for i in range(4)] for q in range(8)]
    part = exchange(piece[8:].reshape(4, 3, 16, 256), quads)
    part = part.transpose(1, 2, 0, 3).reshape(48, PANEL)

    got = exchange(sums).reshape(8, 4, 8, 16, 256).transpose(2, 0, 3, 1, 4)
    panel = front[:, 0, :, :PANEL] + got.reshape(8, 128, PANEL)
    own = from_first([panel[2 * c : 2 * c + 2] for c in range(4)], col_index)

    factored, inverse = factor(diagonal)

    def rows_of_factor(start, count):
        start = jnp.minimum(start, PANEL - count)
        return lax.dynamic_slice_in_dim(factored, start, count, 0)

    in_factor = row_index < 8
    top = rows_of_factor(row_index * 128, 128)
    own = times_transposed(own.reshape(256, PANEL), inverse)
    own = own.at[:128].set(jnp.where(in_factor & (col_index == 0), top, own[:128]))
    own = own.astype(bf16)
    spread = exchange(jnp.broadcast_to(own[None], (4, 256, PANEL)), None, "col")
    spread = spread.reshape(8, 128, PANEL)

    part = times_transposed(part, inverse).reshape(3, 16, PANEL)
    for q in range(3):
        tile = 12 * col_index + 3 * (row_index % 4) + q
        known = rows_of_factor(tile * 128 + row_index // 4 * 16, 16)
        part = part.at[q].set(jnp.where(tile < 8, known, part[q]))
    slab = gather_rows(part.astype(bf16), row_index)
    slab = slab.reshape(8, 4, 3, 16, PANEL).transpose(1, 2, 0, 3, 4).reshape(1536, PANEL)

    lower = times_transposed(panel.reshape(8 * 128, PANEL), inverse).reshape(8, 128, PANEL)
    lower = lower.at[0].set(jnp.where(in_factor, top, lower[0]))

    got_rest = exchange(sums_rest.reshape(32, 8, 16, 128)).reshape(8, 4, 8, 16, 128)
    return finish(col_index, panel, lower, front, got_rest, spread, slab)


def solution(mesh):
    placed = (
        P(None, "row", None, "col"),
        P("row", None, "col"),
        P("row"),
        P("row", None),
        P("row"),
    )
    return jax.shard_map(
        body, mesh=mesh, in_specs=placed, out_specs=P(None, "row", None, "col"), check_vma=False
    )
```

time: 2430 us -> 647 us (0.27)
  waiting for transfers between devices: 1820 us -> 224 us
  other arithmetic: 382 us -> 27.8 us
  Pallas kernels: 0 us -> 202 us
  starting transfers between devices: 19 us -> 96.4 us
  local copies, waits for them, and re-layouts: 113 us -> 64.4 us
  matrix products: 65.7 us -> 21.5 us
    psum x14 -> x0, waiting for transfers between devices: 1460 us -> none  [from_root(): return lax.psum(kept, axis)]
    another operation x35 -> x4, other arithmetic: 259 us -> 7.15 us  [gather_rows(): jnp.stack([jnp.where(first, mine, other), jnp.where(first, other, mine)],...]
    pallas_call x0 -> x6, Pallas kernels: none -> 202 us  [the longest x1 169 us: factor(): pl.pallas_call(factor_kernel, out_shape=[jax.ShapeDtypeStruct((PANEL, PAN...]
    all_to_all x2 -> x10, waiting for transfers between devices: 359 us -> 177 us  [exchange(): lax.all_to_all(x, axis, split_axis=0, concat_axis=0, axis_index_groups=gr...]
    scatter-add x1 -> x0, other arithmetic: 88.1 us -> none  [deposit(): return field.at[got_places.reshape(-1)].add(values, mode='drop')]
    all_to_all x2 -> x10, starting transfers between devices: 18.5 us -> 80.3 us  [exchange(): lax.all_to_all(x, axis, split_axis=0, concat_axis=0, axis_index_groups=gr...]
    ppermute x0 -> x8, waiting for transfers between devices: none -> 47 us  [the longest x6 43.2 us: from_first(): result = result + lax.ppermute(pieces[c], 'col', [(0, c)])]
    another operation x29 -> x0, matrix products: 45.5 us -> none  [the longest x14 23.1 us: factor_panel(): diag_factor = jnp.linalg.cholesky(diagonal)]
  transfers between devices with their start and end apart: 16 -> 18, of which waited for: 15 -> 13; matrix products, arithmetic and copies ran while one was open for 2% -> 13% of each run, Pallas kernels for 0% -> 31%
where the time goes in v1:
time: 647 us; the launch traced here: 638 us
  waiting for transfers between devices  224 us (35%)
  Pallas kernels  202 us (31%)
  starting transfers between devices  96.4 us (15%)
  local copies, waits for them, and re-layouts  64.4 us (10%)
  other arithmetic  27.8 us (4%)
  matrix products  21.5 us (3%)
    all_to_all x10, waiting for transfers between devices, exchange(): lax.all_to_all(x, axis, split_axis=0, concat_axis=0, axis_index_groups=gr...  177 us
    pallas_call x1, Pallas kernels, factor(): pl.pallas_call(factor_kernel, out_shape=[jax.ShapeDtypeStruct((PANEL, PAN...  169 us
    all_to_all x10, starting transfers between devices, exchange(): lax.all_to_all(x, axis, split_axis=0, concat_axis=0, axis_index_groups=gr...  80.3 us
    ppermute x6, waiting for transfers between devices, from_first(): result = result + lax.ppermute(pieces[c], 'col', [(0, c)])  43.2 us
    unnamed x30, local copies, waits for them, and re-layouts  31.7 us
    dot_general x3, matrix products, times_transposed(): lax.dot_general(a, b, (((1,), (1,)), ((), ())), precision=precision, pref...  21.5 us
    pallas_call x2, Pallas kernels, collect(): pl.pallas_call(collect_kernel, grid_spec=pltpu.PrefetchScalarGridSpec(num...  18.8 us
    ppermute x6, starting transfers between devices, from_first(): result = result + lax.ppermute(pieces[c], 'col', [(0, c)])  14.8 us
  transfers between devices with their start and end apart: 18, of which 13 were waited for; matrix products, arithmetic and copies ran while one was open for 13% of the time, Pallas kernels for 31%

profile of v1, /device:TPU:1, one launch (start us, length us, event | category | flops | bytes accessed | tf_op | source)
XLA Modules:
  0.0 637.9 jit_solution(7452469417724816206)
XLA Ops:
  1.3 9.4 %all-to-all-start = ((s32[32,1,32]{2,1,0:T(1,128)}), s32[32,1,32]{2,1,0:T(1,128)S(1)}, u32[]{:S(2)}, u32[]{:S(2)}) async-start(s32[32,1,32]{2,1,0:T(1,128)} %broadcast_in_dim.28), calls=%async_computation | async-start | bytes 32768 | tf_op jit(solution)/shard_map/all_to_all | solution.py:241
  12.2 4.6 copy-done
  16.8 4.5 place_rows.2
  21.2 3.2 copy-done.3
  24.5 7.4 %all-to-all-start.1 = ((bf16[32,32,16,256]{3,2,1,0:T(8,128)(2,1)}), bf16[32,32,16,256]{3,2,1,0:T(8,128)(2,1)}, u32[]{:S(2)}, u32[]{:S(2)}) async-start(bf16[32,32,16,256]{3,2,1,0:T(8,128)(2,1)} %bitcast.92), calls=%async_computation.1 | async-start | bytes 16777216 | tf_op jit(solution)/shard_map/all_to_all | solution.py:241
  34.9 105.5 %all-to-all-done.1.got_ref = bf16[32,32,16,256]{3,2,1,0:T(8,128)(2,1)} async-done(((bf16[32,32,16,256]{3,2,1,0:T(8,128)(2,1)}), bf16[32,32,16,256]{3,2,1,0:T(8,128)(2,1)}, u32[]{:S(2)}, u32[]{:S(2)}) %all-to-all-start.1) | async-done | bytes 8388640 | tf_op jit(solution)/shard_map/all_to_all | solution.py:241
  140.5 21.4 %all-to-all-start.3 = ((f32[32,2,16,256]{3,2,1,0:T(8,128)}), f32[32,2,16,256]{3,2,1,0:T(8,128)S(1)}, u32[]{:S(2)}, u32[]{:S(2)}) async-start(f32[32,2,16,256]{3,2,1,0:T(8,128)} %bitcast.12), calls=%async_computation.3 | async-start | bytes 2097152 | tf_op jit(solution)/shard_map/all_to_all | solution.py:241
  163.2 9.6 %collect_parents.2 = f32[256,16,256]{2,1,0:T(8,128)S(1)} custom-call(s32[1024]{0:T(1024)S(1)} %reshape.228.at_ref, bf16[32,32,16,256]{3,2,1,0:T(8,128)(2,1)} %all-to-all-done.1.got_ref), custom_call_target="tpu_custom_call" | custom-call | flops 4194304 | bytes 12582912 | tf_op jit(solution)/shard_map/collect_parents/pallas_call | solution.py:82
  174.8 4.0 all-to-all-done.3
  180.5 4.6 collective-permute-start.2
  187.8 4.3 collective-permute-done.2
  193.4 7.0 %collective-permute-done = f32[20,16,256]{2,1,0:T(8,128)S(1)} collective-permute-done((f32[20,16,256]{2,1,0:T(8,128)S(1)}, f32[20,16,256]{2,1,0:T(8,128)S(1)}, u32[]{:S(2)}, u32[]{:S(2)}) %collective-permute-start) | collective-permute-done | bytes 327712 | tf_op jit(solution)/shard_map/ppermute | solution.py:259
  201.3 4.3 all-to-all-start.8
  205.6 4.5 all-to-all-done.8
  211.7 3.7 all-to-all-start.4
  215.4 4.6 copy-done.1
  220.0 2.8 place_rows.3
  224.8 18.9 %all-to-all-done.4 = f32[16,8,16,256]{3,2,1,0:T(8,128)S(1)} async-done(((f32[16,8,16,256]{3,2,1,0:T(8,128)}), f32[16,8,16,256]{3,2,1,0:T(8,128)S(1)}, u32[]{:S(2)}, u32[]{:S(2)}) %all-to-all-start.4) | async-done | bytes 2097184 | tf_op jit(solution)/shard_map/all_to_all | solution.py:241
  243.7 7.5 %all-to-all-start.5 = ((bf16[32,32,16,128]{3,2,1,0:T(8,128)(2,1)}), bf16[32,32,16,128]{3,2,1,0:T(8,128)(2,1)}, u32[]{:S(2)}, u32[]{:S(2)}) async-start(bf16[32,32,16,128]{3,2,1,0:T(8,128)(2,1)} %bitcast.95), calls=%async_computation.5 | async-start | bytes 8388608 | tf_op jit(solution)/shard_map/all_to_all | solution.py:241
  251.9 3.7 collective-permute-done.3
  255.6 2.2 select_bitcast_fusion.1
  257.8 2.6 pad_maximum_fusion
  260.4 43.1 %all-to-all-done.5.got_ref = bf16[32,32,16,128]{3,2,1,0:T(8,128)(2,1)} async-done(((bf16[32,32,16,128]{3,2,1,0:T(8,128)(2,1)}), bf16[32,32,16,128]{3,2,1,0:T(8,128)(2,1)}, u32[]{:S(2)}, u32[]{:S(2)}) %all-to-all-start.5) | async-done | bytes 4194336 | tf_op jit(solution)/shard_map/all_to_all | solution.py:241
  303.5 7.2 %all-to-all-start.2 = ((f32[32,8,16,256]{3,2,1,0:T(8,128)}), f32[32,8,16,256]{3,2,1,0:T(8,128)}, u32[]{:S(2)}, u32[]{:S(2)}) async-start(f32[32,8,16,256]{3,2,1,0:T(8,128)} %bitcast.94), calls=%async_computation.2 | async-start | bytes 8388608 | tf_op jit(solution)/shard_map/all_to_all | solution.py:241
  310.7 2.2 copy-done.11
  312.9 168.9 %factor_and_invert.1 = (f32[1024,1024]{1,0:T(8,128)S(1)}, f32[1024,1024]{1,0:T(8,128)S(1)}) custom-call(f32[32,8,16,256]{3,2,1,0:T(8,128)S(1)} %bitcast.98), custom_call_target="tpu_custom_call" | custom-call | flops 99999997952 | bytes 12582912 | tf_op jit(solution)/shard_map/factor_and_invert/pallas_call | solution.py:172
  483.8 4.0 fusion.25
  489.3 6.7 %all-to-all-start.9 = ((bf16[16,3,16,1024]{3,2,1,0:T(8,128)(2,1)}), bf16[16,3,16,1024]{3,2,1,0:T(8,128)(2,1)}, u32[]{:S(2)}, u32[]{:S(2)}) async-start(bf16[16,3,16,1024]{3,2,1,0:T(8,128)(2,1)} %broadcast_in_dim.52), calls=%async_computation.9 | async-start | bytes 3145728 | tf_op jit(solution)/shard_map/all_to_all | solution.py:241
  496.0 9.2 %collect_parents.3 = f32[256,16,128]{2,1,0:T(8,128)} custom-call(s32[1024]{0:T(1024)S(1)} %reshape.228.at_ref, bf16[32,32,16,128]{3,2,1,0:T(8,128)(2,1)} %all-to-all-done.5.got_ref), custom_call_target="tpu_custom_call" | custom-call | flops 2097152 | bytes 6291456 | tf_op jit(solution)/shard_map/collect_parents/pallas_call | solution.py:82
  505.2 8.1 %copy.27 = f32[8,8,16,4,256]{4,3,2,1,0:T(4,128)} copy(f32[8,8,16,4,256]{4,2,0,3,1:T(8,128)} %bitcast.8) | data formatting | bytes 8388608 | tf_op jit(solution)/shard_map/transpose | solution.py:289
  513.4 5.8 reshape.233
  519.2 6.8 %bitcast_add_fusion.1.panel_ref = f32[8,128,1024]{2,1,0:T(8,128)} fusion(f32[8,128,1024]{2,1,0:T(8,128)} %reshape.233, f32[8,1,128,1536]{3,2,0,1:T(8,128)} %bitcast.101), kind=kLoop, calls=%fused_computation.2 | loop fusion | flops 1048576 | bytes 12582912 | tf_op jit(solution)/shard_map/add | solution.py:290
  526.0 7.9 %all-to-all-start.6 = ((f32[32,8,16,128]{3,2,1,0:T(8,128)}), f32[32,8,16,128]{3,2,1,0:T(8,128)S(1)}, u32[]{:S(2)}, u32[]{:S(2)}) async-start(f32[32,8,16,128]{3,2,1,0:T(8,128)} %bitcast.22), calls=%async_computation.6 | async-start | bytes 4194304 | tf_op jit(solution)/shard_map/all_to_all | solution.py:241
  533.8 3.7 fusion.21
  538.9 2.3 collective-permute-start.5
  541.2 3.9 collective-permute-start.4
  545.1 4.7 slice.178
  549.8 5.2 copy.35
  555.0 6.7 %collective-permute-done.6 = f32[2,128,1024]{2,1,0:T(8,128)S(1)} collective-permute-done((f32[2,128,1024]{2,1,0:T(8,128)}, f32[2,128,1024]{2,1,0:T(8,128)S(1)}, u32[]{:S(2)}, u32[]{:S(2)}) %collective-permute-start.6) | collective-permute-done | bytes 1048608 | tf_op jit(solution)/shard_map/ppermute | solution.py:259
  563.1 22.5 %collective-permute-done.4 = f32[2,128,1024]{2,1,0:T(8,128)} collective-permute-done((f32[2,128,1024]{2,1,0:T(8,128)}, f32[2,128,1024]{2,1,0:T(8,128)}, u32[]{:S(2)}, u32[]{:S(2)}) %collective-permute-start.4) | collective-permute-done | bytes 1048608 | tf_op jit(solution)/shard_map/ppermute | solution.py:259
  585.6 2.3 fusion.2
  587.9 3.7 fusion.24
  595.4 4.7 all-to-all-start.7
  600.1 4.5 bitcast_add_fusion
  604.8 13.7 %fusion.23 = f32[1024,1024]{1,0:T(8,128)S(1)} fusion(f32[1024,1024]{1,0:T(8,128)S(1)} %bitcast_add_fusion, f32[1024,1024]{1,0:T(8,128)S(1)} %copy-done.8), kind=kOutput, calls=%fused_computation.49 | convolution fusion | flops 12884901888 | bytes 12582912 | tf_op jit(solution)/shard_map/dot_general | solution.py:16
  622.5 2.1 select_bitcast_fusion.3
  626.4 2.2 copy-done.2
  630.2 7.2 %trailing_update.1 = f32[8,1,128,1536]{3,2,1,0:T(8,128)} custom-call(s32[1]{0:T(128)} %bitcast.col_ref, f32[8,128,1024]{2,1,0:T(8,128)S(1)} %copy-done.2, f32[8,128,1024]{2,1,0:T(8,128)} %fusion.6.lower_ref, f32[8,1,128,1536]{3,2,1,0:T(8,128)} %front_ref.1, f32[8,4,8,16,128]{4,3,2,1,0:T(8,128)S(1)} %bitcast.97, bf16[8,128,1024]{2,1,0:T(8,128)(2,1)} %bitcast.25.spread_ref, ...), custom_call_target="tpu_custom_call" | custom-call | flops 3221225472 | bytes 29360128 | tf_op jit(solution)/shard_map/trailing_update/pallas_call | solution.py:214
  (66 shorter events, 36.6 us)
Async XLA Ops:
  1.3 23.2 %all-to-all-start = ((s32[32,1,32]{2,1,0:T(1,128)}), s32[32,1,32]{2,1,0:T(1,128)S(1)}, u32[]{:S(2)}, u32[]{:S(2)}) async-start(s32[32,1,32]{2,1,0:T(1,128)} %broadcast_in_dim.28), calls=%async_computation | async-start | bytes 32768 | tf_op jit(solution)/shard_map/all_to_all | solution.py:241
  12.2 4.6 copy-start
  21.2 3.3 copy-start.3
  24.5 116.0 %all-to-all-start.1 = ((bf16[32,32,16,256]{3,2,1,0:T(8,128)(2,1)}), bf16[32,32,16,256]{3,2,1,0:T(8,128)(2,1)}, u32[]{:S(2)}, u32[]{:S(2)}) async-start(bf16[32,32,16,256]{3,2,1,0:T(8,128)(2,1)} %bitcast.92), calls=%async_computation.1 | async-start | bytes 16777216 | tf_op jit(solution)/shard_map/all_to_all | solution.py:241
  140.5 38.3 %all-to-all-start.3 = ((f32[32,2,16,256]{3,2,1,0:T(8,128)}), f32[32,2,16,256]{3,2,1,0:T(8,128)S(1)}, u32[]{:S(2)}, u32[]{:S(2)}) async-start(f32[32,2,16,256]{3,2,1,0:T(8,128)} %bitcast.12), calls=%async_computation.3 | async-start | bytes 2097152 | tf_op jit(solution)/shard_map/all_to_all | solution.py:241
  172.8 2.0 copy-start.4
  180.5 11.6 %collective-permute-start.2 = (f32[20,16,256]{2,1,0:T(8,128)S(1)}, f32[20,16,256]{2,1,0:T(8,128)S(1)}, u32[]{:S(2)}, u32[]{:S(2)}) collective-permute-start(f32[20,16,256]{2,1,0:T(8,128)S(1)} %get-tuple-element.82), channel_id=1, source_target_pairs={{0,3},{4,7},{8,11},{12,15},{16,19},{20,23},{24,27},{28,31},{32,35}... | collective-permute-start | bytes 983048 | tf_op jit(solution)/shard_map/ppermute | solution.py:259
  185.2 8.3 %collective-permute-start.1 = (f32[20,16,256]{2,1,0:T(8,128)S(1)}, f32[20,16,256]{2,1,0:T(8,128)S(1)}, u32[]{:S(2)}, u32[]{:S(2)}) collective-permute-start(f32[20,16,256]{2,1,0:T(8,128)S(1)} %get-tuple-element.81), channel_id=1, source_target_pairs={{0,2},{4,6},{8,10},{12,14},{16,18},{20,22},{24,26},{28,30},{32,34}... | collective-permute-start | bytes 983048 | tf_op jit(solution)/shard_map/ppermute | solution.py:259
  186.5 14.0 %collective-permute-start = (f32[20,16,256]{2,1,0:T(8,128)S(1)}, f32[20,16,256]{2,1,0:T(8,128)S(1)}, u32[]{:S(2)}, u32[]{:S(2)}) collective-permute-start(f32[20,16,256]{2,1,0:T(8,128)S(1)} %get-tuple-element.80), channel_id=1, source_target_pairs={{0,1},{4,5},{8,9},{12,13},{16,17},{20,21},{24,25},{28,29},{32,33},... | collective-permute-start | bytes 983048 | tf_op jit(solution)/shard_map/ppermute | solution.py:259
  201.3 8.8 %all-to-all-start.8 = ((f32[4,3,16,256]{3,2,1,0:T(8,128)}), f32[4,3,16,256]{3,2,1,0:T(8,128)S(1)}, u32[]{:S(2)}, u32[]{:S(2)}) async-start(f32[4,3,16,256]{3,2,1,0:T(8,128)} %bitcast.26), calls=%async_computation.8 | async-start | bytes 393216 | tf_op jit(solution)/shard_map/all_to_all | solution.py:241
  211.7 32.0 %all-to-all-start.4 = ((f32[16,8,16,256]{3,2,1,0:T(8,128)}), f32[16,8,16,256]{3,2,1,0:T(8,128)S(1)}, u32[]{:S(2)}, u32[]{:S(2)}) async-start(f32[16,8,16,256]{3,2,1,0:T(8,128)} %broadcast_in_dim.49), calls=%async_computation.4 | async-start | bytes 4194304 | tf_op jit(solution)/shard_map/all_to_all | solution.py:241
  215.4 4.6 copy-start.1
  222.8 2.0 copy-start.5
  243.7 59.8 %all-to-all-start.5 = ((bf16[32,32,16,128]{3,2,1,0:T(8,128)(2,1)}), bf16[32,32,16,128]{3,2,1,0:T(8,128)(2,1)}, u32[]{:S(2)}, u32[]{:S(2)}) async-start(bf16[32,32,16,128]{3,2,1,0:T(8,128)(2,1)} %bitcast.95), calls=%async_computation.5 | async-start | bytes 8388608 | tf_op jit(solution)/shard_map/all_to_all | solution.py:241
  251.2 4.4 collective-permute-start.3
  303.5 184.4 %all-to-all-start.2 = ((f32[32,8,16,256]{3,2,1,0:T(8,128)}), f32[32,8,16,256]{3,2,1,0:T(8,128)}, u32[]{:S(2)}, u32[]{:S(2)}) async-start(f32[32,8,16,256]{3,2,1,0:T(8,128)} %bitcast.94), calls=%async_computation.2 | async-start | bytes 8388608 | tf_op jit(solution)/shard_map/all_to_all | solution.py:241
  310.7 2.2 copy-start.11
  481.7 2.0 copy-start.6
  481.7 6.1 copy-start.12
  489.3 36.7 %all-to-all-start.9 = ((bf16[16,3,16,1024]{3,2,1,0:T(8,128)(2,1)}), bf16[16,3,16,1024]{3,2,1,0:T(8,128)(2,1)}, u32[]{:S(2)}, u32[]{:S(2)}) async-start(bf16[16,3,16,1024]{3,2,1,0:T(8,128)(2,1)} %broadcast_in_dim.52), calls=%async_computation.9 | async-start | bytes 3145728 | tf_op jit(solution)/shard_map/all_to_all | solution.py:241
  526.0 67.6 %all-to-all-start.6 = ((f32[32,8,16,128]{3,2,1,0:T(8,128)}), f32[32,8,16,128]{3,2,1,0:T(8,128)S(1)}, u32[]{:S(2)}, u32[]{:S(2)}) async-start(f32[32,8,16,128]{3,2,1,0:T(8,128)} %bitcast.22), calls=%async_computation.6 | async-start | bytes 4194304 | tf_op jit(solution)/shard_map/all_to_all | solution.py:241
  537.5 24.2 %collective-permute-start.6 = (f32[2,128,1024]{2,1,0:T(8,128)}, f32[2,128,1024]{2,1,0:T(8,128)S(1)}, u32[]{:S(2)}, u32[]{:S(2)}) collective-permute-start(f32[2,128,1024]{2,1,0:T(8,128)} %get-tuple-element.70), channel_id=1, source_target_pairs={{0,3},{4,7},{8,11},{12,15},{16,19},{20,23},{24,27},{28,31},{32,35}... | collective-permute-start | bytes 3145736 | tf_op jit(solution)/shard_map/ppermute | solution.py:259
  538.9 24.2 %collective-permute-start.5 = (f32[2,128,1024]{2,1,0:T(8,128)}, f32[2,128,1024]{2,1,0:T(8,128)}, u32[]{:S(2)}, u32[]{:S(2)}) collective-permute-start(f32[2,128,1024]{2,1,0:T(8,128)} %get-tuple-element.71), channel_id=1, source_target_pairs={{0,2},{4,6},{8,10},{12,14},{16,18},{20,22},{24,26},{28,30},{32,34}... | collective-permute-start | bytes 3145736 | tf_op jit(solution)/shard_map/ppermute | solution.py:259
  541.2 44.4 %collective-permute-start.4 = (f32[2,128,1024]{2,1,0:T(8,128)}, f32[2,128,1024]{2,1,0:T(8,128)}, u32[]{:S(2)}, u32[]{:S(2)}) collective-permute-start(f32[2,128,1024]{2,1,0:T(8,128)} %get-tuple-element.69), channel_id=1, source_target_pairs={{0,1},{4,5},{8,9},{12,13},{16,17},{20,21},{24,25},{28,29},{32,33},... | collective-permute-start | bytes 3145736 | tf_op jit(solution)/shard_map/ppermute | solution.py:259
  555.0 32.9 %copy-start.7 = (f32[1024,1024]{1,0:T(8,128)S(1)}, f32[1024,1024]{1,0:T(8,128)}, u32[]{:S(2)}) copy-start(f32[1024,1024]{1,0:T(8,128)} %copy-done.6) | copy-start | bytes 12582916
  591.6 30.9 %collective-permute-start.7 = (bf16[16,3,16,1024]{3,2,1,0:T(8,128)(2,1)}, bf16[16,3,16,1024]{3,2,1,0:T(8,128)(2,1)}, u32[]{:S(2)}, u32[]{:S(2)}) collective-permute-start(bf16[16,3,16,1024]{3,2,1,0:T(8,128)(2,1)} %all-to-all-done.9), channel_id=1, source_target_pairs={{0,4},{4,0},{8,12},{12,8},{16,20},{20,16},{24,28},{28,24},{32,36},... | collective-permute-start | bytes 4718600 | tf_op jit(solution)/shard_map/ppermute | solution.py:250
  593.6 11.1 %copy-start.9 = (f32[32,8,16,128]{3,2,1,0:T(8,128)}, f32[32,8,16,128]{3,2,1,0:T(8,128)S(1)}, u32[]{:S(2)}) copy-start(f32[32,8,16,128]{3,2,1,0:T(8,128)S(1)} %all-to-all-done.6) | copy-start | bytes 6291460
  595.4 31.0 %all-to-all-start.7 = ((bf16[4,256,1024]{2,1,0:T(8,128)(2,1)}), bf16[4,256,1024]{2,1,0:T(8,128)(2,1)}, u32[]{:S(2)}, u32[]{:S(2)}) async-start(bf16[4,256,1024]{2,1,0:T(8,128)(2,1)} %broadcast_in_dim.51), calls=%async_computation.7 | async-start | bytes 4194304 | tf_op jit(solution)/shard_map/all_to_all | solution.py:241
  600.1 4.6 copy-start.8
  626.4 2.2 copy-start.2
  628.6 1.6 copy-start.10

commit v2 on v1

v2 whole, which is shorter than its diff:
```python
import jax
import jax.numpy as jnp
from jax import lax
from jax.experimental import pallas as pl
from jax.experimental.pallas import tpu as pltpu
from jax.sharding import PartitionSpec as P

PANEL = 1024
HIGH = lax.Precision.HIGHEST
f32 = jnp.float32
bf16 = jnp.bfloat16
MIB = 2**20


def times_transposed(a, b, precision=HIGH):
    return lax.dot_general(
        a, b, (((1,), (1,)), ((), ())), precision=precision, preferred_element_type=f32
    )


def times(a, b):
    return lax.dot_general(
        a, b, (((1,), (0,)), ((), ())), precision=HIGH, preferred_element_type=f32
    )


def place_kernel(rows_ref, child_ref, out_ref):
    width = out_ref.shape[-1]
    position = lax.broadcasted_iota(jnp.int32, (128, 128), 0)
    for slot in range(4):
        hot = jnp.where(rows_ref[0, slot : slot + 1, :] == position, 1.0, 0.0).astype(bf16)
        placed = jnp.dot(hot, child_ref[slot], preferred_element_type=f32).astype(bf16)
        for jp in range(8):
            for jc in range(4):
                out_ref[jp, jc, slot] = placed[
                    jp * 16 : jp * 16 + 16, jc * width : jc * width + width
                ]


def place(rows, child_tiles, width, block):
    slots = child_tiles.shape[0]
    return pl.pallas_call(
        place_kernel,
        grid=(slots // 4,),
        in_specs=[
            pl.BlockSpec((1, 4, 128), lambda t: (t, 0, 0)),
            pl.BlockSpec((4, 128, 4 * width), lambda t: (t, 0, block)),
        ],
        out_specs=pl.BlockSpec((8, 4, 4, 16, width), lambda t: (0, 0, t, 0, 0)),
        out_shape=jax.ShapeDtypeStruct((8, 4, slots, 16, width), bf16),
        compiler_params=pltpu.CompilerParams(vmem_limit_bytes=56 * MIB),
        cost_estimate=pl.CostEstimate(
            flops=2 * slots * 128 * 128 * 4 * width,
            bytes_accessed=2 * slots * 128 * 4 * width * 2,
            transcendentals=0,
        ),
        name="place_rows",
    )(rows.reshape(slots // 4, 4, 128), child_tiles)


def collect_kernel(at_ref, got_ref, out_ref):
    step = pl.program_id(0)

    @pl.when(step == 0)
    def _():
        out_ref[...] = jnp.zeros_like(out_ref)

    sources, slots = got_ref.shape[:2]

    def add(source, carry):
        base = (step * sources + source) * slots
        for slot in range(slots):
            at = at_ref[base + slot]
            out_ref[at] = out_ref[at] + got_ref[source, slot].astype(f32)
        return carry

    lax.fori_loop(0, sources, add, 0)


def collect(at, got):
    sources, slots, _, width = got.shape
    return pl.pallas_call(
        collect_kernel,
        grid_spec=pltpu.PrefetchScalarGridSpec(
            num_scalar_prefetch=1,
            grid=(sources // 4,),
            in_specs=[pl.BlockSpec((4, slots, 16, width), lambda s, at: (s, 0, 0, 0))],
            out_specs=pl.BlockSpec((256, 16, width), lambda s, at: (0, 0, 0)),
        ),
        out_shape=jax.ShapeDtypeStruct((256, 16, width), f32),
        compiler_params=pltpu.CompilerParams(vmem_limit_bytes=56 * MIB),
        cost_estimate=pl.CostEstimate(
            flops=sources * slots * 16 * width,
            bytes_accessed=sources * slots * 16 * width * 2 + 256 * 16 * width * 4,
            transcendentals=0,
        ),
        name="collect_parents",
    )(at, got)


def factor_block(block, u_ref, w_ref):
    sub = lax.broadcasted_iota(jnp.int32, (8, 128), 0)
    lane = lax.broadcasted_iota(jnp.int32, (8, 128), 1)

    def full(x):
        return jnp.broadcast_to(x, (8, 128))

    s = [block[8 * g : 8 * g + 8, :] for g in range(16)]
    v = [jnp.where(lane == sub + 8 * g, 1.0, 0.0).astype(f32) for g in range(16)]
    for b in range(16):
        cols = [full(s[b][:, 8 * b + j : 8 * b + j + 1]) for j in range(8)]
        e = [[full(cols[j][i : i + 1, :]) for j in range(i + 1)] for i in range(8)]
        inv, w, roots = [], [], []
        f = [[None] * 8 for _ in range(8)]
        for t in range(8):
            pivot = e[t][t]
            inv.append(1.0 / pivot)
            root = lax.rsqrt(pivot)
            roots.append(root * (1.5 - 0.5 * pivot * root * root))
            for i in range(t + 1, 8):
                f[i][t] = e[i][t] * inv[t]
            for i in range(t + 1, 8):
                for j in range(t + 1, i + 1):
                    e[i][j] = e[i][j] - f[i][t] * e[j][t]
        for i in range(8):
            r = []
            for j in range(i):
                acc = f[i][j]
                for k in range(j + 1, i):
                    acc = acc + f[i][k] * w[k][j]
                r.append(-acc)
            w.append(r)
        rows, vrows = s[b], v[b]
        new, vnew, scale = rows, vrows, roots[0]
        for i in range(1, 8):
            scale = jnp.where(sub == i, roots[i], scale)
        for j in range(7):
            c = jnp.zeros((8, 128), f32)
            for i in range(j + 1, 8):
                c = jnp.where(sub == i, w[i][j], c)
            new = new + c * full(rows[j : j + 1, :])
            vnew = vnew + c * full(vrows[j : j + 1, :])
        u_ref[8 * b : 8 * b + 8, :] = jnp.where(lane >= sub + 8 * b, new * scale, 0.0)
        w_ref[8 * b : 8 * b + 8, :] = vnew * scale
        if b == 15:
            break
        wi = [[w[t][j] * inv[t] for j in range(t)] for t in range(8)]
        brow = [full(new[t : t + 1, :]) for t in range(8)]
        bvrow = [full(vnew[t : t + 1, :]) for t in range(8)]
        for g in range(b + 1, 16):
            c = [full(s[g][:, 8 * b + j : 8 * b + j + 1]) for j in range(8)]
            for t in range(8):
                m = inv[t] * c[t]
                for j in range(t):
                    m = m + wi[t][j] * c[j]
                s[g] = s[g] - m * brow[t]
                v[g] = v[g] - m * bvrow[t]


def factor_kernel(index_ref, mine_ref, other_ref, l_ref, x_ref, a_ref, u_ref, w_ref):
    for half, ref in enumerate((mine_ref, other_ref)):
        for n in range(16):
            j = index_ref[half * 16 + n]
            cols = pl.ds(pl.multiple_of(j % 4 * 256, 256), 256)
            for tile in range(8):
                rows = pl.ds(pl.multiple_of(tile * 128 + j // 4 * 16, 16), 16)
                a_ref[rows, cols] = ref[n // 4, n % 4, tile]
    l_ref[...] = jnp.zeros_like(l_ref)
    x_ref[...] = jnp.zeros_like(x_ref)
    for i in range(8):
        for j in range(i + 1):
            bi, bj = slice(128 * i, 128 * i + 128), slice(128 * j, 128 * j + 128)
            a_ref[bi, bj] = 0.5 * (a_ref[bi, bj] + a_ref[bj, bi].T)

    def step(b, carry):
        at = pl.ds(pl.multiple_of(b * 128, 128), 128)
        factor_block(a_ref[at, at], u_ref, w_ref)
        w = w_ref[...]
        l_ref[at, at] = u_ref[...].T
        x_ref[at, at] = w
        for n in range(8):

            @pl.when(b == n)
            def _():
                here = slice(128 * n, 128 * n + 128)
                if n < 7:
                    below = slice(128 * n + 128, PANEL)
                    low = times_transposed(a_ref[below, here], w)
                    l_ref[below, here] = low
                    for j in range(n + 1, 8):
                        rows, cols = slice(128 * j, PANEL), slice(128 * j, 128 * j + 128)
                        off = 128 * (j - n - 1)
                        a_ref[rows, cols] = a_ref[rows, cols] - times_transposed(
                            low[off:], low[off : off + 128]
                        )
                if n > 0:
                    done = slice(0, 128 * n)
                    x_ref[here, done] = -times(w, times(l_ref[here, done], x_ref[done, done]))

        return carry

    lax.fori_loop(0, 8, step, 0)


def factor(index, mine, other):
    whole = pl.BlockSpec(memory_space=pltpu.VMEM)
    return pl.pallas_call(
        factor_kernel,
        in_specs=[pl.BlockSpec(memory_space=pltpu.SMEM), whole, whole],
        out_specs=[whole, whole],
        out_shape=[jax.ShapeDtypeStruct((PANEL, PANEL), f32)] * 2,
        scratch_shapes=[
            pltpu.VMEM((PANEL, PANEL), f32),
            pltpu.VMEM((128, 128), f32),
            pltpu.VMEM((128, 128), f32),
        ],
        compiler_params=pltpu.CompilerParams(vmem_limit_bytes=40 * MIB),
        cost_estimate=pl.CostEstimate(
            flops=7 * 10**10, bytes_accessed=12 * MIB, transcendentals=0
        ),
        name="factor_and_invert",
    )(index, mine, other)


def assemble_kernel(front_ref, got_ref, out_ref):
    for jc in range(4):
        cols = slice(jc * 256, jc * 256 + 256)
        out_ref[0, :, cols] = front_ref[0, 0, :, cols] + got_ref[:, jc, 0].reshape(128, 256)


def assemble(front, got):
    k = front.shape[0]
    return pl.pallas_call(
        assemble_kernel,
        grid=(k,),
        in_specs=[
            pl.BlockSpec((1, 1, 128, PANEL), lambda i: (i, 0, 0, 0)),
            pl.BlockSpec((8, 4, 1, 16, 256), lambda i: (0, 0, i, 0, 0)),
        ],
        out_specs=pl.BlockSpec((1, 128, PANEL), lambda i: (i, 0, 0)),
        out_shape=jax.ShapeDtypeStruct((k, 128, PANEL), f32),
        compiler_params=pltpu.CompilerParams(vmem_limit_bytes=56 * MIB),
        cost_estimate=pl.CostEstimate(
            flops=k * 128 * PANEL, bytes_accessed=12 * MIB, transcendentals=0
        ),
        name="assemble_panel",
    )(front, got)


def finish_kernel(
    order_ref, index_ref, panel_ref, lower_ref, top_ref, front_ref, got_ref, spread_ref,
    mine_ref, other_ref, out_ref, slab_ref,
):
    step = pl.program_id(0)
    tiles = panel_ref.shape[0]
    leading = order_ref[4] == 0

    @pl.when(step == 0)
    def _():
        for half, ref in enumerate((mine_ref, other_ref)):
            for n in range(16):
                j = index_ref[half * 16 + n]
                for q in range(3):
                    at = (j % 4 * 3 + q) * 128 + j // 4 * 16
                    slab_ref[pl.ds(pl.multiple_of(at, 16), 16), :] = ref[n // 4, n % 4, q]

    rows = spread_ref[0]

    @pl.when(leading)
    def _():
        out_ref[:, 0, :, :PANEL] = lower_ref[...]

    @pl.when(leading & (order_ref[step] == 0) & (order_ref[5] < 8))
    def _():
        out_ref[0, 0, :, :PANEL] = top_ref[...]

    @pl.when(jnp.logical_not(leading))
    def _():
        update = times_transposed(rows, slab_ref[:PANEL, :], None)
        out_ref[:, 0, :, :PANEL] = panel_ref[...] - update.reshape(tiles, 128, PANEL)

    update = times_transposed(rows, slab_ref[PANEL:, :], None).reshape(tiles, 128, -1)
    for jc in range(4):
        for tile in range(tiles):
            cols = slice(jc * 128, jc * 128 + 128)
            sums = got_ref[:, jc, tile].reshape(128, 128)
            out_ref[tile, 0, :, PANEL + jc * 128 : PANEL + jc * 128 + 128] = (
                front_ref[tile, 0, :, cols] + sums - update[tile, :, cols]
            )


def finish(order, index, panel, lower, top, front, got, spread, mine, other):
    k, _, _, width = front.shape
    step = k // 4
    return pl.pallas_call(
        finish_kernel,
        grid_spec=pltpu.PrefetchScalarGridSpec(
            num_scalar_prefetch=2,
            grid=(4,),
            in_specs=[
                pl.BlockSpec((step, 128, PANEL), lambda i, o, _: (o[i], 0, 0)),
                pl.BlockSpec((step, 128, PANEL), lambda i, o, _: (o[i], 0, 0)),
                pl.BlockSpec((128, PANEL), lambda i, o, _: (0, 0)),
                pl.BlockSpec((step, 1, 128, 512), lambda i, o, _: (o[i], 0, 0, 2)),
                pl.BlockSpec((8, 4, step, 16, 128), lambda i, o, _: (0, 0, o[i], 0, 0)),
                pl.BlockSpec((1, step * 128, PANEL), lambda i, o, _: (i, 0, 0)),
                pl.BlockSpec(mine.shape, lambda i, o, _: (0, 0, 0, 0, 0)),
                pl.BlockSpec(other.shape, lambda i, o, _: (0, 0, 0, 0, 0)),
            ],
            out_specs=pl.BlockSpec((step, 1, 128, width), lambda i, o, _: (o[i], 0, 0, 0)),
            scratch_shapes=[pltpu.VMEM((width, PANEL), bf16)],
        ),
        out_shape=jax.ShapeDtypeStruct(front.shape, f32),
        compiler_params=pltpu.CompilerParams(vmem_limit_bytes=48 * MIB),
        cost_estimate=pl.CostEstimate(
            flops=2 * k * 128 * width * PANEL,
            bytes_accessed=28 * MIB,
            transcendentals=0,
        ),
        name="trailing_update",
    )(order, index, panel, lower, top, front, got, spread, mine, other)


def exchange(x):
    return lax.all_to_all(x, "row", split_axis=0, concat_axis=0, tiled=True)


def row_number(x, z, core):
    return (x % 4 * 4 + z % 4) * 2 + core


def ring_stage(x, stage):
    parts = [x]
    for by in range(1, 4):
        moves = []
        for chip in range(16):
            for core in range(2):
                along_z = core == stage
                to = row_number(
                    chip // 4 + (0 if along_z else by), chip % 4 + (by if along_z else 0), core
                )
                moves.append((chip * 2 + core, to))
        parts.append(lax.ppermute(x, "row", moves))
    return jnp.stack(parts)


def gather_rows(x):
    mine = ring_stage(ring_stage(x, 0), 1)
    other = lax.ppermute(mine, "row", [(r, r ^ 1) for r in range(32)])
    return mine, other


def gathered_index(row_index):
    number = jnp.arange(32, dtype=jnp.int32)
    half, outer, inner = number // 16, number // 4 % 4, number % 4
    core = (row_index + half) % 2
    chip = row_index // 2
    x = chip // 4 - jnp.where(core == 0, outer, inner) + 4
    z = chip % 4 - jnp.where(core == 0, inner, outer) + 4
    return row_number(x, z, core)


def from_first(pieces, col_index):
    result = jnp.where(col_index == 0, pieces[0], 0)
    for c in range(1, len(pieces)):
        result = result + lax.ppermute(pieces[c], "col", [(0, c)])
    return result


def own_rows(tiles, row_index):
    tiles = tiles.reshape(4, 3, 16, 256)
    quarter = row_index % 4
    result = jnp.zeros((3, 16, PANEL), f32)
    for by in range(4):
        part = lax.dynamic_index_in_dim(tiles, quarter ^ by, 0, keepdims=False)
        if by:
            part = lax.ppermute(part, "row", [(r, r ^ by) for r in range(32)])
        result = lax.dynamic_update_slice(result, part, (0, 0, (quarter ^ by) * 256))
    return result.reshape(48, PANEL)


def together(*arrays):
    return lax.optimization_barrier(arrays)


def body(front, child_tiles, tile_parent, tile_rows, tile_count):
    row_index = lax.axis_index("row").astype(jnp.int32)
    col_index = lax.axis_index("col").astype(jnp.int32)
    slots = child_tiles.shape[0]
    index = gathered_index(row_index)
    live = jnp.arange(slots, dtype=jnp.int32) < tile_count[0]
    rows = jnp.where(live[:, None], tile_rows, -1)
    at = (tile_parent % 32) * 8 + tile_parent // 32
    at = lax.all_gather(at, "row", axis=0, tiled=True)

    early = front[:2, 0, :, :PANEL].reshape(2, 8, 16, 4, 256).transpose(1, 3, 0, 2, 4)
    early = exchange(early.reshape(32, 2, 16, 256))

    sent = place(rows, child_tiles, 256, 0).reshape(32, slots, 16, 256)
    sent, early = together(sent, early)
    sums = collect(at, exchange(sent)).reshape(32, 8, 16, 256)
    sent_rest = place(rows, child_tiles, 128, 2).reshape(32, slots, 16, 128)

    tiles = (sums[:, :2] + early).transpose(1, 0, 2, 3).reshape(64, 16, 256)
    diagonal = from_first([tiles[:8]] * 4, col_index)
    part = from_first([tiles[12 * c : 12 * c + 12] for c in range(4)], col_index)
    diagonal = gather_rows(diagonal)
    part = own_rows(part, row_index)

    got, sent_rest = together(exchange(sums), sent_rest)
    panel = assemble(front, got.reshape(8, 4, 8, 16, 256))
    own = from_first([panel[2 * c : 2 * c + 2] for c in range(4)], col_index)
    got_rest = exchange(sent_rest)

    factored, inverse = factor(index, *diagonal)

    def rows_of_factor(start, count):
        start = jnp.minimum(start, PANEL - count)
        return lax.dynamic_slice_in_dim(factored, start, count, 0)

    part = times_transposed(part, inverse).reshape(3, 16, PANEL)
    known, tile = [], 12 * col_index + 3 * (row_index % 4)
    for q in range(3):
        known.append(rows_of_factor((tile + q) * 128 + row_index // 4 * 16, 16))
    inside = tile + jnp.arange(3, dtype=jnp.int32) < 8
    part = jnp.where(inside[:, None, None], jnp.stack(known), part).astype(bf16)
    slab = gather_rows(part)

    top = rows_of_factor(row_index * 128, 128)
    own = times_transposed(own.reshape(256, PANEL), inverse)
    inside = (jnp.arange(256) < 128) & (row_index < 8) & (col_index == 0)
    own = jnp.where(inside[:, None], jnp.concatenate([top, top]), own).astype(bf16)
    spread = jnp.stack(
        [own] + [lax.ppermute(own, "col", [(c, (c + s) % 4) for c in range(4)]) for s in (1, 2, 3)]
    )

    got_rest, inverse, _, _ = together(got_rest, inverse, part, own)
    sums_rest = collect(at, got_rest)
    got_rest = exchange(sums_rest.reshape(32, 8, 16, 128)).reshape(8, 4, 8, 16, 128)
    lower = times_transposed(panel.reshape(8 * 128, PANEL), inverse).reshape(8, 128, PANEL)

    order = (col_index + 4 - jnp.arange(4, dtype=jnp.int32)) % 4
    order = jnp.concatenate([order, jnp.stack([col_index, row_index])])
    return finish(order, index, panel, lower, top, front, got_rest, spread, *slab)


def solution(mesh):
    placed = (
        P(None, "row", None, "col"),
        P("row", None, "col"),
        P("row"),
        P("row", None),
        P("row"),
    )
    return jax.shard_map(
        body, mesh=mesh, in_specs=placed, out_specs=P(None, "row", None, "col"), check_vma=False
    )
```

time: 647 us -> 480 us (0.74)
  waiting for transfers between devices: 224 us -> 94 us
  blocking collectives: 0 us -> 106 us
  Pallas kernels: 202 us -> 131 us
  local copies, waits for them, and re-layouts: 64.4 us -> 6.1 us
  other arithmetic: 27.8 us -> 11.8 us
    all_to_all x10 -> x5, waiting for transfers between devices: 177 us -> 5.19 us  [exchange(): return lax.all_to_all(x, 'row', split_axis=0, concat_axis=0, tiled=True)]
    unnamed x0 -> x1, blocking collectives: none -> 106 us
    pallas_call x1 -> x2, Pallas kernels: 169 us -> 81.6 us  [the longest x1 74 us: factor(): pl.pallas_call(factor_kernel, in_specs=[pl.BlockSpec(memory_space=pltpu.S...]
    ppermute x2 -> x20, waiting for transfers between devices: 3.74 us -> 81.4 us  [the longest x12 54.8 us: ring_stage(): parts.append(lax.ppermute(x, 'row', moves))]
    ppermute x6 -> x9, waiting for transfers between devices: 43.2 us -> 7.42 us  [from_first(): result = result + lax.ppermute(pieces[c], 'col', [(0, c)])]
    unnamed x30 -> x14, local copies, waits for them, and re-layouts: 31.7 us -> 0.61 us
    all_to_all x10 -> x5, starting transfers between devices: 80.3 us -> 51.9 us  [exchange(): return lax.all_to_all(x, 'row', split_axis=0, concat_axis=0, tiled=True)]
    ppermute x2 -> x20, starting transfers between devices: 1.31 us -> 26.1 us  [the longest x12 18.5 us: ring_stage(): parts.append(lax.ppermute(x, 'row', moves))]
  transfers between devices with their start and end apart: 18 -> 34, of which waited for: 13 -> 17; matrix products, arithmetic and copies ran while one was open for 13% -> 9% of each run, Pallas kernels for 31% -> 23%
where the time goes in v2:
time: 480 us; the launch traced here: 476 us
  Pallas kernels  131 us (27%)
  blocking collectives  106 us (22%)
  starting transfers between devices  99.2 us (21%)
  waiting for transfers between devices  94 us (20%)
  matrix products  26.1 us (5%)
  other arithmetic  11.8 us (2%)
  local copies, waits for them, and re-layouts  6.1 us (1%)
    unnamed x1, blocking collectives  106 us
    pallas_call x1, Pallas kernels, factor(): pl.pallas_call(factor_kernel, in_specs=[pl.BlockSpec(memory_space=pltpu.S...  74 us
    ppermute x12, waiting for transfers between devices, ring_stage(): parts.append(lax.ppermute(x, 'row', moves))  54.8 us
    all_to_all x5, starting transfers between devices, exchange(): return lax.all_to_all(x, 'row', split_axis=0, concat_axis=0, tiled=True)  51.9 us
    dot_general x3, matrix products, times_transposed(): lax.dot_general(a, b, (((1,), (1,)), ((), ())), precision=precision, pref...  26.1 us
    ppermute x3, waiting for transfers between devices, body(): lax.ppermute(own, 'col', [(c, (c + s) % 4) for c in range(4)])  23.6 us
    ppermute x9, starting transfers between devices, from_first(): result = result + lax.ppermute(pieces[c], 'col', [(0, c)])  21.2 us
    pallas_call x2, Pallas kernels, collect(): pl.pallas_call(collect_kernel, grid_spec=pltpu.PrefetchScalarGridSpec(num...  20.9 us
  transfers between devices with their start and end apart: 34, of which 17 were waited for; matrix products, arithmetic and copies ran while one was open for 9% of the time, Pallas kernels for 23%

profile of v2, /device:TPU:1, one launch (start us, length us, event | category | flops | bytes accessed | tf_op | source)
XLA Modules:
  0.0 475.9 jit_solution(12792338603932011235)
XLA Ops:
  0.0 1.3 slice.33
  3.0 9.4 %all-to-all-start = ((f32[32,2,16,256]{3,2,1,0:T(8,128)}), f32[32,2,16,256]{3,2,1,0:T(8,128)S(1)}, u32[]{:S(2)}, u32[]{:S(2)}) async-start(f32[32,2,16,256]{3,2,1,0:T(8,128)} %bitcast.7), calls=%async_computation | async-start | bytes 2097152 | tf_op jit(solution)/shard_map/all_to_all | solution.py:325
  13.8 10.4 %place_rows.2 = bf16[8,4,32,16,256]{4,3,2,1,0:T(8,128)(2,1)} custom-call(s32[8,4,128]{2,1,0:T(4,128)} %bitcast.91, bf16[32,128,1536]{2,1,0:T(8,128)(2,1)} %child_ref.3), custom_call_target="tpu_custom_call" | custom-call | flops 1073741824 | bytes 16777216 | tf_op jit(solution)/shard_map/place_rows/pallas_call | solution.py:42
  24.1 5.2 %all-to-all-done = f32[32,2,16,256]{3,2,1,0:T(8,128)S(1)} async-done(((f32[32,2,16,256]{3,2,1,0:T(8,128)}), f32[32,2,16,256]{3,2,1,0:T(8,128)S(1)}, u32[]{:S(2)}, u32[]{:S(2)}) %all-to-all-start) | async-done | bytes 1048608 | tf_op jit(solution)/shard_map/all_to_all | solution.py:325
  29.3 4.9 %all-to-all-start.1 = ((bf16[32,32,16,256]{3,2,1,0:T(8,128)(2,1)}), bf16[32,32,16,256]{3,2,1,0:T(8,128)(2,1)}, u32[]{:S(2)}, u32[]{:S(2)}) async-start(bf16[32,32,16,256]{3,2,1,0:T(8,128)(2,1)} %bitcast.74), calls=%async_computation.1 | async-start | bytes 16777216 | tf_op jit(solution)/shard_map/all_to_all | solution.py:325
  35.6 106.0 %all-reduce.at_ref = s32[1024]{0:T(1024)} all-reduce(s32[1024]{0:T(1024)S(1)} %fusion.26), channel_id=1, replica_groups=mesh['row'=32,'col'=4] {'row'}, use_global_device_ids=true, to_apply=%add | all-reduce | flops 1024 | bytes 8192
  141.6 11.6 %collect_parents.2 = f32[256,16,256]{2,1,0:T(8,128)} custom-call(s32[1024]{0:T(1024)} %all-reduce.at_ref, bf16[32,32,16,256]{3,2,1,0:T(8,128)(2,1)} %all-to-all-done.1.got_ref), custom_call_target="tpu_custom_call" | custom-call | flops 4194304 | bytes 12582912 | tf_op jit(solution)/shard_map/collect_parents/pallas_call | solution.py:82
  153.3 26.3 %all-to-all-start.2 = ((f32[32,8,16,256]{3,2,1,0:T(8,128)}), f32[32,8,16,256]{3,2,1,0:T(8,128)}, u32[]{:S(2)}, u32[]{:S(2)}) async-start(f32[32,8,16,256]{3,2,1,0:T(8,128)} %bitcast.75), calls=%async_computation.2 | async-start | bytes 8388608 | tf_op jit(solution)/shard_map/all_to_all | solution.py:325
  179.6 1.5 fusion.13
  181.2 4.8 %collective-permute-start.1 = (f32[8,16,256]{2,1,0:T(8,128)S(1)}, f32[8,16,256]{2,1,0:T(8,128)S(1)}, u32[]{:S(2)}, u32[]{:S(2)}) collective-permute-start(f32[8,16,256]{2,1,0:T(8,128)S(1)} %slice.45), channel_id=1, source_target_pairs={{0,2},{4,6},{8,10},{12,14},{16,18},{20,22},{24,26},{28,30},{32,34}... | collective-permute-start | bytes 393224 | tf_op jit(solution)/shard_map/ppermute | solution.py:366
  188.6 2.7 collective-permute-done
  191.4 2.7 collective-permute-start.5
  195.2 37.2 %collective-permute-done.5 = f32[8,16,256]{2,1,0:T(8,128)S(1)} collective-permute-done((f32[8,16,256]{2,1,0:T(8,128)S(1)}, f32[8,16,256]{2,1,0:T(8,128)S(1)}, u32[]{:S(2)}, u32[]{:S(2)}) %collective-permute-start.5) | collective-permute-done | bytes 131104 | tf_op jit(solution)/shard_map/ppermute | solution.py:343
  233.4 2.7 collective-permute-start.7
  236.7 2.3 collective-permute-start.8
  239.0 4.1 collective-permute-done.7
  243.1 5.5 %collective-permute-done.6 = f32[4,8,16,256]{3,2,1,0:T(8,128)S(1)} collective-permute-done((f32[4,8,16,256]{3,2,1,0:T(8,128)S(1)}, f32[4,8,16,256]{3,2,1,0:T(8,128)S(1)}, u32[]{:S(2)}, u32[]{:S(2)}) %collective-permute-start.6) | collective-permute-done | bytes 524320 | tf_op jit(solution)/shard_map/ppermute | solution.py:343
  249.3 7.6 %place_rows.3 = bf16[8,4,32,16,128]{4,3,2,1,0:T(8,128)(2,1)} custom-call(s32[8,4,128]{2,1,0:T(4,128)} %bitcast.92, bf16[32,128,1536]{2,1,0:T(8,128)(2,1)} %child_ref.3), custom_call_target="tpu_custom_call" | custom-call | flops 536870912 | bytes 8388608 | tf_op jit(solution)/shard_map/place_rows/pallas_call | solution.py:42
  256.9 3.2 collective-permute-start.10
  260.2 2.1 collective-permute-start.12
  264.1 2.1 collective-permute-done.12
  266.2 2.1 collective-permute-done.11
  269.3 4.0 collective-permute-start.15
  274.7 2.2 collective-permute-done.14
  276.9 5.4 %all-to-all-start.3 = ((bf16[32,32,16,128]{3,2,1,0:T(8,128)(2,1)}), bf16[32,32,16,128]{3,2,1,0:T(8,128)(2,1)}, u32[]{:S(2)}, u32[]{:S(2)}) async-start(bf16[32,32,16,128]{3,2,1,0:T(8,128)(2,1)} %bitcast.77), calls=%async_computation.3 | async-start | bytes 8388608 | tf_op jit(solution)/shard_map/all_to_all | solution.py:325
  282.3 7.6 %assemble_panel.1.panel_ref = f32[8,128,1024]{2,1,0:T(8,128)} custom-call(f32[8,1,128,1536]{3,2,1,0:T(8,128)} %front_ref.3, f32[8,4,8,16,256]{4,3,2,1,0:T(8,128)} %bitcast.10.got_ref), custom_call_target="tpu_custom_call" | custom-call | flops 1048576 | bytes 12582912 | tf_op jit(solution)/shard_map/assemble_panel/pallas_call | solution.py:233
  289.9 2.2 fusion.34
  292.2 1.4 collective-permute-start.16
  293.5 2.6 collective-permute-start.18
  296.1 3.2 collective-permute-start.17
  299.3 74.0 %factor_and_invert.1 = (f32[1024,1024]{1,0:T(8,128)S(1)}, f32[1024,1024]{1,0:T(8,128)S(1)}) custom-call(s32[32]{0:T(128)S(1)} %multiply_add_fusion.index_ref, f32[4,4,8,16,256]{4,3,2,1,0:T(8,128)S(1)} %pad_maximum_fusion.mine_ref, f32[4,4,8,16,256]{4,3,2,1,0:T(8,128)} %collective-permute-done.9.other_ref), custom_call_target="tpu_custom_call" | custom-call | flops 70000001024 | bytes 12582912 | tf_op jit(solution)/shard_map/factor_and_invert/pallas_call | solution.py:207
  373.4 4.0 fusion.7
  377.4 2.7 collective-permute-start.24
  382.4 2.7 collective-permute-done.23
  385.1 3.1 collective-permute-done.22
  389.0 2.6 collective-permute-start.26
  392.0 2.2 collective-permute-start.27
  394.3 1.7 fusion.12
  396.0 4.6 fusion.15
  400.5 9.3 %collect_parents.3 = f32[256,16,128]{2,1,0:T(8,128)} custom-call(s32[1024]{0:T(1024)} %all-reduce.at_ref, bf16[32,32,16,128]{3,2,1,0:T(8,128)(2,1)} %all-to-all-done.3.got_ref), custom_call_target="tpu_custom_call" | custom-call | flops 2097152 | bytes 6291456 | tf_op jit(solution)/shard_map/collect_parents/pallas_call | solution.py:82
  409.8 5.9 %all-to-all-start.4 = ((f32[32,8,16,128]{3,2,1,0:T(8,128)}), f32[32,8,16,128]{3,2,1,0:T(8,128)S(1)}, u32[]{:S(2)}, u32[]{:S(2)}) async-start(f32[32,8,16,128]{3,2,1,0:T(8,128)} %bitcast.78), calls=%async_computation.4 | async-start | bytes 4194304 | tf_op jit(solution)/shard_map/all_to_all | solution.py:325
  415.8 2.6 pad_maximum_fusion.2.mine_ref
  418.7 2.7 collective-permute-start.21
  421.5 12.5 %collective-permute-done.20 = bf16[256,1024]{1,0:T(8,128)(2,1)} collective-permute-done((bf16[256,1024]{1,0:T(8,128)(2,1)}, bf16[256,1024]{1,0:T(8,128)(2,1)}, u32[]{:S(2)}, u32[]{:S(2)}) %collective-permute-start.20) | collective-permute-done | bytes 524320 | tf_op jit(solution)/shard_map/ppermute | solution.py:434
  434.0 11.1 %collective-permute-done.19 = bf16[256,1024]{1,0:T(8,128)(2,1)} collective-permute-done((bf16[256,1024]{1,0:T(8,128)(2,1)}, bf16[256,1024]{1,0:T(8,128)(2,1)}, u32[]{:S(2)}, u32[]{:S(2)}) %collective-permute-start.19) | collective-permute-done | bytes 524320 | tf_op jit(solution)/shard_map/ppermute | solution.py:434
  445.1 3.0 pad_maximum_fusion.1.spread_ref
  448.1 17.5 %fusion.lower_ref = f32[8,128,1024]{2,1,0:T(8,128)} fusion(f32[8,128,1024]{2,1,0:T(8,128)} %assemble_panel.1.panel_ref, f32[1024,1024]{1,0:T(8,128)S(1)} %copy-done.1), kind=kOutput, calls=%fused_computation | convolution fusion | flops 12884901888 | bytes 12582912 | tf_op jit(solution)/shard_map/dot_general | solution.py:16
  465.6 10.1 %trailing_update.1 = f32[8,1,128,1536]{3,2,1,0:T(8,128)} custom-call(s32[6]{0:T(128)S(1)} %pad_add_fusion.order_ref, s32[32]{0:T(128)S(1)} %multiply_add_fusion.index_ref, f32[8,128,1024]{2,1,0:T(8,128)} %assemble_panel.1.panel_ref, f32[8,128,1024]{2,1,0:T(8,128)} %fusion.lower_ref, f32[128,1024]{1,0:T(8,128)S(1)} %constant_dynamic-slice_fusion.top_ref, ...), custom_call_target="tpu_custom_call" | custom-call | flops 3221225472 | bytes 29360128 | tf_op jit(solution)/shard_map/trailing_update/pallas_call | solution.py:295
  (77 shorter events, 17.3 us)
Async XLA Ops:
  0.0 13.1 %copy-start.3 = (s32[32,128]{1,0:T(8,128)S(1)}, s32[32,128]{1,0:T(8,128)}, u32[]{:S(2)}) copy-start(s32[32,128]{1,0:T(8,128)} %param.8) | copy-start | bytes 49156
  3.0 26.4 %all-to-all-start = ((f32[32,2,16,256]{3,2,1,0:T(8,128)}), f32[32,2,16,256]{3,2,1,0:T(8,128)S(1)}, u32[]{:S(2)}, u32[]{:S(2)}) async-start(f32[32,2,16,256]{3,2,1,0:T(8,128)} %bitcast.7), calls=%async_computation | async-start | bytes 2097152 | tf_op jit(solution)/shard_map/all_to_all | solution.py:325
  29.3 4.9 %copy-start.5 = (u32[128]{0:T(128)S(1)}, u32[128]{0:T(128)}, u32[]{:S(2)}) copy-start(u32[128]{0:T(128)} %constant.186) | copy-start | bytes 1540
  29.3 6.2 %copy-start.4 = (s32[32]{0:T(128)S(1)}, s32[32]{0:T(128)}, u32[]{:S(2)}) copy-start(s32[32]{0:T(128)} %param.7) | copy-start | bytes 388
  29.3 112.3 %all-to-all-start.1 = ((bf16[32,32,16,256]{3,2,1,0:T(8,128)(2,1)}), bf16[32,32,16,256]{3,2,1,0:T(8,128)(2,1)}, u32[]{:S(2)}, u32[]{:S(2)}) async-start(bf16[32,32,16,256]{3,2,1,0:T(8,128)(2,1)} %bitcast.74), calls=%async_computation.1 | async-start | bytes 16777216 | tf_op jit(solution)/shard_map/all_to_all | solution.py:325
  153.3 123.7 %all-to-all-start.2 = ((f32[32,8,16,256]{3,2,1,0:T(8,128)}), f32[32,8,16,256]{3,2,1,0:T(8,128)}, u32[]{:S(2)}, u32[]{:S(2)}) async-start(f32[32,8,16,256]{3,2,1,0:T(8,128)} %bitcast.75), calls=%async_computation.2 | async-start | bytes 8388608 | tf_op jit(solution)/shard_map/all_to_all | solution.py:325
  181.2 75.7 %copy-start.2 = (f32[2,32,16,256]{3,2,1,0:T(8,128)}, f32[2,32,16,256]{3,2,1,0:T(8,128)S(1)}, u32[]{:S(2)}) copy-start(f32[2,32,16,256]{3,2,1,0:T(8,128)S(1)} %copy.9) | copy-start | bytes 3145732
  181.2 7.5 %collective-permute-start.1 = (f32[8,16,256]{2,1,0:T(8,128)S(1)}, f32[8,16,256]{2,1,0:T(8,128)S(1)}, u32[]{:S(2)}, u32[]{:S(2)}) collective-permute-start(f32[8,16,256]{2,1,0:T(8,128)S(1)} %slice.45), channel_id=1, source_target_pairs={{0,2},{4,6},{8,10},{12,14},{16,18},{20,22},{24,26},{28,30},{32,34}... | collective-permute-start | bytes 393224 | tf_op jit(solution)/shard_map/ppermute | solution.py:366
  186.0 5.4 %collective-permute-start = (f32[8,16,256]{2,1,0:T(8,128)S(1)}, f32[8,16,256]{2,1,0:T(8,128)S(1)}, u32[]{:S(2)}, u32[]{:S(2)}) collective-permute-start(f32[8,16,256]{2,1,0:T(8,128)S(1)} %slice.45), channel_id=1, source_target_pairs={{0,1},{4,5},{8,9},{12,13},{16,17},{20,21},{24,25},{28,29},{32,33},... | collective-permute-start | bytes 393224 | tf_op jit(solution)/shard_map/ppermute | solution.py:366
  187.3 4.1 collective-permute-start.2
  191.4 41.0 %collective-permute-start.5 = (f32[8,16,256]{2,1,0:T(8,128)S(1)}, f32[8,16,256]{2,1,0:T(8,128)S(1)}, u32[]{:S(2)}, u32[]{:S(2)}) collective-permute-start(f32[8,16,256]{2,1,0:T(8,128)S(1)} %add_add_fusion), channel_id=1, source_target_pairs={{0,24},{4,100},{8,0},{12,108},{16,8},{20,116},{24,16},{28,124},{32... | collective-permute-start | bytes 393224 | tf_op jit(solution)/shard_map/ppermute | solution.py:343
  194.1 39.2 %collective-permute-start.4 = (f32[8,16,256]{2,1,0:T(8,128)S(1)}, f32[8,16,256]{2,1,0:T(8,128)S(1)}, u32[]{:S(2)}, u32[]{:S(2)}) collective-permute-start(f32[8,16,256]{2,1,0:T(8,128)S(1)} %add_add_fusion), channel_id=1, source_target_pairs={{0,16},{4,68},{8,24},{12,76},{16,0},{20,84},{24,8},{28,92},{32,48}... | collective-permute-start | bytes 393224 | tf_op jit(solution)/shard_map/ppermute | solution.py:343
  194.6 38.7 %collective-permute-start.3 = (f32[8,16,256]{2,1,0:T(8,128)S(1)}, f32[8,16,256]{2,1,0:T(8,128)S(1)}, u32[]{:S(2)}, u32[]{:S(2)}) collective-permute-start(f32[8,16,256]{2,1,0:T(8,128)S(1)} %add_add_fusion), channel_id=1, source_target_pairs={{0,8},{4,36},{8,16},{12,44},{16,24},{20,52},{24,0},{28,60},{32,40}... | collective-permute-start | bytes 393224 | tf_op jit(solution)/shard_map/ppermute | solution.py:343
  233.4 9.7 %collective-permute-start.7 = (f32[4,8,16,256]{3,2,1,0:T(8,128)S(1)}, f32[4,8,16,256]{3,2,1,0:T(8,128)S(1)}, u32[]{:S(2)}, u32[]{:S(2)}) collective-permute-start(f32[4,8,16,256]{3,2,1,0:T(8,128)S(1)} %get-tuple-element.33), channel_id=1, source_target_pairs={{0,64},{4,20},{8,72},{12,28},{16,80},{20,4},{24,88},{28,12},{32,96... | collective-permute-start | bytes 1572872 | tf_op jit(solution)/shard_map/ppermute | solution.py:343
  236.1 12.5 %collective-permute-start.6 = (f32[4,8,16,256]{3,2,1,0:T(8,128)S(1)}, f32[4,8,16,256]{3,2,1,0:T(8,128)S(1)}, u32[]{:S(2)}, u32[]{:S(2)}) collective-permute-start(f32[4,8,16,256]{3,2,1,0:T(8,128)S(1)} %get-tuple-element.33), channel_id=1, source_target_pairs={{0,32},{4,12},{8,40},{12,20},{16,48},{20,28},{24,56},{28,4},{32,64... | collective-permute-start | bytes 1572872 | tf_op jit(solution)/shard_map/ppermute | solution.py:343
  236.7 12.1 %collective-permute-start.8 = (f32[4,8,16,256]{3,2,1,0:T(8,128)S(1)}, f32[4,8,16,256]{3,2,1,0:T(8,128)S(1)}, u32[]{:S(2)}, u32[]{:S(2)}) collective-permute-start(f32[4,8,16,256]{3,2,1,0:T(8,128)S(1)} %get-tuple-element.33), channel_id=1, source_target_pairs={{0,96},{4,28},{8,104},{12,4},{16,112},{20,12},{24,120},{28,20},{32... | collective-permute-start | bytes 1572872 | tf_op jit(solution)/shard_map/ppermute | solution.py:343
  249.1 50.3 %collective-permute-start.9 = (f32[4,4,8,16,256]{4,3,2,1,0:T(8,128)S(1)}, f32[4,4,8,16,256]{4,3,2,1,0:T(8,128)}, u32[]{:S(2)}, u32[]{:S(2)}) collective-permute-start(f32[4,4,8,16,256]{4,3,2,1,0:T(8,128)S(1)} %pad_maximum_fusion.mine_ref), channel_id=1, source_target_pairs={{0,4},{4,0},{8,12},{12,8},{16,20},{20,16},{24,28},{28,24},{32,36},... | collective-permute-start | bytes 6291464 | tf_op jit(solution)/shard_map/ppermute | solution.py:349
  256.9 7.1 %collective-permute-start.10 = (f32[12,16,256]{2,1,0:T(8,128)S(1)}, f32[12,16,256]{2,1,0:T(8,128)S(1)}, u32[]{:S(2)}, u32[]{:S(2)}) collective-permute-start(f32[12,16,256]{2,1,0:T(8,128)S(1)} %get-tuple-element.29), channel_id=1, source_target_pairs={{0,1},{4,5},{8,9},{12,13},{16,17},{20,21},{24,25},{28,29},{32,33},... | collective-permute-start | bytes 589832 | tf_op jit(solution)/shard_map/ppermute | solution.py:366
  260.2 6.0 %collective-permute-start.12 = (f32[12,16,256]{2,1,0:T(8,128)S(1)}, f32[12,16,256]{2,1,0:T(8,128)S(1)}, u32[]{:S(2)}, u32[]{:S(2)}) collective-permute-start(f32[12,16,256]{2,1,0:T(8,128)S(1)} %get-tuple-element.30), channel_id=1, source_target_pairs={{0,3},{4,7},{8,11},{12,15},{16,19},{20,23},{24,27},{28,31},{32,35}... | collective-permute-start | bytes 589832 | tf_op jit(solution)/shard_map/ppermute | solution.py:366
  262.3 6.0 %collective-permute-start.11 = (f32[12,16,256]{2,1,0:T(8,128)S(1)}, f32[12,16,256]{2,1,0:T(8,128)S(1)}, u32[]{:S(2)}, u32[]{:S(2)}) collective-permute-start(f32[12,16,256]{2,1,0:T(8,128)S(1)} %get-tuple-element.31), channel_id=1, source_target_pairs={{0,2},{4,6},{8,10},{12,14},{16,18},{20,22},{24,26},{28,30},{32,34}... | collective-permute-start | bytes 589832 | tf_op jit(solution)/shard_map/ppermute | solution.py:366
  269.3 7.6 %collective-permute-start.15 = (f32[3,16,256]{2,1,0:T(8,128)S(1)}, f32[3,16,256]{2,1,0:T(8,128)S(1)}, u32[]{:S(2)}, u32[]{:S(2)}) collective-permute-start(f32[3,16,256]{2,1,0:T(8,128)S(1)} %get-tuple-element.36), channel_id=1, source_target_pairs={{0,12},{4,8},{8,4},{12,0},{16,28},{20,24},{24,20},{28,16},{32,44},... | collective-permute-start | bytes 147464 | tf_op jit(solution)/shard_map/ppermute | solution.py:377
  273.3 3.5 collective-permute-start.14
  273.3 1.4 collective-permute-start.13
  276.9 123.6 %all-to-all-start.3 = ((bf16[32,32,16,128]{3,2,1,0:T(8,128)(2,1)}), bf16[32,32,16,128]{3,2,1,0:T(8,128)(2,1)}, u32[]{:S(2)}, u32[]{:S(2)}) async-start(bf16[32,32,16,128]{3,2,1,0:T(8,128)(2,1)} %bitcast.77), calls=%async_computation.3 | async-start | bytes 8388608 | tf_op jit(solution)/shard_map/all_to_all | solution.py:325
  292.2 99.9 %collective-permute-start.16 = (f32[2,128,1024]{2,1,0:T(8,128)S(1)}, f32[2,128,1024]{2,1,0:T(8,128)S(1)}, u32[]{:S(2)}, u32[]{:S(2)}) collective-permute-start(f32[2,128,1024]{2,1,0:T(8,128)S(1)} %get-tuple-element.21), channel_id=1, source_target_pairs={{0,1},{4,5},{8,9},{12,13},{16,17},{20,21},{24,25},{28,29},{32,33},... | collective-permute-start | bytes 3145736 | tf_op jit(solution)/shard_map/ppermute | solution.py:366
  293.5 100.7 %collective-permute-start.18 = (f32[2,128,1024]{2,1,0:T(8,128)S(1)}, f32[2,128,1024]{2,1,0:T(8,128)S(1)}, u32[]{:S(2)}, u32[]{:S(2)}) collective-permute-start(f32[2,128,1024]{2,1,0:T(8,128)S(1)} %get-tuple-element.22), channel_id=1, source_target_pairs={{0,3},{4,7},{8,11},{12,15},{16,19},{20,23},{24,27},{28,31},{32,35}... | collective-permute-start | bytes 3145736 | tf_op jit(solution)/shard_map/ppermute | solution.py:366
  296.1 98.1 %collective-permute-start.17 = (f32[2,128,1024]{2,1,0:T(8,128)S(1)}, f32[2,128,1024]{2,1,0:T(8,128)S(1)}, u32[]{:S(2)}, u32[]{:S(2)}) collective-permute-start(f32[2,128,1024]{2,1,0:T(8,128)S(1)} %get-tuple-element.23), channel_id=1, source_target_pairs={{0,2},{4,6},{8,10},{12,14},{16,18},{20,22},{24,26},{28,30},{32,34}... | collective-permute-start | bytes 3145736 | tf_op jit(solution)/shard_map/ppermute | solution.py:366
  373.3 22.6 %copy-start = (f32[1024,1024]{1,0:T(8,128)}, f32[1024,1024]{1,0:T(8,128)S(1)}, u32[]{:S(2)}) copy-start(f32[1024,1024]{1,0:T(8,128)S(1)} %get-tuple-element.19) | copy-start | bytes 12582916
  377.4 4.4 collective-permute-start.24
  380.2 5.0 %collective-permute-start.23 = (bf16[3,16,1024]{2,1,0:T(8,128)(2,1)S(1)}, bf16[3,16,1024]{2,1,0:T(8,128)(2,1)S(1)}, u32[]{:S(2)}, u32[]{:S(2)}) collective-permute-start(bf16[3,16,1024]{2,1,0:T(8,128)(2,1)S(1)} %fusion.7), channel_id=1, source_target_pairs={{0,16},{4,68},{8,24},{12,76},{16,0},{20,84},{24,8},{28,92},{32,48}... | collective-permute-start | bytes 294920 | tf_op jit(solution)/shard_map/ppermute | solution.py:343
  381.8 6.4 %collective-permute-start.22 = (bf16[3,16,1024]{2,1,0:T(8,128)(2,1)S(1)}, bf16[3,16,1024]{2,1,0:T(8,128)(2,1)S(1)}, u32[]{:S(2)}, u32[]{:S(2)}) collective-permute-start(bf16[3,16,1024]{2,1,0:T(8,128)(2,1)S(1)} %fusion.7), channel_id=1, source_target_pairs={{0,8},{4,36},{8,16},{12,44},{16,24},{20,52},{24,0},{28,60},{32,40}... | collective-permute-start | bytes 294920 | tf_op jit(solution)/shard_map/ppermute | solution.py:343
  389.0 26.8 %collective-permute-start.26 = (bf16[4,3,16,1024]{3,2,1,0:T(8,128)(2,1)}, bf16[4,3,16,1024]{3,2,1,0:T(8,128)(2,1)}, u32[]{:S(2)}, u32[]{:S(2)}) collective-permute-start(bf16[4,3,16,1024]{3,2,1,0:T(8,128)(2,1)} %get-tuple-element.35), channel_id=1, source_target_pairs={{0,64},{4,20},{8,72},{12,28},{16,80},{20,4},{24,88},{28,12},{32,96... | collective-permute-start | bytes 1179656 | tf_op jit(solution)/shard_map/ppermute | solution.py:343
  391.6 24.2 %collective-permute-start.25 = (bf16[4,3,16,1024]{3,2,1,0:T(8,128)(2,1)}, bf16[4,3,16,1024]{3,2,1,0:T(8,128)(2,1)}, u32[]{:S(2)}, u32[]{:S(2)}) collective-permute-start(bf16[4,3,16,1024]{3,2,1,0:T(8,128)(2,1)} %get-tuple-element.35), channel_id=1, source_target_pairs={{0,32},{4,12},{8,40},{12,20},{16,48},{20,28},{24,56},{28,4},{32,64... | collective-permute-start | bytes 1179656 | tf_op jit(solution)/shard_map/ppermute | solution.py:343
  392.0 23.8 %collective-permute-start.27 = (bf16[4,3,16,1024]{3,2,1,0:T(8,128)(2,1)}, bf16[4,3,16,1024]{3,2,1,0:T(8,128)(2,1)}, u32[]{:S(2)}, u32[]{:S(2)}) collective-permute-start(bf16[4,3,16,1024]{3,2,1,0:T(8,128)(2,1)} %get-tuple-element.35), channel_id=1, source_target_pairs={{0,96},{4,28},{8,104},{12,4},{16,112},{20,12},{24,120},{28,20},{32... | collective-permute-start | bytes 1179656 | tf_op jit(solution)/shard_map/ppermute | solution.py:343
  409.8 55.8 %all-to-all-start.4 = ((f32[32,8,16,128]{3,2,1,0:T(8,128)}), f32[32,8,16,128]{3,2,1,0:T(8,128)S(1)}, u32[]{:S(2)}, u32[]{:S(2)}) async-start(f32[32,8,16,128]{3,2,1,0:T(8,128)} %bitcast.78), calls=%async_computation.4 | async-start | bytes 4194304 | tf_op jit(solution)/shard_map/all_to_all | solution.py:325
  418.4 47.2 %collective-permute-start.28 = (bf16[4,4,3,16,1024]{4,3,2,1,0:T(8,128)(2,1)}, bf16[4,4,3,16,1024]{4,3,2,1,0:T(8,128)(2,1)}, u32[]{:S(2)}, u32[]{:S(2)}) collective-permute-start(bf16[4,4,3,16,1024]{4,3,2,1,0:T(8,128)(2,1)} %pad_maximum_fusion.2.mine_ref), channel_id=1, source_target_pairs={{0,4},{4,0},{8,12},{12,8},{16,20},{20,16},{24,28},{28,24},{32,36},... | collective-permute-start | bytes 4718600 | tf_op jit(solution)/shard_map/ppermute | solution.py:349
  418.7 15.2 %collective-permute-start.20 = (bf16[256,1024]{1,0:T(8,128)(2,1)}, bf16[256,1024]{1,0:T(8,128)(2,1)}, u32[]{:S(2)}, u32[]{:S(2)}) collective-permute-start(bf16[256,1024]{1,0:T(8,128)(2,1)} %get-tuple-element.28), channel_id=1, source_target_pairs={{0,2},{1,3},{2,0},{3,1},{4,6},{5,7},{6,4},{7,5},{8,10},{9,11},{10,... | collective-permute-start | bytes 1572872 | tf_op jit(solution)/shard_map/ppermute | solution.py:434
  418.7 26.4 %collective-permute-start.19 = (bf16[256,1024]{1,0:T(8,128)(2,1)}, bf16[256,1024]{1,0:T(8,128)(2,1)}, u32[]{:S(2)}, u32[]{:S(2)}) collective-permute-start(bf16[256,1024]{1,0:T(8,128)(2,1)} %get-tuple-element.28), channel_id=1, source_target_pairs={{0,1},{1,2},{2,3},{3,0},{4,5},{5,6},{6,7},{7,4},{8,9},{9,10},{10,1... | collective-permute-start | bytes 1572872 | tf_op jit(solution)/shard_map/ppermute | solution.py:434
  418.7 26.4 %collective-permute-start.21 = (bf16[256,1024]{1,0:T(8,128)(2,1)}, bf16[256,1024]{1,0:T(8,128)(2,1)}, u32[]{:S(2)}, u32[]{:S(2)}) collective-permute-start(bf16[256,1024]{1,0:T(8,128)(2,1)} %get-tuple-element.28), channel_id=1, source_target_pairs={{0,3},{1,0},{2,1},{3,2},{4,7},{5,4},{6,5},{7,6},{8,11},{9,8},{10,9... | collective-permute-start | bytes 1572872 | tf_op jit(solution)/shard_map/ppermute | solution.py:434
  421.4 26.7 %copy-start.1 = (f32[1024,1024]{1,0:T(8,128)S(1)}, f32[1024,1024]{1,0:T(8,128)}, u32[]{:S(2)}) copy-start(f32[1024,1024]{1,0:T(8,128)} %copy-done) | copy-start | bytes 12582916

commit v3 on v2

--- a/solution.py
+++ b/solution.py
@@ -58,7 +58,8 @@
     )(rows.reshape(slots // 4, 4, 128), child_tiles)
 
 
-def collect_kernel(at_ref, got_ref, out_ref):
+def collect_kernel(at_ref, got_ref, *refs):
+    out_ref = refs[-1]
     step = pl.program_id(0)
 
     @pl.when(step == 0)
@@ -77,14 +78,15 @@
     lax.fori_loop(0, sources, add, 0)
 
 
-def collect(at, got):
+def collect(at, got, *after):
     sources, slots, _, width = got.shape
     return pl.pallas_call(
         collect_kernel,
         grid_spec=pltpu.PrefetchScalarGridSpec(
             num_scalar_prefetch=1,
             grid=(sources // 4,),
-            in_specs=[pl.BlockSpec((4, slots, 16, width), lambda s, at: (s, 0, 0, 0))],
+            in_specs=[pl.BlockSpec((4, slots, 16, width), lambda s, at: (s, 0, 0, 0))]
+            + [pl.BlockSpec(memory_space=pl.ANY)] * len(after),
             out_specs=pl.BlockSpec((256, 16, width), lambda s, at: (0, 0, 0)),
         ),
         out_shape=jax.ShapeDtypeStruct((256, 16, width), f32),
@@ -95,7 +97,7 @@
             transcendentals=0,
         ),
         name="collect_parents",
-    )(at, got)
+    )(at, got, *after)
 
 
 def factor_block(block, u_ref, w_ref):
@@ -157,14 +159,15 @@
                 v[g] = v[g] - m * bvrow[t]
 
 
-def factor_kernel(index_ref, mine_ref, other_ref, l_ref, x_ref, a_ref, u_ref, w_ref):
-    for half, ref in enumerate((mine_ref, other_ref)):
-        for n in range(16):
-            j = index_ref[half * 16 + n]
+def factor_kernel(index_ref, *refs):
+    pieces, (l_ref, x_ref, a_ref, u_ref, w_ref) = refs[:8], refs[8:]
+    for part, ref in enumerate(pieces):
+        for n in range(4):
+            j = index_ref[part * 4 + n]
             cols = pl.ds(pl.multiple_of(j % 4 * 256, 256), 256)
             for tile in range(8):
                 rows = pl.ds(pl.multiple_of(tile * 128 + j // 4 * 16, 16), 16)
-                a_ref[rows, cols] = ref[n // 4, n % 4, tile]
+                a_ref[rows, cols] = ref[n, tile]
     l_ref[...] = jnp.zeros_like(l_ref)
     x_ref[...] = jnp.zeros_like(x_ref)
     for i in range(8):
@@ -202,11 +205,11 @@
     lax.fori_loop(0, 8, step, 0)
 
 
-def factor(index, mine, other):
+def factor(index, pieces):
     whole = pl.BlockSpec(memory_space=pltpu.VMEM)
     return pl.pallas_call(
         factor_kernel,
-        in_specs=[pl.BlockSpec(memory_space=pltpu.SMEM), whole, whole],
+        in_specs=[pl.BlockSpec(memory_space=pltpu.SMEM)] + [whole] * 8,
         out_specs=[whole, whole],
         out_shape=[jax.ShapeDtypeStruct((PANEL, PANEL), f32)] * 2,
         scratch_shapes=[
@@ -219,7 +222,7 @@
             flops=7 * 10**10, bytes_accessed=12 * MIB, transcendentals=0
         ),
         name="factor_and_invert",
-    )(index, mine, other)
+    )(index, *pieces)
 
 
 def assemble_kernel(front_ref, got_ref, out_ref):
@@ -247,24 +250,32 @@
     )(front, got)
 
 
-def finish_kernel(
-    order_ref, index_ref, panel_ref, lower_ref, top_ref, front_ref, got_ref, spread_ref,
-    mine_ref, other_ref, out_ref, slab_ref,
-):
+def finish_kernel(order_ref, index_ref, panel_ref, lower_ref, top_ref, front_ref, got_ref, *refs):
+    spread, pieces, (out_ref, slab_ref, rows_ref) = refs[:5], refs[5:13], refs[13:]
     step = pl.program_id(0)
     tiles = panel_ref.shape[0]
     leading = order_ref[4] == 0
 
     @pl.when(step == 0)
     def _():
-        for half, ref in enumerate((mine_ref, other_ref)):
-            for n in range(16):
-                j = index_ref[half * 16 + n]
+        for part, ref in enumerate(pieces):
+            for n in range(4):
+                j = index_ref[part * 4 + n]
                 for q in range(3):
                     at = (j % 4 * 3 + q) * 128 + j // 4 * 16
-                    slab_ref[pl.ds(pl.multiple_of(at, 16), 16), :] = ref[n // 4, n % 4, q]
-
-    rows = spread_ref[0]
+                    slab_ref[pl.ds(pl.multiple_of(at, 16), 16), :] = ref[n, q]
+
+    for number in range(4):
+
+        @pl.when(step == number)
+        def _():
+            if number == 2:
+                rows_ref[:128, :] = spread[2][...]
+                rows_ref[128:, :] = spread[3][...]
+            else:
+                rows_ref[...] = spread[number + number // 3][...]
+
+    rows = rows_ref[...]
 
     @pl.when(leading)
     def _():
@@ -289,7 +300,7 @@
             )
 
 
-def finish(order, index, panel, lower, top, front, got, spread, mine, other):
+def finish(order, index, panel, lower, top, front, got, spread, pieces):
     k, _, _, width = front.shape
     step = k // 4
     return pl.pallas_call(
@@ -303,22 +314,24 @@
                 pl.BlockSpec((128, PANEL), lambda i, o, _: (0, 0)),
                 pl.BlockSpec((step, 1, 128, 512), lambda i, o, _: (o[i], 0, 0, 2)),
                 pl.BlockSpec((8, 4, step, 16, 128), lambda i, o, _: (0, 0, o[i], 0, 0)),
-                pl.BlockSpec((1, step * 128, PANEL), lambda i, o, _: (i, 0, 0)),
-                pl.BlockSpec(mine.shape, lambda i, o, _: (0, 0, 0, 0, 0)),
-                pl.BlockSpec(other.shape, lambda i, o, _: (0, 0, 0, 0, 0)),
+            ]
+            + [pl.BlockSpec(x.shape, lambda i, o, _: (0, 0)) for x in spread]
+            + [pl.BlockSpec(x.shape, lambda i, o, _: (0, 0, 0, 0)) for x in pieces],
+            out_specs=pl.BlockSpec((step, 1, 128, width), lambda i, o, _: (o[i], 0, 0, 0)),
+            scratch_shapes=[
+                pltpu.VMEM((width, PANEL), bf16),
+                pltpu.VMEM((step * 128, PANEL), bf16),
             ],
-            out_specs=pl.BlockSpec((step, 1, 128, width), lambda i, o, _: (o[i], 0, 0, 0)),
-            scratch_shapes=[pltpu.VMEM((width, PANEL), bf16)],
         ),
         out_shape=jax.ShapeDtypeStruct(front.shape, f32),
-        compiler_params=pltpu.CompilerParams(vmem_limit_bytes=48 * MIB),
+        compiler_params=pltpu.CompilerParams(vmem_limit_bytes=60 * MIB),
         cost_estimate=pl.CostEstimate(
             flops=2 * k * 128 * width * PANEL,
             bytes_accessed=28 * MIB,
             transcendentals=0,
         ),
         name="trailing_update",
-    )(order, index, panel, lower, top, front, got, spread, mine, other)
+    )(order, index, panel, lower, top, front, got, *spread, *pieces)
 
 
 def exchange(x):
@@ -341,13 +354,12 @@
                 )
                 moves.append((chip * 2 + core, to))
         parts.append(lax.ppermute(x, "row", moves))
-    return jnp.stack(parts)
-
-
-def gather_rows(x):
-    mine = ring_stage(ring_stage(x, 0), 1)
-    other = lax.ppermute(mine, "row", [(r, r ^ 1) for r in range(32)])
-    return mine, other
+    return parts
+
+
+def gather_rows(ring):
+    mine = ring_stage(ring, 1)
+    return mine + [lax.ppermute(part, "row", [(r, r ^ 1) for r in range(32)]) for part in mine]
 
 
 def gathered_index(row_index):
@@ -391,57 +403,71 @@
     live = jnp.arange(slots, dtype=jnp.int32) < tile_count[0]
     rows = jnp.where(live[:, None], tile_rows, -1)
     at = (tile_parent % 32) * 8 + tile_parent // 32
-    at = lax.all_gather(at, "row", axis=0, tiled=True)
 
     early = front[:2, 0, :, :PANEL].reshape(2, 8, 16, 4, 256).transpose(1, 3, 0, 2, 4)
-    early = exchange(early.reshape(32, 2, 16, 256))
+    at = jnp.pad(at.astype(f32).reshape(1, slots), ((0, 7), (0, 256 - slots)))
+    early = jnp.concatenate(
+        [early.reshape(32, 32, 256), jnp.broadcast_to(at[None], (32, 8, 256))], axis=1
+    )
+    early = exchange(early)
+    at = early[:, 32, :slots].astype(jnp.int32).reshape(32 * slots)
+    early = early[:, :32].reshape(32, 2, 16, 256)
 
     sent = place(rows, child_tiles, 256, 0).reshape(32, slots, 16, 256)
-    sent, early = together(sent, early)
-    sums = collect(at, exchange(sent)).reshape(32, 8, 16, 256)
+    sent, early, at = together(sent, early, at)
     sent_rest = place(rows, child_tiles, 128, 2).reshape(32, slots, 16, 128)
+    got, sent_rest = together(exchange(sent), sent_rest)
+    sums = collect(at, got).reshape(32, 8, 16, 256)
 
     tiles = (sums[:, :2] + early).transpose(1, 0, 2, 3).reshape(64, 16, 256)
-    diagonal = from_first([tiles[:8]] * 4, col_index)
-    part = from_first([tiles[12 * c : 12 * c + 12] for c in range(4)], col_index)
-    diagonal = gather_rows(diagonal)
-    part = own_rows(part, row_index)
+    pieces = [jnp.concatenate([tiles[:8], tiles[12 * c : 12 * c + 12]]) for c in range(4)]
+    piece = from_first(pieces, col_index)
+    ring, part = together(jnp.stack(ring_stage(piece[:8], 0)), own_rows(piece[8:], row_index))
+    diagonal = gather_rows(ring)
 
     got, sent_rest = together(exchange(sums), sent_rest)
     panel = assemble(front, got.reshape(8, 4, 8, 16, 256))
     own = from_first([panel[2 * c : 2 * c + 2] for c in range(4)], col_index)
     got_rest = exchange(sent_rest)
 
-    factored, inverse = factor(index, *diagonal)
+    factored, inverse = factor(index, diagonal)
 
     def rows_of_factor(start, count):
         start = jnp.minimum(start, PANEL - count)
         return lax.dynamic_slice_in_dim(factored, start, count, 0)
 
-    part = times_transposed(part, inverse).reshape(3, 16, PANEL)
-    known, tile = [], 12 * col_index + 3 * (row_index % 4)
+    top = rows_of_factor(row_index * 128, 128)
+    known, tile = [top], 12 * col_index + 3 * (row_index % 4)
     for q in range(3):
         known.append(rows_of_factor((tile + q) * 128 + row_index // 4 * 16, 16))
-    inside = tile + jnp.arange(3, dtype=jnp.int32) < 8
-    part = jnp.where(inside[:, None, None], jnp.stack(known), part).astype(bf16)
-    slab = gather_rows(part)
-
-    top = rows_of_factor(row_index * 128, 128)
-    own = times_transposed(own.reshape(256, PANEL), inverse)
-    inside = (jnp.arange(256) < 128) & (row_index < 8) & (col_index == 0)
-    own = jnp.where(inside[:, None], jnp.concatenate([top, top]), own).astype(bf16)
-    spread = jnp.stack(
-        [own] + [lax.ppermute(own, "col", [(c, (c + s) % 4) for c in range(4)]) for s in (1, 2, 3)]
-    )
-
-    got_rest, inverse, _, _ = together(got_rest, inverse, part, own)
-    sums_rest = collect(at, got_rest)
+    known = jnp.concatenate(known)
+    inside = jnp.concatenate(
+        [
+            jnp.broadcast_to((row_index < 8) & (col_index == 0), (128,)),
+            jnp.repeat(tile + jnp.arange(3, dtype=jnp.int32) < 8, 16, total_repeat_length=48),
+        ]
+    )
+    solved = jnp.concatenate([own.reshape(256, PANEL), part])
+    solved = times_transposed(solved, inverse)
+    both = jnp.concatenate([solved[:128], solved[256:]])
+    both = jnp.where(inside[:, None], known, both).astype(bf16)
+    own = jnp.concatenate([both[:128], solved[128:256].astype(bf16)])
+    part = both[128:].reshape(3, 16, PANEL)
+
+    def turn(x, by):
+        return lax.ppermute(x, "col", [(c, (c + by) % 4) for c in range(4)])
+
+    ring, before, behind = together(jnp.stack(ring_stage(part, 0)), turn(own, 1), turn(own, 3))
+    spread = [own, before, turn(before[:128], 1), turn(behind[128:], 3), behind]
+    slab = gather_rows(ring)
+
+    sums_rest = collect(at, got_rest, own, part)
     got_rest = exchange(sums_rest.reshape(32, 8, 16, 128)).reshape(8, 4, 8, 16, 128)
     lower = times_transposed(panel.reshape(8 * 128, PANEL), inverse).reshape(8, 128, PANEL)
 
     order = (col_index + 4 - jnp.arange(4, dtype=jnp.int32)) % 4
     order = jnp.concatenate([order, jnp.stack([col_index, row_index])])
-    return finish(order, index, panel, lower, top, front, got_rest, spread, *slab)
+    return finish(order, index, panel, lower, top, front, got_rest, spread, slab)
 
 
 def solution(mesh):

time: 480 us -> 459 us (0.956)
  blocking collectives: 106 us -> 0 us
  waiting for transfers between devices: 94 us -> 181 us
  local copies, waits for them, and re-layouts: 6.1 us -> 11.7 us
    unnamed x1 -> x0, blocking collectives: 106 us -> none
    all_to_all x5, waiting for transfers between devices: 5.19 us -> 107 us  [exchange(): return lax.all_to_all(x, 'row', split_axis=0, concat_axis=0, tiled=True)]
    ppermute x3, waiting for transfers between devices: 3 us -> 26.2 us  [own_rows(): part = lax.ppermute(part, 'row', [(r, r ^ by) for r in range(32)])]
    ppermute x12, waiting for transfers between devices: 54.8 us -> 33 us  [ring_stage(): parts.append(lax.ppermute(x, 'row', moves))]
    ppermute x5 -> x12, waiting for transfers between devices: 23.6 us -> 3.92 us  [the longest x4 3.9 us: turn(): return lax.ppermute(x, 'col', [(c, (c + by) % 4) for c in range(4)])]
    ppermute x5 -> x12, starting transfers between devices: 3.11 us -> 11.8 us  [the longest x8 10.3 us: gather_rows(): lax.ppermute(part, 'row', [(r, r ^ 1) for r in range(32)])]
    ppermute x9 -> x6, starting transfers between devices: 21.2 us -> 13.6 us  [from_first(): result = result + lax.ppermute(pieces[c], 'col', [(0, c)])]
    another operation x5 -> x2, other arithmetic: 6.69 us -> 0.98 us  [the longest x1 0.94 us: body(): jnp.stack(ring_stage(part, 0))]
  transfers between devices with their start and end apart: 34 -> 38, of which waited for: 17 -> 15; matrix products, arithmetic and copies ran while one was open for 9% -> 8% of each run, Pallas kernels for 23% -> 22%
where the time goes in v3:
time: 459 us; the launch traced here: 456 us
  waiting for transfers between devices  181 us (39%)
  Pallas kernels  131 us (29%)
  starting transfers between devices  97.4 us (21%)
  matrix products  22.1 us (5%)
  local copies, waits for them, and re-layouts  11.7 us (3%)
  other arithmetic  11.4 us (2%)
    all_to_all x5, waiting for transfers between devices, exchange(): return lax.all_to_all(x, 'row', split_axis=0, concat_axis=0, tiled=True)  107 us
    pallas_call x1, Pallas kernels, factor(): pl.pallas_call(factor_kernel, in_specs=[pl.BlockSpec(memory_space=pltpu.S...  73.4 us
    all_to_all x5, starting transfers between devices, exchange(): return lax.all_to_all(x, 'row', split_axis=0, concat_axis=0, tiled=True)  50.9 us
    ppermute x12, waiting for transfers between devices, ring_stage(): parts.append(lax.ppermute(x, 'row', moves))  33 us
    ppermute x3, waiting for transfers between devices, own_rows(): part = lax.ppermute(part, 'row', [(r, r ^ by) for r in range(32)])  26.2 us
    dot_general x2, matrix products, times_transposed(): lax.dot_general(a, b, (((1,), (1,)), ((), ())), precision=precision, pref...  22.1 us
    pallas_call x2, Pallas kernels, collect(): pl.pallas_call(collect_kernel, grid_spec=pltpu.PrefetchScalarGridSpec(num...  21.1 us
    pallas_call x2, Pallas kernels, place(): pl.pallas_call(place_kernel, grid=(slots // 4,), in_specs=[pl.BlockSpec((...  17.9 us
  transfers between devices with their start and end apart: 38, of which 15 were waited for; matrix products, arithmetic and copies ran while one was open for 8% of the time, Pallas kernels for 22%

profile of v3, /device:TPU:1, one launch (start us, length us, event | category | flops | bytes accessed | tf_op | source)
XLA Modules:
  0.0 455.6 jit_solution(14086831732935182377)
XLA Ops:
  3.9 9.4 %all-to-all-start = ((f32[32,40,256]{2,1,0:T(8,128)}), f32[32,40,256]{2,1,0:T(8,128)S(1)}, u32[]{:S(2)}, u32[]{:S(2)}) async-start(f32[32,40,256]{2,1,0:T(8,128)} %pad_maximum_fusion), calls=%async_computation | async-start | bytes 2621440 | tf_op jit(solution)/shard_map/all_to_all | solution.py:338
  14.7 10.3 %place_rows.2 = bf16[8,4,32,16,256]{4,3,2,1,0:T(8,128)(2,1)} custom-call(s32[8,4,128]{2,1,0:T(4,128)} %bitcast.70, bf16[32,128,1536]{2,1,0:T(8,128)(2,1)} %child_ref.3), custom_call_target="tpu_custom_call" | custom-call | flops 1073741824 | bytes 16777216 | tf_op jit(solution)/shard_map/place_rows/pallas_call | solution.py:42
  25.0 8.1 %all-to-all-done = f32[32,40,256]{2,1,0:T(8,128)S(1)} async-done(((f32[32,40,256]{2,1,0:T(8,128)}), f32[32,40,256]{2,1,0:T(8,128)S(1)}, u32[]{:S(2)}, u32[]{:S(2)}) %all-to-all-start) | async-done | bytes 1310752 | tf_op jit(solution)/shard_map/all_to_all | solution.py:338
  34.2 4.9 %all-to-all-start.1 = ((bf16[32,32,16,256]{3,2,1,0:T(8,128)(2,1)}), bf16[32,32,16,256]{3,2,1,0:T(8,128)(2,1)}, u32[]{:S(2)}, u32[]{:S(2)}) async-start(bf16[32,32,16,256]{3,2,1,0:T(8,128)(2,1)} %bitcast.50), calls=%async_computation.1 | async-start | bytes 16777216 | tf_op jit(solution)/shard_map/all_to_all | solution.py:338
  39.2 7.6 %place_rows.3 = bf16[8,4,32,16,128]{4,3,2,1,0:T(8,128)(2,1)} custom-call(s32[8,4,128]{2,1,0:T(4,128)} %bitcast.71, bf16[32,128,1536]{2,1,0:T(8,128)(2,1)} %child_ref.3), custom_call_target="tpu_custom_call" | custom-call | flops 536870912 | bytes 8388608 | tf_op jit(solution)/shard_map/place_rows/pallas_call | solution.py:42
  46.8 99.2 %all-to-all-done.1.got_ref = bf16[32,32,16,256]{3,2,1,0:T(8,128)(2,1)} async-done(((bf16[32,32,16,256]{3,2,1,0:T(8,128)(2,1)}), bf16[32,32,16,256]{3,2,1,0:T(8,128)(2,1)}, u32[]{:S(2)}, u32[]{:S(2)}) %all-to-all-start.1) | async-done | bytes 8388640 | tf_op jit(solution)/shard_map/all_to_all | solution.py:338
  146.0 11.6 %collect_parents.2 = f32[256,16,256]{2,1,0:T(8,128)} custom-call(s32[1024]{0:T(1024)} %convert_element_type.22.at_ref, bf16[32,32,16,256]{3,2,1,0:T(8,128)(2,1)} %all-to-all-done.1.got_ref), custom_call_target="tpu_custom_call" | custom-call | flops 4194304 | bytes 12582912 | tf_op jit(solution)/shard_map/collect_parents/pallas_call | solution.py:83
  157.6 23.7 %all-to-all-start.2 = ((f32[32,8,16,256]{3,2,1,0:T(8,128)}), f32[32,8,16,256]{3,2,1,0:T(8,128)}, u32[]{:S(2)}, u32[]{:S(2)}) async-start(f32[32,8,16,256]{3,2,1,0:T(8,128)} %bitcast.51), calls=%async_computation.2 | async-start | bytes 8388608 | tf_op jit(solution)/shard_map/all_to_all | solution.py:338
  181.3 1.5 fusion.9
  183.1 3.2 collective-permute-start
  186.3 2.3 collective-permute-start.1
  188.6 1.3 collective-permute-start.2
  190.0 3.1 collective-permute-done
  193.1 7.0 %collective-permute-done.1 = f32[20,16,256]{2,1,0:T(8,128)S(1)} collective-permute-done((f32[20,16,256]{2,1,0:T(8,128)S(1)}, f32[20,16,256]{2,1,0:T(8,128)S(1)}, u32[]{:S(2)}, u32[]{:S(2)}) %collective-permute-start.1) | collective-permute-done | bytes 327712 | tf_op jit(solution)/shard_map/ppermute | solution.py:378
  200.2 2.9 collective-permute-start.4
  203.5 2.4 collective-permute-start.5
  208.9 1.6 collective-permute-start.7
  210.6 22.0 %collective-permute-done.7 = f32[3,16,256]{2,1,0:T(8,128)S(1)} collective-permute-done((f32[3,16,256]{2,1,0:T(8,128)S(1)}, f32[3,16,256]{2,1,0:T(8,128)S(1)}, u32[]{:S(2)}, u32[]{:S(2)}) %collective-permute-start.7) | collective-permute-done | bytes 49184 | tf_op jit(solution)/shard_map/ppermute | solution.py:389
  232.6 3.3 collective-permute-done.8
  236.3 3.7 collective-permute-start.10
  241.1 4.1 collective-permute-done.11.refs_3_
  245.1 1.4 collective-permute-start.15
  247.0 1.6 collective-permute-start.14
  248.6 4.0 collective-permute-done.9.refs_1_
  252.5 1.5 collective-permute-start.13
  254.1 1.9 select_select_fusion
  256.2 5.2 %all-to-all-start.3 = ((bf16[32,32,16,128]{3,2,1,0:T(8,128)(2,1)}), bf16[32,32,16,128]{3,2,1,0:T(8,128)(2,1)}, u32[]{:S(2)}, u32[]{:S(2)}) async-start(bf16[32,32,16,128]{3,2,1,0:T(8,128)(2,1)} %bitcast.53), calls=%async_computation.3 | async-start | bytes 8388608 | tf_op jit(solution)/shard_map/all_to_all | solution.py:338
  261.4 7.6 %assemble_panel.1.panel_ref = f32[8,128,1024]{2,1,0:T(8,128)} custom-call(f32[8,1,128,1536]{3,2,1,0:T(8,128)} %front_ref.3, f32[8,4,8,16,256]{4,3,2,1,0:T(8,128)} %bitcast.11.got_ref), custom_call_target="tpu_custom_call" | custom-call | flops 1048576 | bytes 12582912 | tf_op jit(solution)/shard_map/assemble_panel/pallas_call | solution.py:236
  269.0 2.3 fusion.29
  271.3 3.3 collective-permute-start.16
  274.6 2.2 collective-permute-start.18
  276.8 1.4 collective-permute-start.17
  278.1 73.4 %factor_and_invert.1 = (f32[1024,1024]{1,0:T(8,128)S(1)}, f32[1024,1024]{1,0:T(8,128)S(1)}) custom-call(s32[32]{0:T(128)S(1)} %multiply_add_fusion.index_ref, f32[4,8,16,256]{3,2,1,0:T(8,128)S(1)} %pad_maximum_fusion.5.refs_0_, f32[4,8,16,256]{3,2,1,0:T(8,128)S(1)} %collective-permute-done.9.refs_1_, f32[4,8,16,256]{3,2,1,0:T(8,128)S(1)} %collective-permute-done.10.refs_2_, ...), custom_call_target="tpu_custom_call" | custom-call | flops 70000001024 | bytes 12582912 | tf_op jit(solution)/shard_map/factor_and_invert/pallas_call | solution.py:210
  351.7 2.4 fusion.8
  354.2 4.3 fusion.2
  360.2 9.4 %collect_parents.3 = f32[256,16,128]{2,1,0:T(8,128)} custom-call(s32[1024]{0:T(1024)} %convert_element_type.22.at_ref, bf16[32,32,16,128]{3,2,1,0:T(8,128)(2,1)} %all-to-all-done.3.got_ref, bf16[256,1024]{1,0:T(8,128)(2,1)} %pad_maximum_fusion.6.refs_0_, bf16[3,16,1024]{2,1,0:T(8,128)(2,1)} %bitcast.62), custom_call_target="tpu_custom_call" | custom-call | flops 2097152 | bytes 6291456 | tf_op jit(solution)/shard_map/collect_parents/pallas_call | solution.py:83
  369.7 7.7 %all-to-all-start.4 = ((f32[32,8,16,128]{3,2,1,0:T(8,128)}), f32[32,8,16,128]{3,2,1,0:T(8,128)S(1)}, u32[]{:S(2)}, u32[]{:S(2)}) async-start(f32[32,8,16,128]{3,2,1,0:T(8,128)} %bitcast.55), calls=%async_computation.4 | async-start | bytes 4194304 | tf_op jit(solution)/shard_map/all_to_all | solution.py:338
  377.4 1.5 collective-permute-start.22
  378.9 2.6 collective-permute-start.21
  382.6 21.2 %collective-permute-done.21 = bf16[3,16,1024]{2,1,0:T(8,128)(2,1)S(1)} collective-permute-done((bf16[3,16,1024]{2,1,0:T(8,128)(2,1)S(1)}, bf16[3,16,1024]{2,1,0:T(8,128)(2,1)S(1)}, u32[]{:S(2)}, u32[]{:S(2)}) %collective-permute-start.21) | collective-permute-done | bytes 98336 | tf_op jit(solution)/shard_map/ppermute | solution.py:356
  406.6 2.5 collective-permute-start.28
  414.1 3.9 collective-permute-done.25.refs_3_
  418.0 2.3 collective-permute-start.32
  420.4 1.4 collective-permute-done.26.refs_6_
  421.8 1.8 collective-permute-start.30
  423.7 17.8 %fusion.lower_ref = f32[8,128,1024]{2,1,0:T(8,128)} fusion(f32[8,128,1024]{2,1,0:T(8,128)} %assemble_panel.1.panel_ref, f32[1024,1024]{1,0:T(8,128)} %copy-done), kind=kOutput, calls=%fused_computation | convolution fusion | flops 12884901888 | bytes 12582912 | tf_op jit(solution)/shard_map/dot_general | solution.py:16
  443.2 1.3 copy-done.2
  444.5 11.0 %trailing_update.1 = f32[8,1,128,1536]{3,2,1,0:T(8,128)} custom-call(s32[6]{0:T(128)} %pad_add_fusion.order_ref, s32[32]{0:T(128)} %copy-done.1, f32[8,128,1024]{2,1,0:T(8,128)} %assemble_panel.1.panel_ref, f32[8,128,1024]{2,1,0:T(8,128)} %fusion.lower_ref, f32[128,1024]{1,0:T(8,128)} %copy-done.4, f32[8,1,128,1536]{3,2,1,0:T(8,128)} %front_ref.3, ...), custom_call_target="tpu_custom_call" | custom-call | flops 3221225472 | bytes 29360128 | tf_op jit(solution)/shard_map/trailing_update/pallas_call | solution.py:306
  (121 shorter events, 23.9 us)
Async XLA Ops:
  2.5 11.5 %copy-start.15 = (s32[32,128]{1,0:T(8,128)S(1)}, s32[32,128]{1,0:T(8,128)}, u32[]{:S(2)}) copy-start(s32[32,128]{1,0:T(8,128)} %param.10) | copy-start | bytes 49156
  3.9 29.2 %all-to-all-start = ((f32[32,40,256]{2,1,0:T(8,128)}), f32[32,40,256]{2,1,0:T(8,128)S(1)}, u32[]{:S(2)}, u32[]{:S(2)}) async-start(f32[32,40,256]{2,1,0:T(8,128)} %pad_maximum_fusion), calls=%async_computation | async-start | bytes 2621440 | tf_op jit(solution)/shard_map/all_to_all | solution.py:338
  34.2 111.7 %all-to-all-start.1 = ((bf16[32,32,16,256]{3,2,1,0:T(8,128)(2,1)}), bf16[32,32,16,256]{3,2,1,0:T(8,128)(2,1)}, u32[]{:S(2)}, u32[]{:S(2)}) async-start(bf16[32,32,16,256]{3,2,1,0:T(8,128)(2,1)} %bitcast.50), calls=%async_computation.1 | async-start | bytes 16777216 | tf_op jit(solution)/shard_map/all_to_all | solution.py:338
  157.6 23.7 %slice-start = ((f32[32,40,256]{2,1,0:T(8,128)}), f32[32,32,256]{2,1,0:T(8,128)S(1)}, s32[]{:S(2)}) async-start(f32[32,40,256]{2,1,0:T(8,128)} %copy-done.5), calls=%async_computation.5 | async-start | bytes 2097152 | tf_op jit(solution)/shard_map/slice | solution.py:414
  157.6 98.6 %all-to-all-start.2 = ((f32[32,8,16,256]{3,2,1,0:T(8,128)}), f32[32,8,16,256]{3,2,1,0:T(8,128)}, u32[]{:S(2)}, u32[]{:S(2)}) async-start(f32[32,8,16,256]{3,2,1,0:T(8,128)} %bitcast.51), calls=%async_computation.2 | async-start | bytes 8388608 | tf_op jit(solution)/shard_map/all_to_all | solution.py:338
  182.9 71.2 %copy-start.16 = (pred[48]{0:T(512)(128)(4,1)S(1)}, pred[48]{0:T(512)(128)(4,1)}, u32[]{:S(2)}) copy-start(pred[48]{0:T(512)(128)(4,1)} %constant.269) | copy-start | bytes 148
  182.9 71.2 %copy-start.17 = (pred[48]{0:T(512)(128)(4,1)S(1)}, pred[48]{0:T(512)(128)(4,1)}, u32[]{:S(2)}) copy-start(pred[48]{0:T(512)(128)(4,1)} %constant.268) | copy-start | bytes 148
  183.1 10.0 %collective-permute-start = (f32[20,16,256]{2,1,0:T(8,128)S(1)}, f32[20,16,256]{2,1,0:T(8,128)S(1)}, u32[]{:S(2)}, u32[]{:S(2)}) collective-permute-start(f32[20,16,256]{2,1,0:T(8,128)S(1)} %get-tuple-element.62), channel_id=1, source_target_pairs={{0,1},{4,5},{8,9},{12,13},{16,17},{20,21},{24,25},{28,29},{32,33},... | collective-permute-start | bytes 983048 | tf_op jit(solution)/shard_map/ppermute | solution.py:378
  186.3 13.8 %collective-permute-start.1 = (f32[20,16,256]{2,1,0:T(8,128)S(1)}, f32[20,16,256]{2,1,0:T(8,128)S(1)}, u32[]{:S(2)}, u32[]{:S(2)}) collective-permute-start(f32[20,16,256]{2,1,0:T(8,128)S(1)} %get-tuple-element.63), channel_id=1, source_target_pairs={{0,2},{4,6},{8,10},{12,14},{16,18},{20,22},{24,26},{28,30},{32,34}... | collective-permute-start | bytes 983048 | tf_op jit(solution)/shard_map/ppermute | solution.py:378
  188.6 11.5 %collective-permute-start.2 = (f32[20,16,256]{2,1,0:T(8,128)S(1)}, f32[20,16,256]{2,1,0:T(8,128)S(1)}, u32[]{:S(2)}, u32[]{:S(2)}) collective-permute-start(f32[20,16,256]{2,1,0:T(8,128)S(1)} %get-tuple-element.64), channel_id=1, source_target_pairs={{0,3},{4,7},{8,11},{12,15},{16,19},{20,23},{24,27},{28,31},{32,35}... | collective-permute-start | bytes 983048 | tf_op jit(solution)/shard_map/ppermute | solution.py:378
  200.2 35.7 %collective-permute-start.4 = (f32[8,16,256]{2,1,0:T(8,128)S(1)}, f32[8,16,256]{2,1,0:T(8,128)S(1)}, u32[]{:S(2)}, u32[]{:S(2)}) collective-permute-start(f32[8,16,256]{2,1,0:T(8,128)S(1)} %get-tuple-element.58), channel_id=1, source_target_pairs={{0,16},{4,68},{8,24},{12,76},{16,0},{20,84},{24,8},{28,92},{32,48}... | collective-permute-start | bytes 393224 | tf_op jit(solution)/shard_map/ppermute | solution.py:356
  203.2 32.8 %collective-permute-start.3 = (f32[8,16,256]{2,1,0:T(8,128)S(1)}, f32[8,16,256]{2,1,0:T(8,128)S(1)}, u32[]{:S(2)}, u32[]{:S(2)}) collective-permute-start(f32[8,16,256]{2,1,0:T(8,128)S(1)} %get-tuple-element.58), channel_id=1, source_target_pairs={{0,8},{4,36},{8,16},{12,44},{16,24},{20,52},{24,0},{28,60},{32,40}... | collective-permute-start | bytes 393224 | tf_op jit(solution)/shard_map/ppermute | solution.py:356
  203.5 32.5 %collective-permute-start.5 = (f32[8,16,256]{2,1,0:T(8,128)S(1)}, f32[8,16,256]{2,1,0:T(8,128)S(1)}, u32[]{:S(2)}, u32[]{:S(2)}) collective-permute-start(f32[8,16,256]{2,1,0:T(8,128)S(1)} %get-tuple-element.58), channel_id=1, source_target_pairs={{0,24},{4,100},{8,0},{12,108},{16,8},{20,116},{24,16},{28,124},{32... | collective-permute-start | bytes 393224 | tf_op jit(solution)/shard_map/ppermute | solution.py:356
  205.9 30.1 %collective-permute-start.8 = (f32[3,16,256]{2,1,0:T(8,128)S(1)}, f32[3,16,256]{2,1,0:T(8,128)S(1)}, u32[]{:S(2)}, u32[]{:S(2)}) collective-permute-start(f32[3,16,256]{2,1,0:T(8,128)S(1)} %get-tuple-element.59), channel_id=1, source_target_pairs={{0,12},{4,8},{8,4},{12,0},{16,28},{20,24},{24,20},{28,16},{32,44},... | collective-permute-start | bytes 147464 | tf_op jit(solution)/shard_map/ppermute | solution.py:389
  206.9 2.0 collective-permute-start.6
  208.9 23.6 %collective-permute-start.7 = (f32[3,16,256]{2,1,0:T(8,128)S(1)}, f32[3,16,256]{2,1,0:T(8,128)S(1)}, u32[]{:S(2)}, u32[]{:S(2)}) collective-permute-start(f32[3,16,256]{2,1,0:T(8,128)S(1)} %get-tuple-element.60), channel_id=1, source_target_pairs={{0,8},{4,12},{8,0},{12,4},{16,24},{20,28},{24,16},{28,20},{32,40},... | collective-permute-start | bytes 147464 | tf_op jit(solution)/shard_map/ppermute | solution.py:389
  236.0 9.1 %collective-permute-start.11 = (f32[4,8,16,256]{3,2,1,0:T(8,128)S(1)}, f32[4,8,16,256]{3,2,1,0:T(8,128)S(1)}, u32[]{:S(2)}, u32[]{:S(2)}) collective-permute-start(f32[4,8,16,256]{3,2,1,0:T(8,128)S(1)} %pad_maximum_fusion.5.refs_0_), channel_id=1, source_target_pairs={{0,96},{4,28},{8,104},{12,4},{16,112},{20,12},{24,120},{28,20},{32... | collective-permute-start | bytes 1572872 | tf_op jit(solution)/shard_map/ppermute | solution.py:356
  236.3 10.6 %collective-permute-start.10 = (f32[4,8,16,256]{3,2,1,0:T(8,128)S(1)}, f32[4,8,16,256]{3,2,1,0:T(8,128)S(1)}, u32[]{:S(2)}, u32[]{:S(2)}) collective-permute-start(f32[4,8,16,256]{3,2,1,0:T(8,128)S(1)} %pad_maximum_fusion.5.refs_0_), channel_id=1, source_target_pairs={{0,64},{4,20},{8,72},{12,28},{16,80},{20,4},{24,88},{28,12},{32,96... | collective-permute-start | bytes 1572872 | tf_op jit(solution)/shard_map/ppermute | solution.py:356
  240.1 12.5 %collective-permute-start.9 = (f32[4,8,16,256]{3,2,1,0:T(8,128)S(1)}, f32[4,8,16,256]{3,2,1,0:T(8,128)S(1)}, u32[]{:S(2)}, u32[]{:S(2)}) collective-permute-start(f32[4,8,16,256]{3,2,1,0:T(8,128)S(1)} %pad_maximum_fusion.5.refs_0_), channel_id=1, source_target_pairs={{0,32},{4,12},{8,40},{12,20},{16,48},{20,28},{24,56},{28,4},{32,64... | collective-permute-start | bytes 1572872 | tf_op jit(solution)/shard_map/ppermute | solution.py:356
  240.7 33.8 %collective-permute-start.12 = (f32[4,8,16,256]{3,2,1,0:T(8,128)S(1)}, f32[4,8,16,256]{3,2,1,0:T(8,128)S(1)}, u32[]{:S(2)}, u32[]{:S(2)}) collective-permute-start(f32[4,8,16,256]{3,2,1,0:T(8,128)S(1)} %pad_maximum_fusion.5.refs_0_), channel_id=1, source_target_pairs={{0,4},{4,0},{8,12},{12,8},{16,20},{20,16},{24,28},{28,24},{32,36},... | collective-permute-start | bytes 1572872 | tf_op jit(solution)/shard_map/ppermute | solution.py:362
  245.1 31.6 %collective-permute-start.15 = (f32[4,8,16,256]{3,2,1,0:T(8,128)S(1)}, f32[4,8,16,256]{3,2,1,0:T(8,128)S(1)}, u32[]{:S(2)}, u32[]{:S(2)}) collective-permute-start(f32[4,8,16,256]{3,2,1,0:T(8,128)S(1)} %collective-permute-done.11.refs_3_), channel_id=1, source_target_pairs={{0,4},{4,0},{8,12},{12,8},{16,20},{20,16},{24,28},{28,24},{32,36},... | collective-permute-start | bytes 1572872 | tf_op jit(solution)/shard_map/ppermute | solution.py:362
  247.0 31.1 %collective-permute-start.14 = (f32[4,8,16,256]{3,2,1,0:T(8,128)S(1)}, f32[4,8,16,256]{3,2,1,0:T(8,128)}, u32[]{:S(2)}, u32[]{:S(2)}) collective-permute-start(f32[4,8,16,256]{3,2,1,0:T(8,128)S(1)} %collective-permute-done.10.refs_2_), channel_id=1, source_target_pairs={{0,4},{4,0},{8,12},{12,8},{16,20},{20,16},{24,28},{28,24},{32,36},... | collective-permute-start | bytes 1572872 | tf_op jit(solution)/shard_map/ppermute | solution.py:362
  252.5 25.6 %collective-permute-start.13 = (f32[4,8,16,256]{3,2,1,0:T(8,128)S(1)}, f32[4,8,16,256]{3,2,1,0:T(8,128)}, u32[]{:S(2)}, u32[]{:S(2)}) collective-permute-start(f32[4,8,16,256]{3,2,1,0:T(8,128)S(1)} %collective-permute-done.9.refs_1_), channel_id=1, source_target_pairs={{0,4},{4,0},{8,12},{12,8},{16,20},{20,16},{24,28},{28,24},{32,36},... | collective-permute-start | bytes 1572872 | tf_op jit(solution)/shard_map/ppermute | solution.py:362
  256.2 22.0 %copy-start.1 = (s32[32]{0:T(128)}, s32[32]{0:T(128)S(1)}, u32[]{:S(2)}) copy-start(s32[32]{0:T(128)S(1)} %multiply_add_fusion.index_ref) | copy-start | bytes 388
  256.2 104.0 %all-to-all-start.3 = ((bf16[32,32,16,128]{3,2,1,0:T(8,128)(2,1)}), bf16[32,32,16,128]{3,2,1,0:T(8,128)(2,1)}, u32[]{:S(2)}, u32[]{:S(2)}) async-start(bf16[32,32,16,128]{3,2,1,0:T(8,128)(2,1)} %bitcast.53), calls=%async_computation.3 | async-start | bytes 8388608 | tf_op jit(solution)/shard_map/all_to_all | solution.py:338
  271.3 80.4 %collective-permute-start.16 = (f32[2,128,1024]{2,1,0:T(8,128)S(1)}, f32[2,128,1024]{2,1,0:T(8,128)S(1)}, u32[]{:S(2)}, u32[]{:S(2)}) collective-permute-start(f32[2,128,1024]{2,1,0:T(8,128)S(1)} %get-tuple-element.48), channel_id=1, source_target_pairs={{0,1},{4,5},{8,9},{12,13},{16,17},{20,21},{24,25},{28,29},{32,33},... | collective-permute-start | bytes 3145736 | tf_op jit(solution)/shard_map/ppermute | solution.py:378
  274.6 77.1 %collective-permute-start.18 = (f32[2,128,1024]{2,1,0:T(8,128)S(1)}, f32[2,128,1024]{2,1,0:T(8,128)S(1)}, u32[]{:S(2)}, u32[]{:S(2)}) collective-permute-start(f32[2,128,1024]{2,1,0:T(8,128)S(1)} %get-tuple-element.49), channel_id=1, source_target_pairs={{0,3},{4,7},{8,11},{12,15},{16,19},{20,23},{24,27},{28,31},{32,35}... | collective-permute-start | bytes 3145736 | tf_op jit(solution)/shard_map/ppermute | solution.py:378
  276.8 75.0 %collective-permute-start.17 = (f32[2,128,1024]{2,1,0:T(8,128)S(1)}, f32[2,128,1024]{2,1,0:T(8,128)S(1)}, u32[]{:S(2)}, u32[]{:S(2)}) collective-permute-start(f32[2,128,1024]{2,1,0:T(8,128)S(1)} %get-tuple-element.50), channel_id=1, source_target_pairs={{0,2},{4,6},{8,10},{12,14},{16,18},{20,22},{24,26},{28,30},{32,34}... | collective-permute-start | bytes 3145736 | tf_op jit(solution)/shard_map/ppermute | solution.py:378
  360.2 17.1 %copy-start.3 = (bf16[256,1024]{1,0:T(8,128)(2,1)S(1)}, bf16[256,1024]{1,0:T(8,128)(2,1)}, u32[]{:S(2)}) copy-start(bf16[256,1024]{1,0:T(8,128)(2,1)} %pad_maximum_fusion.6.refs_0_) | copy-start | bytes 1572868
  360.2 18.6 %copy-start.9 = (bf16[48,1024]{1,0:T(8,128)(2,1)S(1)}, bf16[48,1024]{1,0:T(8,128)(2,1)}, u32[]{:S(2)}) copy-start(bf16[48,1024]{1,0:T(8,128)(2,1)} %slice.127) | copy-start | bytes 294916
  369.7 73.5 %all-to-all-start.4 = ((f32[32,8,16,128]{3,2,1,0:T(8,128)}), f32[32,8,16,128]{3,2,1,0:T(8,128)S(1)}, u32[]{:S(2)}, u32[]{:S(2)}) async-start(f32[32,8,16,128]{3,2,1,0:T(8,128)} %bitcast.55), calls=%async_computation.4 | async-start | bytes 4194304 | tf_op jit(solution)/shard_map/all_to_all | solution.py:338
  377.3 29.2 %collective-permute-start.23 = (bf16[256,1024]{1,0:T(8,128)(2,1)S(1)}, bf16[256,1024]{1,0:T(8,128)(2,1)S(1)}, u32[]{:S(2)}, u32[]{:S(2)}) collective-permute-start(bf16[256,1024]{1,0:T(8,128)(2,1)S(1)} %copy-done.3), channel_id=1, source_target_pairs={{0,3},{1,0},{2,1},{3,2},{4,7},{5,4},{6,5},{7,6},{8,11},{9,8},{10,9... | collective-permute-start | bytes 1572872 | tf_op jit(solution)/shard_map/ppermute | solution.py:458
  377.4 29.1 %collective-permute-start.22 = (bf16[256,1024]{1,0:T(8,128)(2,1)S(1)}, bf16[256,1024]{1,0:T(8,128)(2,1)S(1)}, u32[]{:S(2)}, u32[]{:S(2)}) collective-permute-start(bf16[256,1024]{1,0:T(8,128)(2,1)S(1)} %copy-done.3), channel_id=1, source_target_pairs={{0,1},{1,2},{2,3},{3,0},{4,5},{5,6},{6,7},{7,4},{8,9},{9,10},{10,1... | collective-permute-start | bytes 1572872 | tf_op jit(solution)/shard_map/ppermute | solution.py:458
  378.9 25.0 %collective-permute-start.21 = (bf16[3,16,1024]{2,1,0:T(8,128)(2,1)S(1)}, bf16[3,16,1024]{2,1,0:T(8,128)(2,1)S(1)}, u32[]{:S(2)}, u32[]{:S(2)}) collective-permute-start(bf16[3,16,1024]{2,1,0:T(8,128)(2,1)S(1)} %bitcast.64), channel_id=1, source_target_pairs={{0,24},{4,100},{8,0},{12,108},{16,8},{20,116},{24,16},{28,124},{32... | collective-permute-start | bytes 294920 | tf_op jit(solution)/shard_map/ppermute | solution.py:356
  381.5 23.5 %collective-permute-start.20 = (bf16[3,16,1024]{2,1,0:T(8,128)(2,1)S(1)}, bf16[3,16,1024]{2,1,0:T(8,128)(2,1)S(1)}, u32[]{:S(2)}, u32[]{:S(2)}) collective-permute-start(bf16[3,16,1024]{2,1,0:T(8,128)(2,1)S(1)} %bitcast.65), channel_id=1, source_target_pairs={{0,16},{4,68},{8,24},{12,76},{16,0},{20,84},{24,8},{28,92},{32,48}... | collective-permute-start | bytes 294920 | tf_op jit(solution)/shard_map/ppermute | solution.py:356
  382.0 23.5 %collective-permute-start.19 = (bf16[3,16,1024]{2,1,0:T(8,128)(2,1)S(1)}, bf16[3,16,1024]{2,1,0:T(8,128)(2,1)S(1)}, u32[]{:S(2)}, u32[]{:S(2)}) collective-permute-start(bf16[3,16,1024]{2,1,0:T(8,128)(2,1)S(1)} %bitcast.66), channel_id=1, source_target_pairs={{0,8},{4,36},{8,16},{12,44},{16,24},{20,52},{24,0},{28,60},{32,40}... | collective-permute-start | bytes 294920 | tf_op jit(solution)/shard_map/ppermute | solution.py:356
  406.5 34.9 %copy-start.6 = (bf16[4,3,16,1024]{3,2,1,0:T(8,128)(2,1)}, bf16[4,3,16,1024]{3,2,1,0:T(8,128)(2,1)S(1)}, u32[]{:S(2)}) copy-start(bf16[4,3,16,1024]{3,2,1,0:T(8,128)(2,1)S(1)} %pad_maximum_fusion.7.refs_5_) | copy-start | bytes 1179652
  406.5 34.9 %copy-start.7 = (bf16[256,1024]{1,0:T(8,128)(2,1)}, bf16[256,1024]{1,0:T(8,128)(2,1)S(1)}, u32[]{:S(2)}) copy-start(bf16[256,1024]{1,0:T(8,128)(2,1)S(1)} %collective-permute-done.23.refs_4_) | copy-start | bytes 1572868
  406.6 11.4 %collective-permute-start.28 = (bf16[4,3,16,1024]{3,2,1,0:T(8,128)(2,1)S(1)}, bf16[4,3,16,1024]{3,2,1,0:T(8,128)(2,1)S(1)}, u32[]{:S(2)}, u32[]{:S(2)}) collective-permute-start(bf16[4,3,16,1024]{3,2,1,0:T(8,128)(2,1)S(1)} %pad_maximum_fusion.7.refs_5_), channel_id=1, source_target_pairs={{0,96},{4,28},{8,104},{12,4},{16,112},{20,12},{24,120},{28,20},{32... | collective-permute-start | bytes 1179656 | tf_op jit(solution)/shard_map/ppermute | solution.py:356
  409.1 11.2 %collective-permute-start.27 = (bf16[4,3,16,1024]{3,2,1,0:T(8,128)(2,1)S(1)}, bf16[4,3,16,1024]{3,2,1,0:T(8,128)(2,1)}, u32[]{:S(2)}, u32[]{:S(2)}) collective-permute-start(bf16[4,3,16,1024]{3,2,1,0:T(8,128)(2,1)S(1)} %pad_maximum_fusion.7.refs_5_), channel_id=1, source_target_pairs={{0,64},{4,20},{8,72},{12,28},{16,80},{20,4},{24,88},{28,12},{32,96... | collective-permute-start | bytes 1179656 | tf_op jit(solution)/shard_map/ppermute | solution.py:356
  410.1 11.7 %collective-permute-start.26 = (bf16[4,3,16,1024]{3,2,1,0:T(8,128)(2,1)S(1)}, bf16[4,3,16,1024]{3,2,1,0:T(8,128)(2,1)}, u32[]{:S(2)}, u32[]{:S(2)}) collective-permute-start(bf16[4,3,16,1024]{3,2,1,0:T(8,128)(2,1)S(1)} %pad_maximum_fusion.7.refs_5_), channel_id=1, source_target_pairs={{0,32},{4,12},{8,40},{12,20},{16,48},{20,28},{24,56},{28,4},{32,64... | collective-permute-start | bytes 1179656 | tf_op jit(solution)/shard_map/ppermute | solution.py:356
  411.2 6.8 %collective-permute-start.25 = (bf16[128,1024]{1,0:T(8,128)(2,1)}, bf16[128,1024]{1,0:T(8,128)(2,1)}, u32[]{:S(2)}, u32[]{:S(2)}) collective-permute-start(bf16[128,1024]{1,0:T(8,128)(2,1)} %slice.104), channel_id=1, source_target_pairs={{0,3},{1,0},{2,1},{3,2},{4,7},{5,4},{6,5},{7,6},{8,11},{9,8},{10,9... | collective-permute-start | bytes 786440 | tf_op jit(solution)/shard_map/ppermute | solution.py:458
  411.8 29.6 %collective-permute-start.29 = (bf16[4,3,16,1024]{3,2,1,0:T(8,128)(2,1)S(1)}, bf16[4,3,16,1024]{3,2,1,0:T(8,128)(2,1)S(1)}, u32[]{:S(2)}, u32[]{:S(2)}) collective-permute-start(bf16[4,3,16,1024]{3,2,1,0:T(8,128)(2,1)S(1)} %pad_maximum_fusion.7.refs_5_), channel_id=1, source_target_pairs={{0,4},{4,0},{8,12},{12,8},{16,20},{20,16},{24,28},{28,24},{32,36},... | collective-permute-start | bytes 1179656 | tf_op jit(solution)/shard_map/ppermute | solution.py:362
  418.0 23.5 %collective-permute-start.24 = (bf16[128,1024]{1,0:T(8,128)(2,1)S(1)}, bf16[128,1024]{1,0:T(8,128)(2,1)S(1)}, u32[]{:S(2)}, u32[]{:S(2)}) collective-permute-start(bf16[128,1024]{1,0:T(8,128)(2,1)S(1)} %slice.103), channel_id=1, source_target_pairs={{0,1},{1,2},{2,3},{3,0},{4,5},{5,6},{6,7},{7,4},{8,9},{9,10},{10,1... | collective-permute-start | bytes 786440 | tf_op jit(solution)/shard_map/ppermute | solution.py:458
  418.0 23.4 %copy-start.10 = (bf16[4,3,16,1024]{3,2,1,0:T(8,128)(2,1)}, bf16[4,3,16,1024]{3,2,1,0:T(8,128)(2,1)S(1)}, u32[]{:S(2)}) copy-start(bf16[4,3,16,1024]{3,2,1,0:T(8,128)(2,1)S(1)} %collective-permute-done.28.refs_8_) | copy-start | bytes 1179652
  418.0 23.5 %collective-permute-start.32 = (bf16[4,3,16,1024]{3,2,1,0:T(8,128)(2,1)S(1)}, bf16[4,3,16,1024]{3,2,1,0:T(8,128)(2,1)S(1)}, u32[]{:S(2)}, u32[]{:S(2)}) collective-permute-start(bf16[4,3,16,1024]{3,2,1,0:T(8,128)(2,1)S(1)} %collective-permute-done.28.refs_8_), channel_id=1, source_target_pairs={{0,4},{4,0},{8,12},{12,8},{16,20},{20,16},{24,28},{28,24},{32,36},... | collective-permute-start | bytes 1179656 | tf_op jit(solution)/shard_map/ppermute | solution.py:362
  420.3 21.2 %collective-permute-start.31 = (bf16[4,3,16,1024]{3,2,1,0:T(8,128)(2,1)}, bf16[4,3,16,1024]{3,2,1,0:T(8,128)(2,1)S(1)}, u32[]{:S(2)}, u32[]{:S(2)}) collective-permute-start(bf16[4,3,16,1024]{3,2,1,0:T(8,128)(2,1)} %collective-permute-done.27.refs_7_), channel_id=1, source_target_pairs={{0,4},{4,0},{8,12},{12,8},{16,20},{20,16},{24,28},{28,24},{32,36},... | collective-permute-start | bytes 1179656 | tf_op jit(solution)/shard_map/ppermute | solution.py:362
  421.8 21.3 %collective-permute-start.30 = (bf16[4,3,16,1024]{3,2,1,0:T(8,128)(2,1)}, bf16[4,3,16,1024]{3,2,1,0:T(8,128)(2,1)}, u32[]{:S(2)}, u32[]{:S(2)}) collective-permute-start(bf16[4,3,16,1024]{3,2,1,0:T(8,128)(2,1)} %collective-permute-done.26.refs_6_), channel_id=1, source_target_pairs={{0,4},{4,0},{8,12},{12,8},{16,20},{20,16},{24,28},{28,24},{32,36},... | collective-permute-start | bytes 1179656 | tf_op jit(solution)/shard_map/ppermute | solution.py:362
  (9 other events, 21.9 us)

commit v4 on v3

--- a/solution.py
+++ b/solution.py
@@ -357,8 +357,7 @@
     return parts
 
 
-def gather_rows(ring):
-    mine = ring_stage(ring, 1)
+def with_cores(mine):
     return mine + [lax.ppermute(part, "row", [(r, r ^ 1) for r in range(32)]) for part in mine]
 
 
@@ -423,7 +422,7 @@
     pieces = [jnp.concatenate([tiles[:8], tiles[12 * c : 12 * c + 12]]) for c in range(4)]
     piece = from_first(pieces, col_index)
     ring, part = together(jnp.stack(ring_stage(piece[:8], 0)), own_rows(piece[8:], row_index))
-    diagonal = gather_rows(ring)
+    diagonal = with_cores(ring_stage(ring, 1))
 
     got, sent_rest = together(exchange(sums), sent_rest)
     panel = assemble(front, got.reshape(8, 4, 8, 16, 256))
@@ -457,13 +456,14 @@
     def turn(x, by):
         return lax.ppermute(x, "col", [(c, (c + by) % 4) for c in range(4)])
 
-    ring, before, behind = together(jnp.stack(ring_stage(part, 0)), turn(own, 1), turn(own, 3))
-    spread = [own, before, turn(before[:128], 1), turn(behind[128:], 3), behind]
-    slab = gather_rows(ring)
-
+    before, behind = turn(own, 1), turn(own, 3)
     sums_rest = collect(at, got_rest, own, part)
+    ring, sums_rest = together(jnp.stack(ring_stage(part, 0)), sums_rest)
     got_rest = exchange(sums_rest.reshape(32, 8, 16, 128)).reshape(8, 4, 8, 16, 128)
     lower = times_transposed(panel.reshape(8 * 128, PANEL), inverse).reshape(8, 128, PANEL)
+    *mine, lower, before, behind = together(*ring_stage(ring, 1), lower, before, behind)
+    spread = [own, before, turn(before[:128], 1), turn(behind[128:], 3), behind]
+    slab = with_cores(mine)
 
     order = (col_index + 4 - jnp.arange(4, dtype=jnp.int32)) % 4
     order = jnp.concatenate([order, jnp.stack([col_index, row_index])])

time: 459 us -> 452 us (0.985)
  starting transfers between devices: 97.4 us -> 92 us
    ppermute x4, waiting for transfers between devices: 3.9 us -> 13.1 us  [turn(): return lax.ppermute(x, 'col', [(c, (c + by) % 4) for c in range(4)])]
    ppermute x12, waiting for transfers between devices: 33 us -> 24.8 us  [ring_stage(): parts.append(lax.ppermute(x, 'row', moves))]
  transfers between devices with their start and end apart: 38 -> 38, of which waited for: 15 -> 17; matrix products, arithmetic and copies ran while one was open for 8% -> 8% of each run, Pallas kernels for 22% -> 22%
where the time goes in v4:
time: 452 us; the launch traced here: 447 us
  waiting for transfers between devices  182 us (40%)
  Pallas kernels  131 us (29%)
  starting transfers between devices  92 us (20%)
  matrix products  22.1 us (5%)
  other arithmetic  10.3 us (2%)
  local copies, waits for them, and re-layouts  8.52 us (2%)
    all_to_all x5, waiting for transfers between devices, exchange(): return lax.all_to_all(x, 'row', split_axis=0, concat_axis=0, tiled=True)  107 us
    pallas_call x1, Pallas kernels, factor(): pl.pallas_call(factor_kernel, in_specs=[pl.BlockSpec(memory_space=pltpu.S...  73.4 us
    all_to_all x5, starting transfers between devices, exchange(): return lax.all_to_all(x, 'row', split_axis=0, concat_axis=0, tiled=True)  49.8 us
    ppermute x3, waiting for transfers between devices, own_rows(): part = lax.ppermute(part, 'row', [(r, r ^ by) for r in range(32)])  26.2 us
    ppermute x12, waiting for transfers between devices, ring_stage(): parts.append(lax.ppermute(x, 'row', moves))  24.8 us
    dot_general x2, matrix products, times_transposed(): lax.dot_general(a, b, (((1,), (1,)), ((), ())), precision=precision, pref...  22.1 us
    pallas_call x2, Pallas kernels, collect(): pl.pallas_call(collect_kernel, grid_spec=pltpu.PrefetchScalarGridSpec(num...  21 us
    pallas_call x2, Pallas kernels, place(): pl.pallas_call(place_kernel, grid=(slots // 4,), in_specs=[pl.BlockSpec((...  17.9 us
  transfers between devices with their start and end apart: 38, of which 17 were waited for; matrix products, arithmetic and copies ran while one was open for 8% of the time, Pallas kernels for 22%

profile of v4, /device:TPU:1, one launch (start us, length us, event | category | flops | bytes accessed | tf_op | source)
XLA Modules:
  0.0 447.0 jit_solution(6435544545949533279)
XLA Ops:
  3.9 9.4 %all-to-all-start = ((f32[32,40,256]{2,1,0:T(8,128)}), f32[32,40,256]{2,1,0:T(8,128)S(1)}, u32[]{:S(2)}, u32[]{:S(2)}) async-start(f32[32,40,256]{2,1,0:T(8,128)} %pad_maximum_fusion), calls=%async_computation | async-start | bytes 2621440 | tf_op jit(solution)/shard_map/all_to_all | solution.py:338
  14.7 10.3 %place_rows.2 = bf16[8,4,32,16,256]{4,3,2,1,0:T(8,128)(2,1)} custom-call(s32[8,4,128]{2,1,0:T(4,128)} %bitcast.70, bf16[32,128,1536]{2,1,0:T(8,128)(2,1)} %child_ref.3), custom_call_target="tpu_custom_call" | custom-call | flops 1073741824 | bytes 16777216 | tf_op jit(solution)/shard_map/place_rows/pallas_call | solution.py:42
  25.0 8.1 %all-to-all-done = f32[32,40,256]{2,1,0:T(8,128)S(1)} async-done(((f32[32,40,256]{2,1,0:T(8,128)}), f32[32,40,256]{2,1,0:T(8,128)S(1)}, u32[]{:S(2)}, u32[]{:S(2)}) %all-to-all-start) | async-done | bytes 1310752 | tf_op jit(solution)/shard_map/all_to_all | solution.py:338
  34.2 4.9 %all-to-all-start.1 = ((bf16[32,32,16,256]{3,2,1,0:T(8,128)(2,1)}), bf16[32,32,16,256]{3,2,1,0:T(8,128)(2,1)}, u32[]{:S(2)}, u32[]{:S(2)}) async-start(bf16[32,32,16,256]{3,2,1,0:T(8,128)(2,1)} %bitcast.50), calls=%async_computation.1 | async-start | bytes 16777216 | tf_op jit(solution)/shard_map/all_to_all | solution.py:338
  39.2 7.6 %place_rows.3 = bf16[8,4,32,16,128]{4,3,2,1,0:T(8,128)(2,1)} custom-call(s32[8,4,128]{2,1,0:T(4,128)} %bitcast.71, bf16[32,128,1536]{2,1,0:T(8,128)(2,1)} %child_ref.3), custom_call_target="tpu_custom_call" | custom-call | flops 536870912 | bytes 8388608 | tf_op jit(solution)/shard_map/place_rows/pallas_call | solution.py:42
  46.8 99.2 %all-to-all-done.1.got_ref = bf16[32,32,16,256]{3,2,1,0:T(8,128)(2,1)} async-done(((bf16[32,32,16,256]{3,2,1,0:T(8,128)(2,1)}), bf16[32,32,16,256]{3,2,1,0:T(8,128)(2,1)}, u32[]{:S(2)}, u32[]{:S(2)}) %all-to-all-start.1) | async-done | bytes 8388640 | tf_op jit(solution)/shard_map/all_to_all | solution.py:338
  146.0 11.6 %collect_parents.2 = f32[256,16,256]{2,1,0:T(8,128)} custom-call(s32[1024]{0:T(1024)} %convert_element_type.22.at_ref, bf16[32,32,16,256]{3,2,1,0:T(8,128)(2,1)} %all-to-all-done.1.got_ref), custom_call_target="tpu_custom_call" | custom-call | flops 4194304 | bytes 12582912 | tf_op jit(solution)/shard_map/collect_parents/pallas_call | solution.py:83
  157.6 23.7 %all-to-all-start.2 = ((f32[32,8,16,256]{3,2,1,0:T(8,128)}), f32[32,8,16,256]{3,2,1,0:T(8,128)}, u32[]{:S(2)}, u32[]{:S(2)}) async-start(f32[32,8,16,256]{3,2,1,0:T(8,128)} %bitcast.51), calls=%async_computation.2 | async-start | bytes 8388608 | tf_op jit(solution)/shard_map/all_to_all | solution.py:338
  181.3 1.5 fusion.9
  183.1 3.2 collective-permute-start
  186.3 2.3 collective-permute-start.1
  188.6 1.3 collective-permute-start.2
  190.0 3.1 collective-permute-done
  193.1 7.0 %collective-permute-done.1 = f32[20,16,256]{2,1,0:T(8,128)S(1)} collective-permute-done((f32[20,16,256]{2,1,0:T(8,128)S(1)}, f32[20,16,256]{2,1,0:T(8,128)S(1)}, u32[]{:S(2)}, u32[]{:S(2)}) %collective-permute-start.1) | collective-permute-done | bytes 327712 | tf_op jit(solution)/shard_map/ppermute | solution.py:377
  200.3 2.9 collective-permute-start.4
  203.5 2.4 collective-permute-start.5
  209.0 1.6 collective-permute-start.7
  210.6 22.0 %collective-permute-done.7 = f32[3,16,256]{2,1,0:T(8,128)S(1)} collective-permute-done((f32[3,16,256]{2,1,0:T(8,128)S(1)}, f32[3,16,256]{2,1,0:T(8,128)S(1)}, u32[]{:S(2)}, u32[]{:S(2)}) %collective-permute-start.7) | collective-permute-done | bytes 49184 | tf_op jit(solution)/shard_map/ppermute | solution.py:388
  232.6 3.3 collective-permute-done.8
  236.4 3.7 collective-permute-start.10
  241.0 4.1 collective-permute-done.11.refs_3_
  245.2 1.4 collective-permute-start.15
  247.0 1.6 collective-permute-start.14
  248.6 4.0 collective-permute-done.9.refs_1_
  252.6 1.5 collective-permute-start.13
  254.1 1.8 select_select_fusion
  256.1 5.2 %all-to-all-start.3 = ((bf16[32,32,16,128]{3,2,1,0:T(8,128)(2,1)}), bf16[32,32,16,128]{3,2,1,0:T(8,128)(2,1)}, u32[]{:S(2)}, u32[]{:S(2)}) async-start(bf16[32,32,16,128]{3,2,1,0:T(8,128)(2,1)} %bitcast.53), calls=%async_computation.3 | async-start | bytes 8388608 | tf_op jit(solution)/shard_map/all_to_all | solution.py:338
  261.3 7.6 %assemble_panel.1.panel_ref = f32[8,128,1024]{2,1,0:T(8,128)} custom-call(f32[8,1,128,1536]{3,2,1,0:T(8,128)} %front_ref.3, f32[8,4,8,16,256]{4,3,2,1,0:T(8,128)} %bitcast.11.got_ref), custom_call_target="tpu_custom_call" | custom-call | flops 1048576 | bytes 12582912 | tf_op jit(solution)/shard_map/assemble_panel/pallas_call | solution.py:236
  268.9 2.3 fusion.29
  271.2 3.3 collective-permute-start.16
  274.5 2.2 collective-permute-start.18
  276.6 1.4 collective-permute-start.17
  278.0 73.4 %factor_and_invert.1 = (f32[1024,1024]{1,0:T(8,128)S(1)}, f32[1024,1024]{1,0:T(8,128)S(1)}) custom-call(s32[32]{0:T(128)S(1)} %multiply_add_fusion.index_ref, f32[4,8,16,256]{3,2,1,0:T(8,128)S(1)} %pad_maximum_fusion.5.refs_0_, f32[4,8,16,256]{3,2,1,0:T(8,128)S(1)} %collective-permute-done.9.refs_1_, f32[4,8,16,256]{3,2,1,0:T(8,128)S(1)} %collective-permute-done.10.refs_2_, ...), custom_call_target="tpu_custom_call" | custom-call | flops 70000001024 | bytes 12582912 | tf_op jit(solution)/shard_map/factor_and_invert/pallas_call | solution.py:210
  351.6 2.4 fusion.8
  354.1 4.3 fusion.2
  358.7 2.7 collective-permute-start.21
  363.3 3.1 collective-permute-done.20
  367.8 9.4 %collect_parents.3 = f32[256,16,128]{2,1,0:T(8,128)} custom-call(s32[1024]{0:T(1024)} %convert_element_type.22.at_ref, bf16[32,32,16,128]{3,2,1,0:T(8,128)(2,1)} %all-to-all-done.3.got_ref, bf16[256,1024]{1,0:T(8,128)(2,1)} %pad_maximum_fusion.6.refs_0_, bf16[3,16,1024]{2,1,0:T(8,128)(2,1)} %bitcast.66), custom_call_target="tpu_custom_call" | custom-call | flops 2097152 | bytes 6291456 | tf_op jit(solution)/shard_map/collect_parents/pallas_call | solution.py:83
  377.2 6.6 %all-to-all-start.4 = ((f32[32,8,16,128]{3,2,1,0:T(8,128)}), f32[32,8,16,128]{3,2,1,0:T(8,128)S(1)}, u32[]{:S(2)}, u32[]{:S(2)}) async-start(f32[32,8,16,128]{3,2,1,0:T(8,128)} %bitcast.55), calls=%async_computation.4 | async-start | bytes 4194304 | tf_op jit(solution)/shard_map/all_to_all | solution.py:338
  383.9 1.5 collective-permute-start.25
  385.3 2.6 collective-permute-start.24
  389.1 17.8 %fusion.lower_ref = f32[8,128,1024]{2,1,0:T(8,128)} fusion(f32[8,128,1024]{2,1,0:T(8,128)} %assemble_panel.1.panel_ref, f32[1024,1024]{1,0:T(8,128)} %copy-done), kind=kOutput, calls=%fused_computation | convolution fusion | flops 12884901888 | bytes 12582912 | tf_op jit(solution)/shard_map/dot_general | solution.py:16
  406.9 6.5 %collective-permute-done.24.refs_8_ = bf16[4,3,16,1024]{3,2,1,0:T(8,128)(2,1)} collective-permute-done((bf16[4,3,16,1024]{3,2,1,0:T(8,128)(2,1)S(1)}, bf16[4,3,16,1024]{3,2,1,0:T(8,128)(2,1)}, u32[]{:S(2)}, u32[]{:S(2)}) %collective-permute-start.24) | collective-permute-done | bytes 393248 | tf_op jit(solution)/shard_map/ppermute | solution.py:356
  413.4 1.9 collective-permute-done.23.refs_7_
  415.4 3.3 collective-permute-done.22.refs_6_
  420.7 5.7 %collective-permute-done.28.refs_3_ = bf16[128,1024]{1,0:T(8,128)(2,1)} collective-permute-done((bf16[128,1024]{1,0:T(8,128)(2,1)S(1)}, bf16[128,1024]{1,0:T(8,128)(2,1)}, u32[]{:S(2)}, u32[]{:S(2)}) %collective-permute-start.28) | collective-permute-done | bytes 262176 | tf_op jit(solution)/shard_map/ppermute | solution.py:457
  427.0 7.4 %collective-permute-done.27.refs_2_ = bf16[128,1024]{1,0:T(8,128)(2,1)} collective-permute-done((bf16[128,1024]{1,0:T(8,128)(2,1)}, bf16[128,1024]{1,0:T(8,128)(2,1)}, u32[]{:S(2)}, u32[]{:S(2)}) %collective-permute-start.27) | collective-permute-done | bytes 262176 | tf_op jit(solution)/shard_map/ppermute | solution.py:457
  435.9 11.0 %trailing_update.1 = f32[8,1,128,1536]{3,2,1,0:T(8,128)} custom-call(s32[6]{0:T(128)} %pad_add_fusion.order_ref, s32[32]{0:T(128)} %copy-done.1, f32[8,128,1024]{2,1,0:T(8,128)} %assemble_panel.1.panel_ref, f32[8,128,1024]{2,1,0:T(8,128)} %fusion.lower_ref, f32[128,1024]{1,0:T(8,128)} %copy-done.4, f32[8,1,128,1536]{3,2,1,0:T(8,128)} %front_ref.3, ...), custom_call_target="tpu_custom_call" | custom-call | flops 3221225472 | bytes 29360128 | tf_op jit(solution)/shard_map/trailing_update/pallas_call | solution.py:306
  (113 shorter events, 20.2 us)
Async XLA Ops:
  2.5 11.5 %copy-start.11 = (s32[32,128]{1,0:T(8,128)S(1)}, s32[32,128]{1,0:T(8,128)}, u32[]{:S(2)}) copy-start(s32[32,128]{1,0:T(8,128)} %param.10) | copy-start | bytes 49156
  3.9 29.2 %all-to-all-start = ((f32[32,40,256]{2,1,0:T(8,128)}), f32[32,40,256]{2,1,0:T(8,128)S(1)}, u32[]{:S(2)}, u32[]{:S(2)}) async-start(f32[32,40,256]{2,1,0:T(8,128)} %pad_maximum_fusion), calls=%async_computation | async-start | bytes 2621440 | tf_op jit(solution)/shard_map/all_to_all | solution.py:338
  34.2 111.7 %all-to-all-start.1 = ((bf16[32,32,16,256]{3,2,1,0:T(8,128)(2,1)}), bf16[32,32,16,256]{3,2,1,0:T(8,128)(2,1)}, u32[]{:S(2)}, u32[]{:S(2)}) async-start(bf16[32,32,16,256]{3,2,1,0:T(8,128)(2,1)} %bitcast.50), calls=%async_computation.1 | async-start | bytes 16777216 | tf_op jit(solution)/shard_map/all_to_all | solution.py:338
  157.6 23.7 %slice-start = ((f32[32,40,256]{2,1,0:T(8,128)}), f32[32,32,256]{2,1,0:T(8,128)S(1)}, s32[]{:S(2)}) async-start(f32[32,40,256]{2,1,0:T(8,128)} %copy-done.5), calls=%async_computation.5 | async-start | bytes 2097152 | tf_op jit(solution)/shard_map/slice | solution.py:413
  157.6 98.5 %all-to-all-start.2 = ((f32[32,8,16,256]{3,2,1,0:T(8,128)}), f32[32,8,16,256]{3,2,1,0:T(8,128)}, u32[]{:S(2)}, u32[]{:S(2)}) async-start(f32[32,8,16,256]{3,2,1,0:T(8,128)} %bitcast.51), calls=%async_computation.2 | async-start | bytes 8388608 | tf_op jit(solution)/shard_map/all_to_all | solution.py:338
  182.9 71.2 %copy-start.12 = (pred[48]{0:T(512)(128)(4,1)S(1)}, pred[48]{0:T(512)(128)(4,1)}, u32[]{:S(2)}) copy-start(pred[48]{0:T(512)(128)(4,1)} %constant.269) | copy-start | bytes 148
  182.9 71.2 %copy-start.13 = (pred[48]{0:T(512)(128)(4,1)S(1)}, pred[48]{0:T(512)(128)(4,1)}, u32[]{:S(2)}) copy-start(pred[48]{0:T(512)(128)(4,1)} %constant.268) | copy-start | bytes 148
  183.1 10.0 %collective-permute-start = (f32[20,16,256]{2,1,0:T(8,128)S(1)}, f32[20,16,256]{2,1,0:T(8,128)S(1)}, u32[]{:S(2)}, u32[]{:S(2)}) collective-permute-start(f32[20,16,256]{2,1,0:T(8,128)S(1)} %get-tuple-element.74), channel_id=1, source_target_pairs={{0,1},{4,5},{8,9},{12,13},{16,17},{20,21},{24,25},{28,29},{32,33},... | collective-permute-start | bytes 983048 | tf_op jit(solution)/shard_map/ppermute | solution.py:377
  186.3 13.8 %collective-permute-start.1 = (f32[20,16,256]{2,1,0:T(8,128)S(1)}, f32[20,16,256]{2,1,0:T(8,128)S(1)}, u32[]{:S(2)}, u32[]{:S(2)}) collective-permute-start(f32[20,16,256]{2,1,0:T(8,128)S(1)} %get-tuple-element.75), channel_id=1, source_target_pairs={{0,2},{4,6},{8,10},{12,14},{16,18},{20,22},{24,26},{28,30},{32,34}... | collective-permute-start | bytes 983048 | tf_op jit(solution)/shard_map/ppermute | solution.py:377
  188.6 11.5 %collective-permute-start.2 = (f32[20,16,256]{2,1,0:T(8,128)S(1)}, f32[20,16,256]{2,1,0:T(8,128)S(1)}, u32[]{:S(2)}, u32[]{:S(2)}) collective-permute-start(f32[20,16,256]{2,1,0:T(8,128)S(1)} %get-tuple-element.76), channel_id=1, source_target_pairs={{0,3},{4,7},{8,11},{12,15},{16,19},{20,23},{24,27},{28,31},{32,35}... | collective-permute-start | bytes 983048 | tf_op jit(solution)/shard_map/ppermute | solution.py:377
  200.3 35.7 %collective-permute-start.4 = (f32[8,16,256]{2,1,0:T(8,128)S(1)}, f32[8,16,256]{2,1,0:T(8,128)S(1)}, u32[]{:S(2)}, u32[]{:S(2)}) collective-permute-start(f32[8,16,256]{2,1,0:T(8,128)S(1)} %get-tuple-element.70), channel_id=1, source_target_pairs={{0,16},{4,68},{8,24},{12,76},{16,0},{20,84},{24,8},{28,92},{32,48}... | collective-permute-start | bytes 393224 | tf_op jit(solution)/shard_map/ppermute | solution.py:356
  203.2 32.8 %collective-permute-start.3 = (f32[8,16,256]{2,1,0:T(8,128)S(1)}, f32[8,16,256]{2,1,0:T(8,128)S(1)}, u32[]{:S(2)}, u32[]{:S(2)}) collective-permute-start(f32[8,16,256]{2,1,0:T(8,128)S(1)} %get-tuple-element.70), channel_id=1, source_target_pairs={{0,8},{4,36},{8,16},{12,44},{16,24},{20,52},{24,0},{28,60},{32,40}... | collective-permute-start | bytes 393224 | tf_op jit(solution)/shard_map/ppermute | solution.py:356
  203.5 32.5 %collective-permute-start.5 = (f32[8,16,256]{2,1,0:T(8,128)S(1)}, f32[8,16,256]{2,1,0:T(8,128)S(1)}, u32[]{:S(2)}, u32[]{:S(2)}) collective-permute-start(f32[8,16,256]{2,1,0:T(8,128)S(1)} %get-tuple-element.70), channel_id=1, source_target_pairs={{0,24},{4,100},{8,0},{12,108},{16,8},{20,116},{24,16},{28,124},{32... | collective-permute-start | bytes 393224 | tf_op jit(solution)/shard_map/ppermute | solution.py:356
  205.9 30.1 %collective-permute-start.8 = (f32[3,16,256]{2,1,0:T(8,128)S(1)}, f32[3,16,256]{2,1,0:T(8,128)S(1)}, u32[]{:S(2)}, u32[]{:S(2)}) collective-permute-start(f32[3,16,256]{2,1,0:T(8,128)S(1)} %get-tuple-element.71), channel_id=1, source_target_pairs={{0,12},{4,8},{8,4},{12,0},{16,28},{20,24},{24,20},{28,16},{32,44},... | collective-permute-start | bytes 147464 | tf_op jit(solution)/shard_map/ppermute | solution.py:388
  206.9 2.0 collective-permute-start.6
  209.0 23.6 %collective-permute-start.7 = (f32[3,16,256]{2,1,0:T(8,128)S(1)}, f32[3,16,256]{2,1,0:T(8,128)S(1)}, u32[]{:S(2)}, u32[]{:S(2)}) collective-permute-start(f32[3,16,256]{2,1,0:T(8,128)S(1)} %get-tuple-element.72), channel_id=1, source_target_pairs={{0,8},{4,12},{8,0},{12,4},{16,24},{20,28},{24,16},{28,20},{32,40},... | collective-permute-start | bytes 147464 | tf_op jit(solution)/shard_map/ppermute | solution.py:388
  236.0 9.1 %collective-permute-start.11 = (f32[4,8,16,256]{3,2,1,0:T(8,128)S(1)}, f32[4,8,16,256]{3,2,1,0:T(8,128)S(1)}, u32[]{:S(2)}, u32[]{:S(2)}) collective-permute-start(f32[4,8,16,256]{3,2,1,0:T(8,128)S(1)} %pad_maximum_fusion.5.refs_0_), channel_id=1, source_target_pairs={{0,96},{4,28},{8,104},{12,4},{16,112},{20,12},{24,120},{28,20},{32... | collective-permute-start | bytes 1572872 | tf_op jit(solution)/shard_map/ppermute | solution.py:356
  236.4 10.6 %collective-permute-start.10 = (f32[4,8,16,256]{3,2,1,0:T(8,128)S(1)}, f32[4,8,16,256]{3,2,1,0:T(8,128)S(1)}, u32[]{:S(2)}, u32[]{:S(2)}) collective-permute-start(f32[4,8,16,256]{3,2,1,0:T(8,128)S(1)} %pad_maximum_fusion.5.refs_0_), channel_id=1, source_target_pairs={{0,64},{4,20},{8,72},{12,28},{16,80},{20,4},{24,88},{28,12},{32,96... | collective-permute-start | bytes 1572872 | tf_op jit(solution)/shard_map/ppermute | solution.py:356
  240.1 12.5 %collective-permute-start.9 = (f32[4,8,16,256]{3,2,1,0:T(8,128)S(1)}, f32[4,8,16,256]{3,2,1,0:T(8,128)S(1)}, u32[]{:S(2)}, u32[]{:S(2)}) collective-permute-start(f32[4,8,16,256]{3,2,1,0:T(8,128)S(1)} %pad_maximum_fusion.5.refs_0_), channel_id=1, source_target_pairs={{0,32},{4,12},{8,40},{12,20},{16,48},{20,28},{24,56},{28,4},{32,64... | collective-permute-start | bytes 1572872 | tf_op jit(solution)/shard_map/ppermute | solution.py:356
  240.7 33.7 %collective-permute-start.12 = (f32[4,8,16,256]{3,2,1,0:T(8,128)S(1)}, f32[4,8,16,256]{3,2,1,0:T(8,128)S(1)}, u32[]{:S(2)}, u32[]{:S(2)}) collective-permute-start(f32[4,8,16,256]{3,2,1,0:T(8,128)S(1)} %pad_maximum_fusion.5.refs_0_), channel_id=1, source_target_pairs={{0,4},{4,0},{8,12},{12,8},{16,20},{20,16},{24,28},{28,24},{32,36},... | collective-permute-start | bytes 1572872 | tf_op jit(solution)/shard_map/ppermute | solution.py:361
  245.2 31.5 %collective-permute-start.15 = (f32[4,8,16,256]{3,2,1,0:T(8,128)S(1)}, f32[4,8,16,256]{3,2,1,0:T(8,128)S(1)}, u32[]{:S(2)}, u32[]{:S(2)}) collective-permute-start(f32[4,8,16,256]{3,2,1,0:T(8,128)S(1)} %collective-permute-done.11.refs_3_), channel_id=1, source_target_pairs={{0,4},{4,0},{8,12},{12,8},{16,20},{20,16},{24,28},{28,24},{32,36},... | collective-permute-start | bytes 1572872 | tf_op jit(solution)/shard_map/ppermute | solution.py:361
  247.0 31.0 %collective-permute-start.14 = (f32[4,8,16,256]{3,2,1,0:T(8,128)S(1)}, f32[4,8,16,256]{3,2,1,0:T(8,128)}, u32[]{:S(2)}, u32[]{:S(2)}) collective-permute-start(f32[4,8,16,256]{3,2,1,0:T(8,128)S(1)} %collective-permute-done.10.refs_2_), channel_id=1, source_target_pairs={{0,4},{4,0},{8,12},{12,8},{16,20},{20,16},{24,28},{28,24},{32,36},... | collective-permute-start | bytes 1572872 | tf_op jit(solution)/shard_map/ppermute | solution.py:361
  252.6 25.5 %collective-permute-start.13 = (f32[4,8,16,256]{3,2,1,0:T(8,128)S(1)}, f32[4,8,16,256]{3,2,1,0:T(8,128)}, u32[]{:S(2)}, u32[]{:S(2)}) collective-permute-start(f32[4,8,16,256]{3,2,1,0:T(8,128)S(1)} %collective-permute-done.9.refs_1_), channel_id=1, source_target_pairs={{0,4},{4,0},{8,12},{12,8},{16,20},{20,16},{24,28},{28,24},{32,36},... | collective-permute-start | bytes 1572872 | tf_op jit(solution)/shard_map/ppermute | solution.py:361
  256.1 22.0 %copy-start.1 = (s32[32]{0:T(128)}, s32[32]{0:T(128)S(1)}, u32[]{:S(2)}) copy-start(s32[32]{0:T(128)S(1)} %multiply_add_fusion.index_ref) | copy-start | bytes 388
  256.1 111.7 %all-to-all-start.3 = ((bf16[32,32,16,128]{3,2,1,0:T(8,128)(2,1)}), bf16[32,32,16,128]{3,2,1,0:T(8,128)(2,1)}, u32[]{:S(2)}, u32[]{:S(2)}) async-start(bf16[32,32,16,128]{3,2,1,0:T(8,128)(2,1)} %bitcast.53), calls=%async_computation.3 | async-start | bytes 8388608 | tf_op jit(solution)/shard_map/all_to_all | solution.py:338
  271.2 80.4 %collective-permute-start.16 = (f32[2,128,1024]{2,1,0:T(8,128)S(1)}, f32[2,128,1024]{2,1,0:T(8,128)S(1)}, u32[]{:S(2)}, u32[]{:S(2)}) collective-permute-start(f32[2,128,1024]{2,1,0:T(8,128)S(1)} %get-tuple-element.57), channel_id=1, source_target_pairs={{0,1},{4,5},{8,9},{12,13},{16,17},{20,21},{24,25},{28,29},{32,33},... | collective-permute-start | bytes 3145736 | tf_op jit(solution)/shard_map/ppermute | solution.py:377
  274.5 77.1 %collective-permute-start.18 = (f32[2,128,1024]{2,1,0:T(8,128)S(1)}, f32[2,128,1024]{2,1,0:T(8,128)S(1)}, u32[]{:S(2)}, u32[]{:S(2)}) collective-permute-start(f32[2,128,1024]{2,1,0:T(8,128)S(1)} %get-tuple-element.58), channel_id=1, source_target_pairs={{0,3},{4,7},{8,11},{12,15},{16,19},{20,23},{24,27},{28,31},{32,35}... | collective-permute-start | bytes 3145736 | tf_op jit(solution)/shard_map/ppermute | solution.py:377
  276.6 75.0 %collective-permute-start.17 = (f32[2,128,1024]{2,1,0:T(8,128)S(1)}, f32[2,128,1024]{2,1,0:T(8,128)S(1)}, u32[]{:S(2)}, u32[]{:S(2)}) collective-permute-start(f32[2,128,1024]{2,1,0:T(8,128)S(1)} %get-tuple-element.59), channel_id=1, source_target_pairs={{0,2},{4,6},{8,10},{12,14},{16,18},{20,22},{24,26},{28,30},{32,34}... | collective-permute-start | bytes 3145736 | tf_op jit(solution)/shard_map/ppermute | solution.py:377
  358.6 9.2 %copy-start.9 = (bf16[48,1024]{1,0:T(8,128)(2,1)}, bf16[48,1024]{1,0:T(8,128)(2,1)S(1)}, u32[]{:S(2)}) copy-start(bf16[48,1024]{1,0:T(8,128)(2,1)S(1)} %slice.125) | copy-start | bytes 294916
  358.7 4.7 %collective-permute-start.21 = (bf16[3,16,1024]{2,1,0:T(8,128)(2,1)S(1)}, bf16[3,16,1024]{2,1,0:T(8,128)(2,1)S(1)}, u32[]{:S(2)}, u32[]{:S(2)}) collective-permute-start(bf16[3,16,1024]{2,1,0:T(8,128)(2,1)S(1)} %bitcast.62), channel_id=1, source_target_pairs={{0,24},{4,100},{8,0},{12,108},{16,8},{20,116},{24,16},{28,124},{32... | collective-permute-start | bytes 294920 | tf_op jit(solution)/shard_map/ppermute | solution.py:356
  361.4 5.1 %collective-permute-start.20 = (bf16[3,16,1024]{2,1,0:T(8,128)(2,1)S(1)}, bf16[3,16,1024]{2,1,0:T(8,128)(2,1)S(1)}, u32[]{:S(2)}, u32[]{:S(2)}) collective-permute-start(bf16[3,16,1024]{2,1,0:T(8,128)(2,1)S(1)} %bitcast.63), channel_id=1, source_target_pairs={{0,16},{4,68},{8,24},{12,76},{16,0},{20,84},{24,8},{28,92},{32,48}... | collective-permute-start | bytes 294920 | tf_op jit(solution)/shard_map/ppermute | solution.py:356
  361.9 5.8 %collective-permute-start.19 = (bf16[3,16,1024]{2,1,0:T(8,128)(2,1)S(1)}, bf16[3,16,1024]{2,1,0:T(8,128)(2,1)S(1)}, u32[]{:S(2)}, u32[]{:S(2)}) collective-permute-start(bf16[3,16,1024]{2,1,0:T(8,128)(2,1)S(1)} %bitcast.64), channel_id=1, source_target_pairs={{0,8},{4,36},{8,16},{12,44},{16,24},{20,52},{24,0},{28,60},{32,40}... | collective-permute-start | bytes 294920 | tf_op jit(solution)/shard_map/ppermute | solution.py:356
  367.7 51.1 %copy-start.6 = (bf16[4,3,16,1024]{3,2,1,0:T(8,128)(2,1)}, bf16[4,3,16,1024]{3,2,1,0:T(8,128)(2,1)S(1)}, u32[]{:S(2)}) copy-start(bf16[4,3,16,1024]{3,2,1,0:T(8,128)(2,1)S(1)} %pad_maximum_fusion.7.refs_5_) | copy-start | bytes 1179652
  367.7 16.0 %copy-start.3 = (bf16[256,1024]{1,0:T(8,128)(2,1)S(1)}, bf16[256,1024]{1,0:T(8,128)(2,1)}, u32[]{:S(2)}) copy-start(bf16[256,1024]{1,0:T(8,128)(2,1)} %pad_maximum_fusion.6.refs_0_) | copy-start | bytes 1572868
  377.2 57.3 %all-to-all-start.4 = ((f32[32,8,16,128]{3,2,1,0:T(8,128)}), f32[32,8,16,128]{3,2,1,0:T(8,128)S(1)}, u32[]{:S(2)}, u32[]{:S(2)}) async-start(f32[32,8,16,128]{3,2,1,0:T(8,128)} %bitcast.55), calls=%async_computation.4 | async-start | bytes 4194304 | tf_op jit(solution)/shard_map/all_to_all | solution.py:338
  383.8 23.1 %collective-permute-start.26 = (bf16[256,1024]{1,0:T(8,128)(2,1)S(1)}, bf16[256,1024]{1,0:T(8,128)(2,1)S(1)}, u32[]{:S(2)}, u32[]{:S(2)}) collective-permute-start(bf16[256,1024]{1,0:T(8,128)(2,1)S(1)} %copy-done.3), channel_id=1, source_target_pairs={{0,3},{1,0},{2,1},{3,2},{4,7},{5,4},{6,5},{7,6},{8,11},{9,8},{10,9... | collective-permute-start | bytes 1572872 | tf_op jit(solution)/shard_map/ppermute | solution.py:457
  383.9 23.0 %collective-permute-start.25 = (bf16[256,1024]{1,0:T(8,128)(2,1)S(1)}, bf16[256,1024]{1,0:T(8,128)(2,1)S(1)}, u32[]{:S(2)}, u32[]{:S(2)}) collective-permute-start(bf16[256,1024]{1,0:T(8,128)(2,1)S(1)} %copy-done.3), channel_id=1, source_target_pairs={{0,1},{1,2},{2,3},{3,0},{4,5},{5,6},{6,7},{7,4},{8,9},{9,10},{10,1... | collective-permute-start | bytes 1572872 | tf_op jit(solution)/shard_map/ppermute | solution.py:457
  385.3 28.1 %collective-permute-start.24 = (bf16[4,3,16,1024]{3,2,1,0:T(8,128)(2,1)S(1)}, bf16[4,3,16,1024]{3,2,1,0:T(8,128)(2,1)}, u32[]{:S(2)}, u32[]{:S(2)}) collective-permute-start(bf16[4,3,16,1024]{3,2,1,0:T(8,128)(2,1)S(1)} %pad_maximum_fusion.7.refs_5_), channel_id=1, source_target_pairs={{0,96},{4,28},{8,104},{12,4},{16,112},{20,12},{24,120},{28,20},{32... | collective-permute-start | bytes 1179656 | tf_op jit(solution)/shard_map/ppermute | solution.py:356
  387.9 27.5 %collective-permute-start.23 = (bf16[4,3,16,1024]{3,2,1,0:T(8,128)(2,1)S(1)}, bf16[4,3,16,1024]{3,2,1,0:T(8,128)(2,1)}, u32[]{:S(2)}, u32[]{:S(2)}) collective-permute-start(bf16[4,3,16,1024]{3,2,1,0:T(8,128)(2,1)S(1)} %pad_maximum_fusion.7.refs_5_), channel_id=1, source_target_pairs={{0,64},{4,20},{8,72},{12,28},{16,80},{20,4},{24,88},{28,12},{32,96... | collective-permute-start | bytes 1179656 | tf_op jit(solution)/shard_map/ppermute | solution.py:356
  388.5 30.2 %collective-permute-start.22 = (bf16[4,3,16,1024]{3,2,1,0:T(8,128)(2,1)S(1)}, bf16[4,3,16,1024]{3,2,1,0:T(8,128)(2,1)}, u32[]{:S(2)}, u32[]{:S(2)}) collective-permute-start(bf16[4,3,16,1024]{3,2,1,0:T(8,128)(2,1)S(1)} %pad_maximum_fusion.7.refs_5_), channel_id=1, source_target_pairs={{0,32},{4,12},{8,40},{12,20},{16,48},{20,28},{24,56},{28,4},{32,64... | collective-permute-start | bytes 1179656 | tf_op jit(solution)/shard_map/ppermute | solution.py:356
  406.9 27.6 %copy-start.7 = (bf16[256,1024]{1,0:T(8,128)(2,1)}, bf16[256,1024]{1,0:T(8,128)(2,1)S(1)}, u32[]{:S(2)}) copy-start(bf16[256,1024]{1,0:T(8,128)(2,1)S(1)} %collective-permute-done.26.refs_4_) | copy-start | bytes 1572868
  406.9 13.1 %copy-start.8 = (bf16[256,1024]{1,0:T(8,128)(2,1)}, bf16[256,1024]{1,0:T(8,128)(2,1)S(1)}, u32[]{:S(2)}) copy-start(bf16[256,1024]{1,0:T(8,128)(2,1)S(1)} %collective-permute-done.25.refs_1_) | copy-start | bytes 1572868
  418.7 7.6 %collective-permute-start.28 = (bf16[128,1024]{1,0:T(8,128)(2,1)S(1)}, bf16[128,1024]{1,0:T(8,128)(2,1)}, u32[]{:S(2)}, u32[]{:S(2)}) collective-permute-start(bf16[128,1024]{1,0:T(8,128)(2,1)S(1)} %slice.104), channel_id=1, source_target_pairs={{0,3},{1,0},{2,1},{3,2},{4,7},{5,4},{6,5},{7,6},{8,11},{9,8},{10,9... | collective-permute-start | bytes 786440 | tf_op jit(solution)/shard_map/ppermute | solution.py:457
  418.8 15.6 %collective-permute-start.29 = (bf16[4,3,16,1024]{3,2,1,0:T(8,128)(2,1)S(1)}, bf16[4,3,16,1024]{3,2,1,0:T(8,128)(2,1)S(1)}, u32[]{:S(2)}, u32[]{:S(2)}) collective-permute-start(bf16[4,3,16,1024]{3,2,1,0:T(8,128)(2,1)S(1)} %pad_maximum_fusion.7.refs_5_), channel_id=1, source_target_pairs={{0,4},{4,0},{8,12},{12,8},{16,20},{20,16},{24,28},{28,24},{32,36},... | collective-permute-start | bytes 1179656 | tf_op jit(solution)/shard_map/ppermute | solution.py:361
  419.3 15.1 %collective-permute-start.30 = (bf16[4,3,16,1024]{3,2,1,0:T(8,128)(2,1)}, bf16[4,3,16,1024]{3,2,1,0:T(8,128)(2,1)}, u32[]{:S(2)}, u32[]{:S(2)}) collective-permute-start(bf16[4,3,16,1024]{3,2,1,0:T(8,128)(2,1)} %collective-permute-done.22.refs_6_), channel_id=1, source_target_pairs={{0,4},{4,0},{8,12},{12,8},{16,20},{20,16},{24,28},{28,24},{32,36},... | collective-permute-start | bytes 1179656 | tf_op jit(solution)/shard_map/ppermute | solution.py:361
  419.4 15.0 %collective-permute-start.31 = (bf16[4,3,16,1024]{3,2,1,0:T(8,128)(2,1)}, bf16[4,3,16,1024]{3,2,1,0:T(8,128)(2,1)}, u32[]{:S(2)}, u32[]{:S(2)}) collective-permute-start(bf16[4,3,16,1024]{3,2,1,0:T(8,128)(2,1)} %collective-permute-done.23.refs_7_), channel_id=1, source_target_pairs={{0,4},{4,0},{8,12},{12,8},{16,20},{20,16},{24,28},{28,24},{32,36},... | collective-permute-start | bytes 1179656 | tf_op jit(solution)/shard_map/ppermute | solution.py:361
  419.9 14.6 %collective-permute-start.32 = (bf16[4,3,16,1024]{3,2,1,0:T(8,128)(2,1)}, bf16[4,3,16,1024]{3,2,1,0:T(8,128)(2,1)}, u32[]{:S(2)}, u32[]{:S(2)}) collective-permute-start(bf16[4,3,16,1024]{3,2,1,0:T(8,128)(2,1)} %collective-permute-done.24.refs_8_), channel_id=1, source_target_pairs={{0,4},{4,0},{8,12},{12,8},{16,20},{20,16},{24,28},{28,24},{32,36},... | collective-permute-start | bytes 1179656 | tf_op jit(solution)/shard_map/ppermute | solution.py:361
  426.4 8.1 %collective-permute-start.27 = (bf16[128,1024]{1,0:T(8,128)(2,1)}, bf16[128,1024]{1,0:T(8,128)(2,1)}, u32[]{:S(2)}, u32[]{:S(2)}) collective-permute-start(bf16[128,1024]{1,0:T(8,128)(2,1)} %slice.103), channel_id=1, source_target_pairs={{0,1},{1,2},{2,3},{3,0},{4,5},{5,6},{6,7},{7,4},{8,9},{9,10},{10,1... | collective-permute-start | bytes 786440 | tf_op jit(solution)/shard_map/ppermute | solution.py:457
  (5 other events, 17.1 us)

commit v5 on v4

--- a/solution.py
+++ b/solution.py
@@ -59,23 +59,30 @@
 
 
 def collect_kernel(at_ref, got_ref, *refs):
-    out_ref = refs[-1]
+    out_ref, odd_ref = refs[-2:]
     step = pl.program_id(0)
 
     @pl.when(step == 0)
     def _():
         out_ref[...] = jnp.zeros_like(out_ref)
+        odd_ref[...] = jnp.zeros_like(odd_ref)
 
     sources, slots = got_ref.shape[:2]
 
-    def add(source, carry):
+    def add(pair, carry):
+        source = pair * 2
         base = (step * sources + source) * slots
         for slot in range(slots):
-            at = at_ref[base + slot]
+            at, odd = at_ref[base + slot], at_ref[base + slots + slot]
             out_ref[at] = out_ref[at] + got_ref[source, slot].astype(f32)
+            odd_ref[odd] = odd_ref[odd] + got_ref[source + 1, slot].astype(f32)
         return carry
 
-    lax.fori_loop(0, sources, add, 0)
+    lax.fori_loop(0, sources // 2, add, 0)
+
+    @pl.when(step == pl.num_programs(0) - 1)
+    def _():
+        out_ref[...] = out_ref[...] + odd_ref[...]
 
 
 def collect(at, got, *after):
@@ -88,6 +95,7 @@
             in_specs=[pl.BlockSpec((4, slots, 16, width), lambda s, at: (s, 0, 0, 0))]
             + [pl.BlockSpec(memory_space=pl.ANY)] * len(after),
             out_specs=pl.BlockSpec((256, 16, width), lambda s, at: (0, 0, 0)),
+            scratch_shapes=[pltpu.VMEM((256, 16, width), f32)],
         ),
         out_shape=jax.ShapeDtypeStruct((256, 16, width), f32),
         compiler_params=pltpu.CompilerParams(vmem_limit_bytes=56 * MIB),
@@ -226,21 +234,23 @@
 
 
 def assemble_kernel(front_ref, got_ref, out_ref):
-    for jc in range(4):
-        cols = slice(jc * 256, jc * 256 + 256)
-        out_ref[0, :, cols] = front_ref[0, 0, :, cols] + got_ref[:, jc, 0].reshape(128, 256)
+    for tile in range(2):
+        for jc in range(4):
+            cols = slice(jc * 256, jc * 256 + 256)
+            sums = got_ref[:, jc, tile].reshape(128, 256)
+            out_ref[tile, :, cols] = front_ref[tile, 0, :, cols] + sums
 
 
 def assemble(front, got):
     k = front.shape[0]
     return pl.pallas_call(
         assemble_kernel,
-        grid=(k,),
+        grid=(k // 2,),
         in_specs=[
-            pl.BlockSpec((1, 1, 128, PANEL), lambda i: (i, 0, 0, 0)),
-            pl.BlockSpec((8, 4, 1, 16, 256), lambda i: (0, 0, i, 0, 0)),
+            pl.BlockSpec((2, 1, 128, PANEL), lambda i: (i, 0, 0, 0)),
+            pl.BlockSpec((8, 4, 2, 16, 256), lambda i: (0, 0, i, 0, 0)),
         ],
-        out_specs=pl.BlockSpec((1, 128, PANEL), lambda i: (i, 0, 0)),
+        out_specs=pl.BlockSpec((2, 128, PANEL), lambda i: (i, 0, 0)),
         out_shape=jax.ShapeDtypeStruct((k, 128, PANEL), f32),
         compiler_params=pltpu.CompilerParams(vmem_limit_bytes=56 * MIB),
         cost_estimate=pl.CostEstimate(
@@ -458,11 +468,14 @@
 
     before, behind = turn(own, 1), turn(own, 3)
     sums_rest = collect(at, got_rest, own, part)
-    ring, sums_rest = together(jnp.stack(ring_stage(part, 0)), sums_rest)
+    ring, sums_rest, before, behind = together(
+        jnp.stack(ring_stage(part, 0)), sums_rest, before, behind
+    )
     got_rest = exchange(sums_rest.reshape(32, 8, 16, 128)).reshape(8, 4, 8, 16, 128)
     lower = times_transposed(panel.reshape(8 * 128, PANEL), inverse).reshape(8, 128, PANEL)
-    *mine, lower, before, behind = together(*ring_stage(ring, 1), lower, before, behind)
-    spread = [own, before, turn(before[:128], 1), turn(behind[128:], 3), behind]
+    far = turn(before[:128], 1), turn(behind[128:], 3)
+    *mine, lower, far_before, far_behind = together(*ring_stage(ring, 1), lower, *far)
+    spread = [own, before, far_before, far_behind, behind]
     slab = with_cores(mine)
 
     order = (col_index + 4 - jnp.arange(4, dtype=jnp.int32)) % 4

time: 452 us -> 438 us (0.969)
  waiting for transfers between devices: 182 us -> 170 us
    ppermute x4, waiting for transfers between devices: 13.1 us -> 0.01 us  [turn(): return lax.ppermute(x, 'col', [(c, (c + by) % 4) for c in range(4)])]
  transfers between devices with their start and end apart: 38 -> 38, of which waited for: 17 -> 19; matrix products, arithmetic and copies ran while one was open for 8% -> 8% of each run, Pallas kernels for 22% -> 24%
where the time goes in v5:
time: 438 us; the launch traced here: 434 us
  waiting for transfers between devices  170 us (39%)
  Pallas kernels  127 us (29%)
  starting transfers between devices  94 us (21%)
  matrix products  22.1 us (5%)
  other arithmetic  9.52 us (2%)
  local copies, waits for them, and re-layouts  9.48 us (2%)
    all_to_all x5, waiting for transfers between devices, exchange(): return lax.all_to_all(x, 'row', split_axis=0, concat_axis=0, tiled=True)  107 us
    pallas_call x1, Pallas kernels, factor(): pl.pallas_call(factor_kernel, in_specs=[pl.BlockSpec(memory_space=pltpu.S...  73.4 us
    all_to_all x5, starting transfers between devices, exchange(): return lax.all_to_all(x, 'row', split_axis=0, concat_axis=0, tiled=True)  50.4 us
    ppermute x3, waiting for transfers between devices, own_rows(): part = lax.ppermute(part, 'row', [(r, r ^ by) for r in range(32)])  26.2 us
    ppermute x12, waiting for transfers between devices, ring_stage(): parts.append(lax.ppermute(x, 'row', moves))  24.6 us
    dot_general x2, matrix products, times_transposed(): lax.dot_general(a, b, (((1,), (1,)), ((), ())), precision=precision, pref...  22.1 us
    pallas_call x2, Pallas kernels, collect(): pl.pallas_call(collect_kernel, grid_spec=pltpu.PrefetchScalarGridSpec(num...  19.2 us
    pallas_call x2, Pallas kernels, place(): pl.pallas_call(place_kernel, grid=(slots // 4,), in_specs=[pl.BlockSpec((...  18 us
  transfers between devices with their start and end apart: 38, of which 19 were waited for; matrix products, arithmetic and copies ran while one was open for 8% of the time, Pallas kernels for 24%

profile of v5, /device:TPU:1, one launch (start us, length us, event | category | flops | bytes accessed | tf_op | source)
XLA Modules:
  0.0 434.3 jit_solution(2207342087853193106)
XLA Ops:
  0.7 1.3 slice.83
  3.9 9.4 %all-to-all-start = ((f32[32,40,256]{2,1,0:T(8,128)}), f32[32,40,256]{2,1,0:T(8,128)S(1)}, u32[]{:S(2)}, u32[]{:S(2)}) async-start(f32[32,40,256]{2,1,0:T(8,128)} %pad_maximum_fusion), calls=%async_computation | async-start | bytes 2621440 | tf_op jit(solution)/shard_map/all_to_all | solution.py:348
  14.7 10.4 %place_rows.2 = bf16[8,4,32,16,256]{4,3,2,1,0:T(8,128)(2,1)} custom-call(s32[8,4,128]{2,1,0:T(4,128)} %bitcast.70, bf16[32,128,1536]{2,1,0:T(8,128)(2,1)} %child_ref.3), custom_call_target="tpu_custom_call" | custom-call | flops 1073741824 | bytes 16777216 | tf_op jit(solution)/shard_map/place_rows/pallas_call | solution.py:42
  25.1 8.0 %all-to-all-done = f32[32,40,256]{2,1,0:T(8,128)S(1)} async-done(((f32[32,40,256]{2,1,0:T(8,128)}), f32[32,40,256]{2,1,0:T(8,128)S(1)}, u32[]{:S(2)}, u32[]{:S(2)}) %all-to-all-start) | async-done | bytes 1310752 | tf_op jit(solution)/shard_map/all_to_all | solution.py:348
  34.2 4.9 %all-to-all-start.1 = ((bf16[32,32,16,256]{3,2,1,0:T(8,128)(2,1)}), bf16[32,32,16,256]{3,2,1,0:T(8,128)(2,1)}, u32[]{:S(2)}, u32[]{:S(2)}) async-start(bf16[32,32,16,256]{3,2,1,0:T(8,128)(2,1)} %bitcast.50), calls=%async_computation.1 | async-start | bytes 16777216 | tf_op jit(solution)/shard_map/all_to_all | solution.py:348
  39.2 7.6 %place_rows.3 = bf16[8,4,32,16,128]{4,3,2,1,0:T(8,128)(2,1)} custom-call(s32[8,4,128]{2,1,0:T(4,128)} %bitcast.71, bf16[32,128,1536]{2,1,0:T(8,128)(2,1)} %child_ref.3), custom_call_target="tpu_custom_call" | custom-call | flops 536870912 | bytes 8388608 | tf_op jit(solution)/shard_map/place_rows/pallas_call | solution.py:42
  46.8 99.2 %all-to-all-done.1.got_ref = bf16[32,32,16,256]{3,2,1,0:T(8,128)(2,1)} async-done(((bf16[32,32,16,256]{3,2,1,0:T(8,128)(2,1)}), bf16[32,32,16,256]{3,2,1,0:T(8,128)(2,1)}, u32[]{:S(2)}, u32[]{:S(2)}) %all-to-all-start.1) | async-done | bytes 8388640 | tf_op jit(solution)/shard_map/all_to_all | solution.py:348
  146.0 10.7 %collect_parents.2 = f32[256,16,256]{2,1,0:T(8,128)} custom-call(s32[1024]{0:T(1024)} %convert_element_type.22.at_ref, bf16[32,32,16,256]{3,2,1,0:T(8,128)(2,1)} %all-to-all-done.1.got_ref), custom_call_target="tpu_custom_call" | custom-call | flops 4194304 | bytes 12582912 | tf_op jit(solution)/shard_map/collect_parents/pallas_call | solution.py:90
  156.7 23.7 %all-to-all-start.2 = ((f32[32,8,16,256]{3,2,1,0:T(8,128)}), f32[32,8,16,256]{3,2,1,0:T(8,128)}, u32[]{:S(2)}, u32[]{:S(2)}) async-start(f32[32,8,16,256]{3,2,1,0:T(8,128)} %bitcast.51), calls=%async_computation.2 | async-start | bytes 8388608 | tf_op jit(solution)/shard_map/all_to_all | solution.py:348
  180.4 1.5 fusion.9
  182.2 3.2 collective-permute-start
  185.4 2.3 collective-permute-start.1
  187.7 1.3 collective-permute-start.2
  189.1 3.1 collective-permute-done
  192.2 7.0 %collective-permute-done.1 = f32[20,16,256]{2,1,0:T(8,128)S(1)} collective-permute-done((f32[20,16,256]{2,1,0:T(8,128)S(1)}, f32[20,16,256]{2,1,0:T(8,128)S(1)}, u32[]{:S(2)}, u32[]{:S(2)}) %collective-permute-start.1) | collective-permute-done | bytes 327712 | tf_op jit(solution)/shard_map/ppermute | solution.py:387
  199.4 2.9 collective-permute-start.4
  202.6 2.4 collective-permute-start.5
  208.1 1.6 collective-permute-start.7
  209.7 22.0 %collective-permute-done.7 = f32[3,16,256]{2,1,0:T(8,128)S(1)} collective-permute-done((f32[3,16,256]{2,1,0:T(8,128)S(1)}, f32[3,16,256]{2,1,0:T(8,128)S(1)}, u32[]{:S(2)}, u32[]{:S(2)}) %collective-permute-start.7) | collective-permute-done | bytes 49184 | tf_op jit(solution)/shard_map/ppermute | solution.py:398
  231.7 3.3 collective-permute-done.8
  235.5 3.7 collective-permute-start.10
  240.1 4.2 collective-permute-done.11.refs_3_
  244.3 1.4 collective-permute-start.15
  246.1 1.6 collective-permute-start.14
  247.7 4.0 collective-permute-done.9.refs_1_
  251.7 1.5 collective-permute-start.13
  253.2 1.8 select_select_fusion
  255.2 5.2 %all-to-all-start.3 = ((bf16[32,32,16,128]{3,2,1,0:T(8,128)(2,1)}), bf16[32,32,16,128]{3,2,1,0:T(8,128)(2,1)}, u32[]{:S(2)}, u32[]{:S(2)}) async-start(bf16[32,32,16,128]{3,2,1,0:T(8,128)(2,1)} %bitcast.53), calls=%async_computation.3 | async-start | bytes 8388608 | tf_op jit(solution)/shard_map/all_to_all | solution.py:348
  260.4 5.8 %assemble_panel.1.panel_ref = f32[8,128,1024]{2,1,0:T(8,128)} custom-call(f32[8,1,128,1536]{3,2,1,0:T(8,128)} %front_ref.3, f32[8,4,8,16,256]{4,3,2,1,0:T(8,128)} %bitcast.11.got_ref), custom_call_target="tpu_custom_call" | custom-call | flops 1048576 | bytes 12582912 | tf_op jit(solution)/shard_map/assemble_panel/pallas_call | solution.py:246
  266.2 2.3 fusion.29
  268.4 3.3 collective-permute-start.16
  271.7 2.2 collective-permute-start.18
  273.9 1.4 collective-permute-start.17
  275.3 73.4 %factor_and_invert.1 = (f32[1024,1024]{1,0:T(8,128)S(1)}, f32[1024,1024]{1,0:T(8,128)S(1)}) custom-call(s32[32]{0:T(128)S(1)} %multiply_add_fusion.index_ref, f32[4,8,16,256]{3,2,1,0:T(8,128)S(1)} %pad_maximum_fusion.5.refs_0_, f32[4,8,16,256]{3,2,1,0:T(8,128)S(1)} %collective-permute-done.9.refs_1_, f32[4,8,16,256]{3,2,1,0:T(8,128)S(1)} %collective-permute-done.10.refs_2_, ...), custom_call_target="tpu_custom_call" | custom-call | flops 70000001024 | bytes 12582912 | tf_op jit(solution)/shard_map/factor_and_invert/pallas_call | solution.py:218
  348.9 2.4 fusion.8
  351.3 4.3 fusion.2
  356.0 1.5 collective-permute-start.22
  357.5 2.7 collective-permute-start.21
  361.8 3.4 collective-permute-done.20
  366.6 8.5 %collect_parents.3 = f32[256,16,128]{2,1,0:T(8,128)} custom-call(s32[1024]{0:T(1024)} %convert_element_type.22.at_ref, bf16[32,32,16,128]{3,2,1,0:T(8,128)(2,1)} %all-to-all-done.3.got_ref, bf16[256,1024]{1,0:T(8,128)(2,1)} %copy-done.3, bf16[3,16,1024]{2,1,0:T(8,128)(2,1)} %bitcast.66), custom_call_target="tpu_custom_call" | custom-call | flops 2097152 | bytes 6291456 | tf_op jit(solution)/shard_map/collect_parents/pallas_call | solution.py:90
  375.9 7.1 %all-to-all-start.4 = ((f32[32,8,16,128]{3,2,1,0:T(8,128)}), f32[32,8,16,128]{3,2,1,0:T(8,128)S(1)}, u32[]{:S(2)}, u32[]{:S(2)}) async-start(f32[32,8,16,128]{3,2,1,0:T(8,128)} %bitcast.55), calls=%async_computation.4 | async-start | bytes 4194304 | tf_op jit(solution)/shard_map/all_to_all | solution.py:348
  383.1 2.7 collective-permute-start.26
  389.4 17.8 %fusion.lower_ref = f32[8,128,1024]{2,1,0:T(8,128)} fusion(f32[8,128,1024]{2,1,0:T(8,128)} %assemble_panel.1.panel_ref, f32[1024,1024]{1,0:T(8,128)} %copy-done), kind=kOutput, calls=%fused_computation | convolution fusion | flops 12884901888 | bytes 12582912 | tf_op jit(solution)/shard_map/dot_general | solution.py:16
  407.3 5.5 %collective-permute-done.26.refs_8_ = bf16[4,3,16,1024]{3,2,1,0:T(8,128)(2,1)S(1)} collective-permute-done((bf16[4,3,16,1024]{3,2,1,0:T(8,128)(2,1)S(1)}, bf16[4,3,16,1024]{3,2,1,0:T(8,128)(2,1)S(1)}, u32[]{:S(2)}, u32[]{:S(2)}) %collective-permute-start.26) | collective-permute-done | bytes 393248 | tf_op jit(solution)/shard_map/ppermute | solution.py:366
  412.7 1.9 collective-permute-done.25.refs_7_
  414.7 3.3 collective-permute-done.24.refs_6_
  421.9 1.3 copy-done.2
  423.2 11.0 %trailing_update.1 = f32[8,1,128,1536]{3,2,1,0:T(8,128)} custom-call(s32[6]{0:T(128)} %pad_add_fusion.order_ref, s32[32]{0:T(128)} %copy-done.1, f32[8,128,1024]{2,1,0:T(8,128)} %assemble_panel.1.panel_ref, f32[8,128,1024]{2,1,0:T(8,128)} %fusion.lower_ref, f32[128,1024]{1,0:T(8,128)} %copy-done.4, f32[8,1,128,1536]{3,2,1,0:T(8,128)} %front_ref.3, ...), custom_call_target="tpu_custom_call" | custom-call | flops 3221225472 | bytes 29360128 | tf_op jit(solution)/shard_map/trailing_update/pallas_call | solution.py:316
  (119 shorter events, 21.7 us)
Async XLA Ops:
  2.5 11.5 %copy-start.14 = (s32[32,128]{1,0:T(8,128)S(1)}, s32[32,128]{1,0:T(8,128)}, u32[]{:S(2)}) copy-start(s32[32,128]{1,0:T(8,128)} %param.10) | copy-start | bytes 49156
  3.9 29.2 %all-to-all-start = ((f32[32,40,256]{2,1,0:T(8,128)}), f32[32,40,256]{2,1,0:T(8,128)S(1)}, u32[]{:S(2)}, u32[]{:S(2)}) async-start(f32[32,40,256]{2,1,0:T(8,128)} %pad_maximum_fusion), calls=%async_computation | async-start | bytes 2621440 | tf_op jit(solution)/shard_map/all_to_all | solution.py:348
  34.2 111.7 %all-to-all-start.1 = ((bf16[32,32,16,256]{3,2,1,0:T(8,128)(2,1)}), bf16[32,32,16,256]{3,2,1,0:T(8,128)(2,1)}, u32[]{:S(2)}, u32[]{:S(2)}) async-start(bf16[32,32,16,256]{3,2,1,0:T(8,128)(2,1)} %bitcast.50), calls=%async_computation.1 | async-start | bytes 16777216 | tf_op jit(solution)/shard_map/all_to_all | solution.py:348
  156.7 23.7 %slice-start = ((f32[32,40,256]{2,1,0:T(8,128)}), f32[32,32,256]{2,1,0:T(8,128)S(1)}, s32[]{:S(2)}) async-start(f32[32,40,256]{2,1,0:T(8,128)} %copy-done.5), calls=%async_computation.5 | async-start | bytes 2097152 | tf_op jit(solution)/shard_map/slice | solution.py:423
  156.7 98.5 %all-to-all-start.2 = ((f32[32,8,16,256]{3,2,1,0:T(8,128)}), f32[32,8,16,256]{3,2,1,0:T(8,128)}, u32[]{:S(2)}, u32[]{:S(2)}) async-start(f32[32,8,16,256]{3,2,1,0:T(8,128)} %bitcast.51), calls=%async_computation.2 | async-start | bytes 8388608 | tf_op jit(solution)/shard_map/all_to_all | solution.py:348
  182.0 71.2 %copy-start.15 = (pred[48]{0:T(512)(128)(4,1)S(1)}, pred[48]{0:T(512)(128)(4,1)}, u32[]{:S(2)}) copy-start(pred[48]{0:T(512)(128)(4,1)} %constant.269) | copy-start | bytes 148
  182.0 71.2 %copy-start.16 = (pred[48]{0:T(512)(128)(4,1)S(1)}, pred[48]{0:T(512)(128)(4,1)}, u32[]{:S(2)}) copy-start(pred[48]{0:T(512)(128)(4,1)} %constant.268) | copy-start | bytes 148
  182.2 10.0 %collective-permute-start = (f32[20,16,256]{2,1,0:T(8,128)S(1)}, f32[20,16,256]{2,1,0:T(8,128)S(1)}, u32[]{:S(2)}, u32[]{:S(2)}) collective-permute-start(f32[20,16,256]{2,1,0:T(8,128)S(1)} %get-tuple-element.78), channel_id=1, source_target_pairs={{0,1},{4,5},{8,9},{12,13},{16,17},{20,21},{24,25},{28,29},{32,33},... | collective-permute-start | bytes 983048 | tf_op jit(solution)/shard_map/ppermute | solution.py:387
  185.4 13.8 %collective-permute-start.1 = (f32[20,16,256]{2,1,0:T(8,128)S(1)}, f32[20,16,256]{2,1,0:T(8,128)S(1)}, u32[]{:S(2)}, u32[]{:S(2)}) collective-permute-start(f32[20,16,256]{2,1,0:T(8,128)S(1)} %get-tuple-element.79), channel_id=1, source_target_pairs={{0,2},{4,6},{8,10},{12,14},{16,18},{20,22},{24,26},{28,30},{32,34}... | collective-permute-start | bytes 983048 | tf_op jit(solution)/shard_map/ppermute | solution.py:387
  187.7 11.5 %collective-permute-start.2 = (f32[20,16,256]{2,1,0:T(8,128)S(1)}, f32[20,16,256]{2,1,0:T(8,128)S(1)}, u32[]{:S(2)}, u32[]{:S(2)}) collective-permute-start(f32[20,16,256]{2,1,0:T(8,128)S(1)} %get-tuple-element.80), channel_id=1, source_target_pairs={{0,3},{4,7},{8,11},{12,15},{16,19},{20,23},{24,27},{28,31},{32,35}... | collective-permute-start | bytes 983048 | tf_op jit(solution)/shard_map/ppermute | solution.py:387
  199.4 35.7 %collective-permute-start.4 = (f32[8,16,256]{2,1,0:T(8,128)S(1)}, f32[8,16,256]{2,1,0:T(8,128)S(1)}, u32[]{:S(2)}, u32[]{:S(2)}) collective-permute-start(f32[8,16,256]{2,1,0:T(8,128)S(1)} %get-tuple-element.74), channel_id=1, source_target_pairs={{0,16},{4,68},{8,24},{12,76},{16,0},{20,84},{24,8},{28,92},{32,48}... | collective-permute-start | bytes 393224 | tf_op jit(solution)/shard_map/ppermute | solution.py:366
  202.3 32.8 %collective-permute-start.3 = (f32[8,16,256]{2,1,0:T(8,128)S(1)}, f32[8,16,256]{2,1,0:T(8,128)S(1)}, u32[]{:S(2)}, u32[]{:S(2)}) collective-permute-start(f32[8,16,256]{2,1,0:T(8,128)S(1)} %get-tuple-element.74), channel_id=1, source_target_pairs={{0,8},{4,36},{8,16},{12,44},{16,24},{20,52},{24,0},{28,60},{32,40}... | collective-permute-start | bytes 393224 | tf_op jit(solution)/shard_map/ppermute | solution.py:366
  202.6 32.5 %collective-permute-start.5 = (f32[8,16,256]{2,1,0:T(8,128)S(1)}, f32[8,16,256]{2,1,0:T(8,128)S(1)}, u32[]{:S(2)}, u32[]{:S(2)}) collective-permute-start(f32[8,16,256]{2,1,0:T(8,128)S(1)} %get-tuple-element.74), channel_id=1, source_target_pairs={{0,24},{4,100},{8,0},{12,108},{16,8},{20,116},{24,16},{28,124},{32... | collective-permute-start | bytes 393224 | tf_op jit(solution)/shard_map/ppermute | solution.py:366
  205.0 30.1 %collective-permute-start.8 = (f32[3,16,256]{2,1,0:T(8,128)S(1)}, f32[3,16,256]{2,1,0:T(8,128)S(1)}, u32[]{:S(2)}, u32[]{:S(2)}) collective-permute-start(f32[3,16,256]{2,1,0:T(8,128)S(1)} %get-tuple-element.75), channel_id=1, source_target_pairs={{0,12},{4,8},{8,4},{12,0},{16,28},{20,24},{24,20},{28,16},{32,44},... | collective-permute-start | bytes 147464 | tf_op jit(solution)/shard_map/ppermute | solution.py:398
  206.0 2.0 collective-permute-start.6
  208.1 23.6 %collective-permute-start.7 = (f32[3,16,256]{2,1,0:T(8,128)S(1)}, f32[3,16,256]{2,1,0:T(8,128)S(1)}, u32[]{:S(2)}, u32[]{:S(2)}) collective-permute-start(f32[3,16,256]{2,1,0:T(8,128)S(1)} %get-tuple-element.76), channel_id=1, source_target_pairs={{0,8},{4,12},{8,0},{12,4},{16,24},{20,28},{24,16},{28,20},{32,40},... | collective-permute-start | bytes 147464 | tf_op jit(solution)/shard_map/ppermute | solution.py:398
  235.1 9.1 %collective-permute-start.11 = (f32[4,8,16,256]{3,2,1,0:T(8,128)S(1)}, f32[4,8,16,256]{3,2,1,0:T(8,128)S(1)}, u32[]{:S(2)}, u32[]{:S(2)}) collective-permute-start(f32[4,8,16,256]{3,2,1,0:T(8,128)S(1)} %pad_maximum_fusion.5.refs_0_), channel_id=1, source_target_pairs={{0,96},{4,28},{8,104},{12,4},{16,112},{20,12},{24,120},{28,20},{32... | collective-permute-start | bytes 1572872 | tf_op jit(solution)/shard_map/ppermute | solution.py:366
  235.5 10.6 %collective-permute-start.10 = (f32[4,8,16,256]{3,2,1,0:T(8,128)S(1)}, f32[4,8,16,256]{3,2,1,0:T(8,128)S(1)}, u32[]{:S(2)}, u32[]{:S(2)}) collective-permute-start(f32[4,8,16,256]{3,2,1,0:T(8,128)S(1)} %pad_maximum_fusion.5.refs_0_), channel_id=1, source_target_pairs={{0,64},{4,20},{8,72},{12,28},{16,80},{20,4},{24,88},{28,12},{32,96... | collective-permute-start | bytes 1572872 | tf_op jit(solution)/shard_map/ppermute | solution.py:366
  239.2 12.5 %collective-permute-start.9 = (f32[4,8,16,256]{3,2,1,0:T(8,128)S(1)}, f32[4,8,16,256]{3,2,1,0:T(8,128)S(1)}, u32[]{:S(2)}, u32[]{:S(2)}) collective-permute-start(f32[4,8,16,256]{3,2,1,0:T(8,128)S(1)} %pad_maximum_fusion.5.refs_0_), channel_id=1, source_target_pairs={{0,32},{4,12},{8,40},{12,20},{16,48},{20,28},{24,56},{28,4},{32,64... | collective-permute-start | bytes 1572872 | tf_op jit(solution)/shard_map/ppermute | solution.py:366
  239.8 31.9 %collective-permute-start.12 = (f32[4,8,16,256]{3,2,1,0:T(8,128)S(1)}, f32[4,8,16,256]{3,2,1,0:T(8,128)S(1)}, u32[]{:S(2)}, u32[]{:S(2)}) collective-permute-start(f32[4,8,16,256]{3,2,1,0:T(8,128)S(1)} %pad_maximum_fusion.5.refs_0_), channel_id=1, source_target_pairs={{0,4},{4,0},{8,12},{12,8},{16,20},{20,16},{24,28},{28,24},{32,36},... | collective-permute-start | bytes 1572872 | tf_op jit(solution)/shard_map/ppermute | solution.py:371
  244.3 29.7 %collective-permute-start.15 = (f32[4,8,16,256]{3,2,1,0:T(8,128)S(1)}, f32[4,8,16,256]{3,2,1,0:T(8,128)S(1)}, u32[]{:S(2)}, u32[]{:S(2)}) collective-permute-start(f32[4,8,16,256]{3,2,1,0:T(8,128)S(1)} %collective-permute-done.11.refs_3_), channel_id=1, source_target_pairs={{0,4},{4,0},{8,12},{12,8},{16,20},{20,16},{24,28},{28,24},{32,36},... | collective-permute-start | bytes 1572872 | tf_op jit(solution)/shard_map/ppermute | solution.py:371
  246.1 29.2 %collective-permute-start.14 = (f32[4,8,16,256]{3,2,1,0:T(8,128)S(1)}, f32[4,8,16,256]{3,2,1,0:T(8,128)}, u32[]{:S(2)}, u32[]{:S(2)}) collective-permute-start(f32[4,8,16,256]{3,2,1,0:T(8,128)S(1)} %collective-permute-done.10.refs_2_), channel_id=1, source_target_pairs={{0,4},{4,0},{8,12},{12,8},{16,20},{20,16},{24,28},{28,24},{32,36},... | collective-permute-start | bytes 1572872 | tf_op jit(solution)/shard_map/ppermute | solution.py:371
  251.7 23.6 %collective-permute-start.13 = (f32[4,8,16,256]{3,2,1,0:T(8,128)S(1)}, f32[4,8,16,256]{3,2,1,0:T(8,128)}, u32[]{:S(2)}, u32[]{:S(2)}) collective-permute-start(f32[4,8,16,256]{3,2,1,0:T(8,128)S(1)} %collective-permute-done.9.refs_1_), channel_id=1, source_target_pairs={{0,4},{4,0},{8,12},{12,8},{16,20},{20,16},{24,28},{28,24},{32,36},... | collective-permute-start | bytes 1572872 | tf_op jit(solution)/shard_map/ppermute | solution.py:371
  255.2 20.1 %copy-start.1 = (s32[32]{0:T(128)}, s32[32]{0:T(128)S(1)}, u32[]{:S(2)}) copy-start(s32[32]{0:T(128)S(1)} %multiply_add_fusion.index_ref) | copy-start | bytes 388
  255.2 111.4 %all-to-all-start.3 = ((bf16[32,32,16,128]{3,2,1,0:T(8,128)(2,1)}), bf16[32,32,16,128]{3,2,1,0:T(8,128)(2,1)}, u32[]{:S(2)}, u32[]{:S(2)}) async-start(bf16[32,32,16,128]{3,2,1,0:T(8,128)(2,1)} %bitcast.53), calls=%async_computation.3 | async-start | bytes 8388608 | tf_op jit(solution)/shard_map/all_to_all | solution.py:348
  268.4 80.4 %collective-permute-start.16 = (f32[2,128,1024]{2,1,0:T(8,128)S(1)}, f32[2,128,1024]{2,1,0:T(8,128)S(1)}, u32[]{:S(2)}, u32[]{:S(2)}) collective-permute-start(f32[2,128,1024]{2,1,0:T(8,128)S(1)} %get-tuple-element.61), channel_id=1, source_target_pairs={{0,1},{4,5},{8,9},{12,13},{16,17},{20,21},{24,25},{28,29},{32,33},... | collective-permute-start | bytes 3145736 | tf_op jit(solution)/shard_map/ppermute | solution.py:387
  271.7 77.1 %collective-permute-start.18 = (f32[2,128,1024]{2,1,0:T(8,128)S(1)}, f32[2,128,1024]{2,1,0:T(8,128)S(1)}, u32[]{:S(2)}, u32[]{:S(2)}) collective-permute-start(f32[2,128,1024]{2,1,0:T(8,128)S(1)} %get-tuple-element.62), channel_id=1, source_target_pairs={{0,3},{4,7},{8,11},{12,15},{16,19},{20,23},{24,27},{28,31},{32,35}... | collective-permute-start | bytes 3145736 | tf_op jit(solution)/shard_map/ppermute | solution.py:387
  273.9 75.0 %collective-permute-start.17 = (f32[2,128,1024]{2,1,0:T(8,128)S(1)}, f32[2,128,1024]{2,1,0:T(8,128)S(1)}, u32[]{:S(2)}, u32[]{:S(2)}) collective-permute-start(f32[2,128,1024]{2,1,0:T(8,128)S(1)} %get-tuple-element.63), channel_id=1, source_target_pairs={{0,2},{4,6},{8,10},{12,14},{16,18},{20,22},{24,26},{28,30},{32,34}... | collective-permute-start | bytes 3145736 | tf_op jit(solution)/shard_map/ppermute | solution.py:387
  355.9 10.7 %copy-start.3 = (bf16[256,1024]{1,0:T(8,128)(2,1)}, bf16[256,1024]{1,0:T(8,128)(2,1)S(1)}, u32[]{:S(2)}) copy-start(bf16[256,1024]{1,0:T(8,128)(2,1)S(1)} %pad_maximum_fusion.6.refs_0_) | copy-start | bytes 1572868
  355.9 19.2 %collective-permute-start.23 = (bf16[256,1024]{1,0:T(8,128)(2,1)S(1)}, bf16[256,1024]{1,0:T(8,128)(2,1)S(1)}, u32[]{:S(2)}, u32[]{:S(2)}) collective-permute-start(bf16[256,1024]{1,0:T(8,128)(2,1)S(1)} %pad_maximum_fusion.6.refs_0_), channel_id=1, source_target_pairs={{0,3},{1,0},{2,1},{3,2},{4,7},{5,4},{6,5},{7,6},{8,11},{9,8},{10,9... | collective-permute-start | bytes 1572872 | tf_op jit(solution)/shard_map/ppermute | solution.py:467
  356.0 19.1 %collective-permute-start.22 = (bf16[256,1024]{1,0:T(8,128)(2,1)S(1)}, bf16[256,1024]{1,0:T(8,128)(2,1)S(1)}, u32[]{:S(2)}, u32[]{:S(2)}) collective-permute-start(bf16[256,1024]{1,0:T(8,128)(2,1)S(1)} %pad_maximum_fusion.6.refs_0_), channel_id=1, source_target_pairs={{0,1},{1,2},{2,3},{3,0},{4,5},{5,6},{6,7},{7,4},{8,9},{9,10},{10,1... | collective-permute-start | bytes 1572872 | tf_op jit(solution)/shard_map/ppermute | solution.py:467
  357.5 4.3 %collective-permute-start.21 = (bf16[3,16,1024]{2,1,0:T(8,128)(2,1)S(1)}, bf16[3,16,1024]{2,1,0:T(8,128)(2,1)S(1)}, u32[]{:S(2)}, u32[]{:S(2)}) collective-permute-start(bf16[3,16,1024]{2,1,0:T(8,128)(2,1)S(1)} %bitcast.62), channel_id=1, source_target_pairs={{0,24},{4,100},{8,0},{12,108},{16,8},{20,116},{24,16},{28,124},{32... | collective-permute-start | bytes 294920 | tf_op jit(solution)/shard_map/ppermute | solution.py:366
  360.2 5.1 %collective-permute-start.20 = (bf16[3,16,1024]{2,1,0:T(8,128)(2,1)S(1)}, bf16[3,16,1024]{2,1,0:T(8,128)(2,1)S(1)}, u32[]{:S(2)}, u32[]{:S(2)}) collective-permute-start(bf16[3,16,1024]{2,1,0:T(8,128)(2,1)S(1)} %bitcast.63), channel_id=1, source_target_pairs={{0,16},{4,68},{8,24},{12,76},{16,0},{20,84},{24,8},{28,92},{32,48}... | collective-permute-start | bytes 294920 | tf_op jit(solution)/shard_map/ppermute | solution.py:366
  360.7 5.8 %collective-permute-start.19 = (bf16[3,16,1024]{2,1,0:T(8,128)(2,1)S(1)}, bf16[3,16,1024]{2,1,0:T(8,128)(2,1)S(1)}, u32[]{:S(2)}, u32[]{:S(2)}) collective-permute-start(bf16[3,16,1024]{2,1,0:T(8,128)(2,1)S(1)} %bitcast.64), channel_id=1, source_target_pairs={{0,8},{4,36},{8,16},{12,44},{16,24},{20,52},{24,0},{28,60},{32,40}... | collective-permute-start | bytes 294920 | tf_op jit(solution)/shard_map/ppermute | solution.py:366
  366.6 51.5 %copy-start.6 = (bf16[4,3,16,1024]{3,2,1,0:T(8,128)(2,1)}, bf16[4,3,16,1024]{3,2,1,0:T(8,128)(2,1)S(1)}, u32[]{:S(2)}) copy-start(bf16[4,3,16,1024]{3,2,1,0:T(8,128)(2,1)S(1)} %pad_maximum_fusion.7.refs_5_) | copy-start | bytes 1179652
  375.1 32.1 %copy-start.7 = (bf16[256,1024]{1,0:T(8,128)(2,1)}, bf16[256,1024]{1,0:T(8,128)(2,1)S(1)}, u32[]{:S(2)}) copy-start(bf16[256,1024]{1,0:T(8,128)(2,1)S(1)} %collective-permute-done.23.refs_4_) | copy-start | bytes 1572868
  375.9 45.9 %all-to-all-start.4 = ((f32[32,8,16,128]{3,2,1,0:T(8,128)}), f32[32,8,16,128]{3,2,1,0:T(8,128)S(1)}, u32[]{:S(2)}, u32[]{:S(2)}) async-start(f32[32,8,16,128]{3,2,1,0:T(8,128)} %bitcast.55), calls=%async_computation.4 | async-start | bytes 4194304 | tf_op jit(solution)/shard_map/all_to_all | solution.py:348
  383.1 29.7 %collective-permute-start.26 = (bf16[4,3,16,1024]{3,2,1,0:T(8,128)(2,1)S(1)}, bf16[4,3,16,1024]{3,2,1,0:T(8,128)(2,1)S(1)}, u32[]{:S(2)}, u32[]{:S(2)}) collective-permute-start(bf16[4,3,16,1024]{3,2,1,0:T(8,128)(2,1)S(1)} %pad_maximum_fusion.7.refs_5_), channel_id=1, source_target_pairs={{0,96},{4,28},{8,104},{12,4},{16,112},{20,12},{24,120},{28,20},{32... | collective-permute-start | bytes 1179656 | tf_op jit(solution)/shard_map/ppermute | solution.py:366
  385.8 28.9 %collective-permute-start.25 = (bf16[4,3,16,1024]{3,2,1,0:T(8,128)(2,1)S(1)}, bf16[4,3,16,1024]{3,2,1,0:T(8,128)(2,1)}, u32[]{:S(2)}, u32[]{:S(2)}) collective-permute-start(bf16[4,3,16,1024]{3,2,1,0:T(8,128)(2,1)S(1)} %pad_maximum_fusion.7.refs_5_), channel_id=1, source_target_pairs={{0,64},{4,20},{8,72},{12,28},{16,80},{20,4},{24,88},{28,12},{32,96... | collective-permute-start | bytes 1179656 | tf_op jit(solution)/shard_map/ppermute | solution.py:366
  386.3 31.7 %collective-permute-start.24 = (bf16[4,3,16,1024]{3,2,1,0:T(8,128)(2,1)S(1)}, bf16[4,3,16,1024]{3,2,1,0:T(8,128)(2,1)}, u32[]{:S(2)}, u32[]{:S(2)}) collective-permute-start(bf16[4,3,16,1024]{3,2,1,0:T(8,128)(2,1)S(1)} %pad_maximum_fusion.7.refs_5_), channel_id=1, source_target_pairs={{0,32},{4,12},{8,40},{12,20},{16,48},{20,28},{24,56},{28,4},{32,64... | collective-permute-start | bytes 1179656 | tf_op jit(solution)/shard_map/ppermute | solution.py:366
  387.9 19.3 %collective-permute-start.28 = (bf16[128,1024]{1,0:T(8,128)(2,1)S(1)}, bf16[128,1024]{1,0:T(8,128)(2,1)S(1)}, u32[]{:S(2)}, u32[]{:S(2)}) collective-permute-start(bf16[128,1024]{1,0:T(8,128)(2,1)S(1)} %slice.104), channel_id=1, source_target_pairs={{0,3},{1,0},{2,1},{3,2},{4,7},{5,4},{6,5},{7,6},{8,11},{9,8},{10,9... | collective-permute-start | bytes 786440 | tf_op jit(solution)/shard_map/ppermute | solution.py:467
  389.0 18.3 %collective-permute-start.27 = (bf16[128,1024]{1,0:T(8,128)(2,1)S(1)}, bf16[128,1024]{1,0:T(8,128)(2,1)S(1)}, u32[]{:S(2)}, u32[]{:S(2)}) collective-permute-start(bf16[128,1024]{1,0:T(8,128)(2,1)S(1)} %slice.103), channel_id=1, source_target_pairs={{0,1},{1,2},{2,3},{3,0},{4,5},{5,6},{6,7},{7,4},{8,9},{9,10},{10,1... | collective-permute-start | bytes 786440 | tf_op jit(solution)/shard_map/ppermute | solution.py:467
  407.2 11.3 %copy-start.12 = (bf16[128,1024]{1,0:T(8,128)(2,1)}, bf16[128,1024]{1,0:T(8,128)(2,1)S(1)}, u32[]{:S(2)}) copy-start(bf16[128,1024]{1,0:T(8,128)(2,1)S(1)} %collective-permute-done.28.refs_3_) | copy-start | bytes 786436
  407.3 11.7 %copy-start.13 = (bf16[128,1024]{1,0:T(8,128)(2,1)}, bf16[128,1024]{1,0:T(8,128)(2,1)S(1)}, u32[]{:S(2)}) copy-start(bf16[128,1024]{1,0:T(8,128)(2,1)S(1)} %collective-permute-done.27.refs_2_) | copy-start | bytes 786436
  418.0 1.8 collective-permute-start.29
  418.5 2.3 collective-permute-start.30
  418.5 3.3 collective-permute-start.31
  419.0 2.9 collective-permute-start.32
  (8 other events, 37.3 us)
